TPU v7x, 32 devices: a whole 2x2x4 slice. The times are simulated.
32 devices in a mesh: clip: 8 (over z, core), col: 4 (over y, x).
Axes of the slice: x: 2, y: 2, z: 4, core: 2. Of those that a mesh axis runs over, the one named last changes fastest.
Arguments:
- frames: bfloat16 [128, 256, 768], P('clip', 'col'), may hold values from -6 to 6
- cotangent: bfloat16 [128, 256, 768], P('clip', 'col'), may hold values from -6 to 6
- frame_len: int32 [128], P('clip'), may hold values from 64 to 256, as said below
- column_rank: int32 [256], replicated, may hold values from 0 to 255, each once
- gain_one: bfloat16 [768], replicated, may hold values from 0.25 to 1.75
- shift_one: bfloat16 [768], replicated, may hold values from -4 to 4
- w_qkv: bfloat16 [768, 2304], replicated, may hold values from -0.3125 to 0.3125
- bias_qv: bfloat16 [1536], replicated, may hold values from -4 to 4
- w_out: bfloat16 [768, 768], replicated, may hold values from -0.4375 to 0.4375
- bias_out: bfloat16 [768], replicated, may hold values from -4 to 4
- gain_two: bfloat16 [768], replicated, may hold values from 0.25 to 1.75
- shift_two: bfloat16 [768], replicated, may hold values from -4 to 4
- w_up: bfloat16 [768, 3072], replicated, may hold values from -0.21875 to 0.21875
- bias_up: bfloat16 [3072], replicated, may hold values from -4 to 4
- w_down: bfloat16 [3072, 768], replicated, may hold values from -0.109375 to 0.109375
- bias_down: bfloat16 [768], replicated, may hold values from -4 to 4
Outputs:
- output: bfloat16 [128, 256, 768], P('clip', 'col')
- grad_input: float32 [128, 256, 768], P('clip', 'col')
- grad_gain_one: float32 [768], P('col')
- grad_shift_one: float32 [768], P('col')
- grad_w_qkv: float32 [768, 2304], P(None, 'col')
- grad_bias_qv: float32 [1536], P('col')
- grad_w_out: float32 [768, 768], P(None, 'col')
- grad_bias_out: float32 [768], P('col')
- grad_gain_two: float32 [768], P('col')
- grad_shift_two: float32 [768], P('col')
- grad_w_up: float32 [768, 3072], P(None, 'col')
- grad_bias_up: float32 [3072], P('col')
- grad_w_down: float32 [3072, 768], P(None, 'col')
- grad_bias_down: float32 [768], P('col')
Inputs may be any that keep to these rules, and one draw needn't show every extreme that they name: `frame_len`: every frame holds 256 or 64 live tokens; among the 16 frames of each index of clip at least one holds 256.
All inputs are finite; a program needn't handle non-finite values.
Results may differ from a plain program's by a relative error of at most 0.02.
Values may be sent and summed in bfloat16 or wider, within the bound.
No kernel may reach another device: no remote copies, remote signals or barrier semaphores. Data moves between devices by JAX's collectives and lax.ppermute only.
A program may use at most 512 MiB of HBM per device.

v0:
```python
import functools
import jax
import jax.numpy as jnp
from jax import lax
from jax.experimental import pallas as pl
from jax.experimental.pallas import tpu as pltpu
from jax.sharding import PartitionSpec as P

HEADS = 12
EPSILON = 1e-06
MASKED = -1e30
F32 = jnp.float32
BF16 = jnp.bfloat16
INV_SQRT2 = 0.5**0.5
INV_SQRT_2PI = 0.3989422804014327
MIB = 1 << 20
PACE = 1_500_000
GAIN_ONE, SHIFT_ONE, BIAS_OUT, GAIN_TWO, SHIFT_TWO, BIAS_DOWN, BIAS_Q, BIAS_V, BIAS_UP = range(9)


def dot(left, right):
    return lax.dot_general(left, right, (((1,), (0,)), ((), ())), preferred_element_type=F32)


def dot_nt(left, right):
    return lax.dot_general(left, right, (((1,), (1,)), ((), ())), preferred_element_type=F32)


def add_low(left, right):
    return (left.astype(F32) + right.astype(F32)).astype(BF16)


def in_hbm(array):
    return pltpu.with_memory_space_constraint(array, pltpu.HBM)


def whole(shape):
    return pl.BlockSpec(shape, lambda *_: (0,) * len(shape), pipeline_mode=pl.Buffered(1))


def lanes(rows, size):
    return pl.BlockSpec((rows, size), lambda f, *_: (0, f))


def tokens_of(size, columns):
    return pl.BlockSpec((size, columns), lambda f, *_: (f, 0))


def params(limit, steps=1):
    return pltpu.CompilerParams(
        vmem_limit_bytes=limit * MIB, dimension_semantics=("arbitrary",) * steps
    )


def cost(micros):
    return pl.CostEstimate(flops=0, bytes_accessed=int(micros * PACE), transcendentals=0)


def standardise(value):
    centred = value - jnp.mean(value, axis=1, keepdims=True)
    root = lax.rsqrt(jnp.mean(centred * centred, axis=1, keepdims=True) + EPSILON)
    return centred * root, root


def standardise_back(grad, gain, xhat, root):
    scaled = grad * gain
    first = jnp.mean(scaled, axis=1, keepdims=True)
    second = jnp.mean(scaled * xhat, axis=1, keepdims=True)
    return root * (scaled - first - xhat * second)


def lane_sums(value):
    total = value[:, :128]
    for at in range(128, value.shape[1], 128):
        total = total + value[:, at : at + 128]
    return total


def row_sum(value):
    return jnp.sum(value, axis=0, keepdims=True)


def pair_diagonal(upper, lower):
    zero = jnp.zeros_like(upper)
    return jnp.concatenate(
        [jnp.concatenate([upper, zero], axis=0), jnp.concatenate([zero, lower], axis=0)], axis=1
    )


def token_rows(pieces):
    return jnp.concatenate([piece[0] for piece in pieces], axis=0)


def pairs_and_blocks(size, block, stages):
    if size == block:
        for stage in stages:
            for pair in range(HEADS // 2):
                stage(pair, 0, pair)
    else:

        @pl.loop(0, HEADS // 2 * (size // block))
        def _(step):
            blocks = size // block
            pair = step // blocks
            for stage in stages:
                stage(pair, pl.multiple_of((step - pair * blocks) * block, block), 0)


def slots(size, block):
    return HEADS // 2 if size == block else 1


def mask_lanes(ranks, length, target):
    target[...] = jnp.broadcast_to(jnp.where(ranks[...] < length, 0.0, MASKED), target.shape)


def across(value, width):
    return jnp.concatenate([value] * (width // value.shape[1]), axis=1)


def _(step):
            blocks = size // block
            pair = step // blocks
            one(pair, pl.multiple_of((step - pair * blocks) * block, block))


def attend_kernel(ncol, block, first, info, lens, *refs):
    pieces = refs[:ncol]
    ranks, vecs, w_qkv, w_out = refs[ncol : ncol + 4]
    qkv_t, mixed_t, middle_n, lse, mixed_f, keys_n, mask, scores, probs, inverse = refs[-10:]
    size, model = middle_n.shape
    head = model // HEADS
    rows = token_rows(pieces).astype(F32)
    xhat, _ = standardise(rows)
    normed = (xhat * vecs[GAIN_ONE : GAIN_ONE + 1] + vecs[SHIFT_ONE : SHIFT_ONE + 1]).astype(BF16)
    queries = dot(normed, w_qkv[:, :model]) + vecs[BIAS_Q : BIAS_Q + 1]
    qkv_t[:model] = queries.T.astype(BF16) * BF16(head**-0.5)
    keys = dot(normed, w_qkv[:, model : 2 * model])
    keys_n[...] = keys.astype(BF16)
    qkv_t[model : 2 * model] = keys.T.astype(BF16)
    values = dot(normed, w_qkv[:, 2 * model :]) + vecs[BIAS_V : BIAS_V + 1]
    qkv_t[2 * model :] = values.T.astype(BF16)
    mask_lanes(ranks, lens[first + pl.program_id(0)], mask)

    def begin(pair, at, slot):
        low, high = pair * 2 * head, (pair * 2 + 1) * head
        where = pl.ds(at, block)
        right = pair_diagonal(qkv_t[pl.ds(low, head), where], qkv_t[pl.ds(high, head), where])
        scores[slot] = dot(keys_n[:, pl.ds(low, 2 * head)], right)

    def weigh(pair, at, slot):
        value = scores[slot] + across(mask[...], 2 * block)
        top = jnp.max(value, axis=0, keepdims=True)
        weight = jnp.exp(value - top)
        total = jnp.sum(weight, axis=0, keepdims=True)
        probs[slot] = weight.astype(BF16)
        inverse[slot] = 1.0 / total
        stats = top + jnp.log(total)
        for side in range(2):
            lse[0, pl.ds(pair * 2 + side, 1), pl.ds(at, block)] = stats[:, side * block : (side + 1) * block]

    def mix(pair, at, slot):
        for side in range(2):
            start, cut = (pair * 2 + side) * head, slice(side * block, (side + 1) * block)
            value = qkv_t[pl.ds(2 * model + start, head), :]
            mixed_f[pl.ds(start, head), pl.ds(at, block)] = dot(value, probs[slot, :, cut]) * inverse[slot, :, cut]

    pairs_and_blocks(size, block, (begin, weigh, mix))
    mixed_t[...] = mixed_f[...].astype(BF16)
    middle = rows + dot(mixed_f[...].T.astype(BF16), w_out[...]) + vecs[BIAS_OUT : BIAS_OUT + 1]
    middle_n[...] = middle


def attend_call(info, lens, pieces, ranks, vecs, w_qkv, w_out, first, frames, per, earlier=()):
    ncol = len(pieces)
    width, model = pieces[1].shape[1:]
    size = ncol * width
    tokens = per * size
    block = min(size, 256)
    own = pl.BlockSpec((1, width, model), lambda f, info, *_: (info[0] * per + first + f, 0, 0))
    other = pl.BlockSpec((1, width, model), lambda f, *_: (f, 0, 0))

    def rows_of(columns):
        return pl.BlockSpec((size, columns), lambda f, *_: (first + f, 0))

    def lanes_of(rows):
        return pl.BlockSpec((rows, size), lambda f, *_: (0, first + f))

    return pl.pallas_call(
        functools.partial(attend_kernel, ncol, block, first),
        grid_spec=pltpu.PrefetchScalarGridSpec(
            num_scalar_prefetch=2,
            grid=(frames,),
            in_specs=[own]
            + [other] * (ncol - 1)
            + [whole(ranks.shape), whole(vecs.shape), whole(w_qkv.shape), whole(w_out.shape)]
            + [pl.BlockSpec(memory_space=pl.ANY)] * len(earlier),
            out_specs=[
                lanes_of(3 * model),
                lanes_of(model),
                rows_of(model),
                pl.BlockSpec((1, 16, size), lambda f, *_: (first + f, 0, 0)),
            ],
            scratch_shapes=[
                pltpu.VMEM((model, size), F32),
                pltpu.VMEM((size, model), BF16),
                pltpu.VMEM((size, 128), F32),
                pltpu.VMEM((slots(size, block), size, 2 * block), F32),
                pltpu.VMEM((slots(size, block), size, 2 * block), BF16),
                pltpu.VMEM((slots(size, block), 1, 2 * block), F32),
            ],
        ),
        out_shape=[
            pltpu.HBM((3 * model, tokens), BF16),
            pltpu.HBM((model, tokens), BF16),
            pltpu.HBM((tokens, model), F32),
            pltpu.HBM((per, 16, size), F32),
        ],
        input_output_aliases={ncol + 6 + i: i for i in range(len(earlier))},
        compiler_params=params(40),
        cost_estimate=cost(10),
        name="attend",
    )(info, lens, *pieces, ranks, vecs, in_hbm(w_qkv), in_hbm(w_out), *earlier)


def gather_tokens(pieces, target):
    frames, width = pieces[1].shape[:2]
    at = 0
    for f in range(frames):
        for piece in pieces:
            target[at : at + width] = piece[f]
            at += width


def halves_apart(info, value):
    first, chunk = info[1] == 0, value.shape[1] // 2
    low, high = value[:, :chunk], value[:, chunk:]
    return jnp.where(first, low, high), jnp.where(first, high, low)


def mlp_kernel(ncol, info, *refs):
    own_in, *pieces_in = refs[:ncol]
    middle_n, mixed_in, vecs, w_up, w_down = refs[ncol : ncol + 5]
    outs = refs[ncol + 5 : 2 * ncol + 5]
    gmiddle_out, sums, down_keep, down_send, up_keep, up_send = refs[2 * ncol + 5 : 2 * ncol + 11]
    (
        cot_p, cot_n, cot_t, second_n, second_t, active_n, hidden_n, total, grad, mixed_t, up_slots, down_slots, out_slots,
        in_sems, up_sems, down_sems, out_sems, g_sems,
    ) = refs[2 * ncol + 11 :]
    tokens, model = total.shape
    frames, width = outs[0].shape[:2]
    part = model // 4
    rows = min(tokens, 256)
    step, steps = pl.program_id(0), pl.num_programs(0) - 1
    gain = vecs[GAIN_TWO : GAIN_TWO + 1]
    coming = [
        pltpu.make_async_copy(own_in.at[pl.ds(info[0] * frames, frames)], cot_p.at[0], in_sems.at[0]),
        *[pltpu.make_async_copy(p, cot_p.at[i + 1], in_sems.at[i + 1]) for i, p in enumerate(pieces_in)],
        pltpu.make_async_copy(mixed_in, mixed_t, in_sems.at[ncol]),
    ]

    def down_copy(j):
        target = down_keep if j >= 2 else down_send
        return pltpu.make_async_copy(down_slots.at[j], target.at[:, pl.ds(j % 2 * part, part), :], down_sems.at[j])

    def up_copies(j, block):
        return [
            pltpu.make_async_copy(up_slots.at[side, j], target.at[block, pl.ds(0, model), :], up_sems.at[side, j])
            for side, target in enumerate((up_keep, up_send))
        ]

    @pl.when(step == 0)
    def _():
        for copy in coming:
            copy.start()
        sums[...] = jnp.zeros_like(sums)
        for at in range(0, tokens, rows):
            cut = slice(at, at + rows)
            middle = middle_n[cut]
            xhat, _ = standardise(middle)
            second = xhat * gain + vecs[SHIFT_TWO : SHIFT_TWO + 1]
            second_n[cut] = second.astype(BF16)
            second_t[:, cut] = second.T.astype(BF16)
            total[cut] = middle + vecs[BIAS_DOWN : BIAS_DOWN + 1]
            grad[cut] = jnp.zeros((rows, model), F32)
        for copy in coming[:ncol]:
            copy.wait()
        gather_tokens([cot_p.at[i] for i in range(ncol)], cot_n)
        cot_t[...] = cot_n[...].astype(F32).T.astype(BF16)

    @pl.when(step < steps)
    def _():
        block = block_of(step, info)
        bias = vecs[pl.ds(BIAS_UP + block, 1), :]
        for at in range(0, tokens, rows):
            cut = slice(at, at + rows)
            hidden = dot(second_n[cut], w_up[...]) + bias
            half = 0.5 + 0.5 * lax.erf(hidden * INV_SQRT2)
            active = (hidden * half).astype(BF16)
            bell = jnp.exp(hidden * hidden * -0.5) * INV_SQRT_2PI
            slope = half + hidden * bell
            active_n[cut] = active
            total[cut] += dot(active, w_down[...])
            low = (dot_nt(cot_n[cut], w_down[...]) * slope).astype(BF16)
            hidden_n[cut] = low
            sums[pl.ds(4 + block, 1), :] += row_sum(low.astype(F32))
            grad[cut] += dot_nt(low, w_up[...])
        result = dot(cot_t[...], active_n[...]).astype(BF16)
        for c in range(4):
            down_slots[step, c] = result[c * part : (c + 1) * part]
        up_slots[0, step], up_slots[1, step] = halves_apart(info, dot(second_t[...], hidden_n[...]).astype(BF16))
        for copy in up_copies(step, block):
            copy.start()

    for j in range(4):

        @pl.when(step == j)
        def _(j=j):
            down_copy(j).start()

    @pl.when(step == steps)
    def _():
        at = 0
        for f in range(frames):
            for out in outs:
                out[f] = total[at : at + width].astype(BF16)
                at += width
        going = []
        for i, at in enumerate(range(0, tokens, rows)):
            cut = slice(at, at + rows)
            xhat, root = standardise(middle_n[cut])
            cot_f32, back = cot_n[cut].astype(F32), grad[cut]
            grad_middle = cot_f32 + standardise_back(back, gain, xhat, root)
            total[cut] = grad_middle
            copy = pltpu.make_async_copy(total.at[pl.ds(at, rows)], gmiddle_out.at[pl.ds(at, rows)], g_sems.at[i])
            copy.start()
            going.append(copy)
            low = grad_middle.astype(BF16)
            hidden_n[cut] = low
            sums[0:1] += row_sum(back * xhat)
            sums[1:2] += row_sum(back)
            sums[2:3] += row_sum(low.astype(F32))
            sums[3:4] += row_sum(cot_f32)
        coming[ncol].wait()
        both = halves_apart(info, dot(mixed_t[...], hidden_n[...]).T.astype(BF16))
        for side, target in enumerate((up_keep, up_send)):
            for c in range(4):
                out_slots[side, c] = both[side][c * part : (c + 1) * part]
                copy = pltpu.make_async_copy(out_slots.at[side, c], target.at[c, pl.ds(model, part), :], out_sems.at[side, c])
                copy.start()
                going.append(copy)
        for j in range(4):
            going += [down_copy(j), *up_copies(j, block_of(j, info))]
        for copy in going:
            copy.wait()


def block_of(step, info):
    return lax.bitwise_xor(step // 2, 1 - info[1]) * 2 + step % 2


def mlp_call(info, pieces, middle_n, mixed_t, vecs, w_up, w_down):
    ncol = len(pieces)
    piece = pieces[1].shape
    tokens, model = middle_n.shape
    steps = w_down.shape[0] // model
    part, chunk = model // 4, model // 2
    rows = min(tokens, 256)
    stays = pl.BlockSpec(memory_space=pltpu.HBM)

    def block(j, info):
        return block_of(jnp.minimum(j, steps - 1), info)

    down, up = (4, 2 * part, model), (steps, model + part, chunk)
    return pl.pallas_call(
        functools.partial(mlp_kernel, ncol),
        grid_spec=pltpu.PrefetchScalarGridSpec(
            num_scalar_prefetch=1,
            grid=(steps + 1,),
            in_specs=[stays] * ncol
            + [
                whole(middle_n.shape),
                stays,
                whole(vecs.shape),
                pl.BlockSpec((model, model), lambda j, info: (0, block(j, info))),
                pl.BlockSpec((model, model), lambda j, info: (block(j, info), 0)),
            ],
            out_specs=[whole(piece)] * ncol + [stays, whole((16, model))] + [stays] * 4,
            scratch_shapes=[
                pltpu.VMEM((ncol,) + piece, BF16),
                pltpu.VMEM((tokens, model), BF16),
                pltpu.VMEM((model, tokens), BF16),
                pltpu.VMEM((tokens, model), BF16),
                pltpu.VMEM((model, tokens), BF16),
                pltpu.VMEM((tokens, model), BF16),
                pltpu.VMEM((tokens, model), BF16),
                pltpu.VMEM((tokens, model), F32),
                pltpu.VMEM((tokens, model), F32),
                pltpu.VMEM((model, tokens), BF16),
                pltpu.VMEM((2, steps, model, chunk), BF16),
                pltpu.VMEM((steps, 4, part, model), BF16),
                pltpu.VMEM((2, 4, part, chunk), BF16),
                pltpu.SemaphoreType.DMA((ncol + 1,)),
                pltpu.SemaphoreType.DMA((2, steps)),
                pltpu.SemaphoreType.DMA((steps,)),
                pltpu.SemaphoreType.DMA((2, 4)),
                pltpu.SemaphoreType.DMA((tokens // rows,)),
            ],
        ),
        out_shape=[pltpu.HBM(piece, BF16)] * ncol
        + [pltpu.HBM((tokens, model), F32), jax.ShapeDtypeStruct((16, model), F32)]
        + [pltpu.HBM(s, BF16) for s in (down, down, up, up)],
        compiler_params=params(60),
        cost_estimate=cost(40),
        name="mlp",
    )(info, *[in_hbm(p) for p in pieces], in_hbm(middle_n), in_hbm(mixed_t), vecs, in_hbm(w_up), in_hbm(w_down))


def attend_back_kernel(ncol, block, first, info, lens, *refs):
    pieces = refs[:ncol]
    ranks, vecs, w_qkv_in, w_out, qkv_t, lse, mixed_t, gmiddle_n = refs[ncol : ncol + 8]
    gproj_t, normed_n, sums, *outs = refs[-15 - ncol : -12]
    gmixed_t, gacc, columns, kv_n, mask, scores, gprobs, probs, gscores, inner, w_qkv, sem = refs[-12:]
    size, model = gmiddle_n.shape
    head = model // HEADS
    step = pl.program_id(0)

    coming = pltpu.make_async_copy(w_qkv_in, w_qkv, sem.at[0])

    @pl.when(step == 0)
    def _():
        coming.start()
        sums[...] = jnp.zeros_like(sums)
        columns[...] = jnp.zeros_like(columns)

    gmixed_t[...] = dot_nt(w_out[...], gmiddle_n[...].astype(BF16)).astype(BF16)
    kv_n[...] = qkv_t[model:].astype(F32).T.astype(BF16)
    mask_lanes(ranks, lens[first + step], mask)
    product = gmixed_t[...].astype(F32) * mixed_t[...].astype(F32)
    for h in range(HEADS):
        inner[h : h + 1] = row_sum(product[h * head : (h + 1) * head])
    many = size != block
    if many:
        gacc[...] = jnp.zeros_like(gacc)

    def begin(pair, at, slot):
        low, high = pair * 2 * head, (pair * 2 + 1) * head
        where = pl.ds(at, block)
        right = pair_diagonal(qkv_t[pl.ds(low, head), where], qkv_t[pl.ds(high, head), where])
        scores[slot] = dot(kv_n[:, pl.ds(low, 2 * head)], right)
        right = pair_diagonal(gmixed_t[pl.ds(low, head), where], gmixed_t[pl.ds(high, head), where])
        gprobs[slot] = dot(kv_n[:, pl.ds(model + low, 2 * head)], right)

    def weigh(pair, at, slot):
        where = pl.ds(at, block)
        stats, means = (
            jnp.concatenate([rows[pl.ds(pair * 2 + i, 1), where] for i in range(2)], axis=1) for rows in (lse.at[0], inner)
        )
        value = jnp.exp(scores[slot] + across(mask[...], 2 * block) - stats)
        probs[slot] = value.astype(BF16)
        gscores[slot] = (value * (gprobs[slot] - means)).astype(BF16)

    def spread(pair, at, slot):
        where = pl.ds(at, block)
        for side in range(2):
            start, cut = (pair * 2 + side) * head, slice(side * block, (side + 1) * block)
            grad_side = gscores[slot, :, cut]
            grad_q = dot(qkv_t[pl.ds(model + start, head), :], grad_side) * head**-0.5
            grad_k = dot_nt(qkv_t[pl.ds(start, head), where], grad_side)
            grad_v = dot_nt(gmixed_t[pl.ds(start, head), where], probs[slot, :, cut])
            gproj_t[pl.ds(start, head), where] = grad_q.astype(BF16)
            if many:
                gacc[pl.ds(start, head), :] += grad_k
                gacc[pl.ds(model + start, head), :] += grad_v
            else:
                gproj_t[pl.ds(model + start, head), :] = grad_k.astype(BF16)
                gproj_t[pl.ds(2 * model + start, head), :] = grad_v.astype(BF16)

    pairs_and_blocks(size, block, (begin, weigh, spread))
    if many:
        gproj_t[model:] = gacc[...].astype(BF16)
    columns[:model] += lane_sums(gproj_t[:model].astype(F32))
    columns[model:] += lane_sums(gproj_t[2 * model :].astype(F32))

    @pl.when(step == 0)
    def _():
        coming.wait()

    grad = dot(w_qkv[...], gproj_t[...]).T
    xhat, root = standardise(token_rows(pieces).astype(F32))
    gain = vecs[GAIN_ONE : GAIN_ONE + 1]
    normed_n[...] = (xhat * gain + vecs[SHIFT_ONE : SHIFT_ONE + 1]).astype(BF16)
    sums[0:1] += row_sum(grad * xhat)
    sums[1:2] += row_sum(grad)
    total = gmiddle_n[...] + standardise_back(grad, gain, xhat, root)
    result = total.astype(BF16)
    width = size // ncol
    for k in range(ncol):
        outs[k][0] = result[k * width : (k + 1) * width]

    @pl.when(step == pl.num_programs(0) - 1)
    def _():
        for i in range(2):
            sums[2 + i : 3 + i] = row_sum(columns[i * model : (i + 1) * model].T)


def attend_back_call(
    info, lens, pieces, ranks, vecs, w_qkv, w_out, qkv_t, lse, mixed_t, gmiddle_n, first, frames, per, earlier=()
):
    ncol = len(pieces)
    width, model = pieces[1].shape[1:]
    size = ncol * width
    tokens = per * size
    block = min(size, 256)
    acc = (2 * model, size) if size != block else (8, 128)

    def later(spec_lanes, shape):
        if spec_lanes:
            return pl.BlockSpec(shape, lambda f, *_: (0, first + f))
        return pl.BlockSpec(shape, lambda f, *_: (first + f,) + (0,) * (len(shape) - 1))

    own = pl.BlockSpec((1, width, model), lambda f, info, *_: (info[0] * per + first + f, 0, 0))
    piece = later(False, (1, width, model))
    return pl.pallas_call(
        functools.partial(attend_back_kernel, ncol, block, first),
        grid_spec=pltpu.PrefetchScalarGridSpec(
            num_scalar_prefetch=2,
            grid=(frames,),
            in_specs=[own]
            + [piece] * (ncol - 1)
            + [
                whole(ranks.shape),
                whole(vecs.shape),
                pl.BlockSpec(memory_space=pltpu.HBM),
                whole(w_out.shape),
                later(True, (3 * model, size)),
                later(False, (1, 16, size)),
                later(True, (model, size)),
                later(False, (size, model)),
            ]
            + [pl.BlockSpec(memory_space=pl.ANY)] * len(earlier),
            out_specs=[later(True, (3 * model, size)), later(False, (size, model)), whole((16, model))] + [piece] * ncol,
            scratch_shapes=[
                pltpu.VMEM((model, size), BF16),
                pltpu.VMEM(acc, F32),
                pltpu.VMEM((2 * model, 128), F32),
                pltpu.VMEM((size, 2 * model), BF16),
                pltpu.VMEM((size, 128), F32),
                pltpu.VMEM((slots(size, block), size, 2 * block), F32),
                pltpu.VMEM((slots(size, block), size, 2 * block), F32),
                pltpu.VMEM((slots(size, block), size, 2 * block), BF16),
                pltpu.VMEM((slots(size, block), size, 2 * block), BF16),
                pltpu.VMEM((16, size), F32),
                pltpu.VMEM(w_qkv.shape, BF16),
                pltpu.SemaphoreType.DMA((1,)),
            ],
        ),
        out_shape=[
            pltpu.HBM((3 * model, tokens), BF16),
            pltpu.HBM((tokens, model), BF16),
            pltpu.HBM((16, model), F32),
        ]
        + [pltpu.HBM((per, width, model), BF16)] * ncol,
        input_output_aliases={ncol + 10 + i: i + (i > 1) for i in range(len(earlier))},
        compiler_params=params(40 if size == block else 62),
        cost_estimate=cost(15),
        name="attend_back",
    )(info, lens, *pieces, ranks, vecs, in_hbm(w_qkv), in_hbm(w_out), in_hbm(qkv_t), lse, in_hbm(mixed_t), in_hbm(gmiddle_n), *earlier)


def take_kernel(info, *refs):
    half = len(refs) // 2
    for source, target in zip(refs[:half], refs[half:]):
        target[...] = source[...]


def take_frames(info, array, ncol, group=0, groups=1):
    per = array.shape[0] // ncol // groups
    shape = (per,) + array.shape[1:]
    specs = [
        pl.BlockSpec(shape, lambda i, info, k=k: (lax.bitwise_xor(info[0], k) * groups + group, 0, 0))
        for k in range(1, ncol)
    ]
    return pl.pallas_call(
        take_kernel,
        grid_spec=pltpu.PrefetchScalarGridSpec(
            num_scalar_prefetch=1,
            grid=(1,),
            in_specs=specs,
            out_specs=[pl.BlockSpec(shape, lambda i, *_: (0, 0, 0))] * (ncol - 1),
        ),
        out_shape=[pltpu.HBM(shape, array.dtype)] * (ncol - 1),
        compiler_params=params(8),
        cost_estimate=cost(1),
        name="take_frames",
    )(info, *[in_hbm(array)] * (ncol - 1))


def place_kernel(info, *refs):
    *pieces, out = refs
    for k, piece in enumerate(pieces):

        @pl.when(pl.program_id(0) == k)
        def _(piece=piece):
            out[...] = piece[...].astype(out.dtype)


def place_frames(info, pieces, dtype):
    shape = pieces[0].shape
    return pl.pallas_call(
        place_kernel,
        grid_spec=pltpu.PrefetchScalarGridSpec(
            num_scalar_prefetch=1,
            grid=(len(pieces),),
            in_specs=[whole(shape)] * len(pieces),
            out_specs=pl.BlockSpec(shape, lambda k, info: (lax.bitwise_xor(info[0], k), 0, 0)),
        ),
        out_shape=pltpu.HBM((len(pieces) * shape[0],) + shape[1:], dtype),
        compiler_params=params(12),
        cost_estimate=cost(2),
        name="place_frames",
    )(info, *pieces)


def pick(array, index, axis):
    return lax.dynamic_index_in_dim(array, index, axis, keepdims=False)


class Comm:
    def __init__(self, mesh):
        self.ncol = mesh.shape["col"]
        self.nclip = mesh.shape["clip"]
        self.nz = self.nclip // 2
        self.me = lax.axis_index("col")
        self.clip = lax.axis_index("clip")
        self.core = lax.rem(self.clip, 2)
        self.z = lax.div(self.clip, 2)

    def col_swap(self, array, distance):
        return lax.ppermute(array, "col", [(i, i ^ distance) for i in range(self.ncol)])

    def core_swap(self, array):
        return lax.ppermute(array, "clip", [(i, i ^ 1) for i in range(self.nclip)])

    def z_move(self, array, pairs):
        moves = [(2 * a + c, 2 * b + c) for a, b in pairs for c in range(2)]
        return lax.ppermute(array, "clip", moves)

    def z_swap(self, array, distance):
        return lax.ppermute(array, "clip", [(i, i ^ (2 * distance)) for i in range(self.nclip)])

    def halve(self, terms, bits):
        nbits = self.ncol.bit_length() - 1
        present = list(range(nbits - 1, -1, -1))
        for bit in bits:
            axis = present.index(bit)
            mine = lax.rem(lax.shift_right_logical(self.me, bit), 2)
            away = [pick(t, 1 - mine, axis) for t in terms]
            total = away[0]
            if len(away) > 1:
                total = add_low(away[0], away[1])
            landed = self.col_swap(total, 1 << bit)
            near = [pick(t, mine, axis) for t in terms]
            if len(near) > 1:
                near = [add_low(near[0], near[1])]
            terms = [near[0], landed]
            present.pop(axis)
        return add_low(terms[0], terms[1])

    def reduce_rows(self, grad):
        rows, depth = grad.shape
        part = rows // self.ncol // 4
        nbits = self.ncol.bit_length() - 1
        split = grad.reshape(self.ncol, 2, 2, part, depth)
        keep = pick(split, self.core, 1)
        landed = self.core_swap(pick(split, 1 - self.core, 1))
        order = list(range(nbits))
        half = nbits // 2
        orders = (order, order[half:] + order[:half])
        done = []
        for side in range(2):
            terms = [
                t[:, side].reshape((2,) * nbits + (part, depth)) for t in (keep, landed)
            ]
            done.append(self.halve(terms, orders[side]))
        total = jnp.concatenate(done, axis=0)
        total = self.sum_line(total)
        other = self.core_swap(total)
        first = self.core == 0
        return jnp.concatenate(
            [jnp.where(first, total, other), jnp.where(first, other, total)], axis=0
        )

    def sum_line(self, total):
        nz = self.nz
        for step in range(nz // 2 - 1):
            total = add_low(total, self.z_move(total, [(step, step + 1), (nz - 1 - step, nz - 2 - step)]))
        low, high = nz // 2 - 1, nz // 2
        total = add_low(total, self.z_move(total, [(low, high), (high, low)]))
        for step in range(nz // 2 - 1, 0, -1):
            landed = self.z_move(total, [(step, step - 1), (nz - 1 - step, nz - step)])
            takes = jnp.logical_or(self.z == step - 1, self.z == nz - step)
            total = jnp.where(takes, landed, total)
        return total


def qkv_kernel(info, gproj_t, normed_n, mlp_sums, *refs):
    *att, keep, send, total, vectors = refs
    c = pl.program_id(0)
    model = mlp_sums.shape[1]
    rows = total.shape[0] // 2
    part = model // 4
    total[...] = dot(gproj_t[...], normed_n[...])

    for i in range(4):

        @pl.when(c == i)
        def _(i=i):
            att_sums = att[0][...]
            for more in att[1:]:
                att_sums = att_sums + more[...]
            vectors[...] = jnp.zeros_like(vectors)
            vectors[0, 0:4, :part] = mlp_sums[0:4, i * part : (i + 1) * part]
            vectors[0, 4:5, :] = mlp_sums[4 + i : 5 + i]
            vectors[1, 0:2, :part] = att_sums[0:2, i * part : (i + 1) * part]
            start = i % 2 * 2 * part
            vectors[1, 2:3, : 2 * part] = att_sums[2 + i // 2 : 3 + i // 2, start : start + 2 * part]

    for side, target in enumerate((keep, send)):
        which = lax.bitwise_xor(info[1], side)
        target[0, :rows] = total[pl.ds(pl.multiple_of(which * rows, rows), rows), :].astype(BF16)
        target[0, rows:] = vectors[which].astype(BF16)


VECTOR_ROWS = 32


def qkv_call(info, gproj_t, normed_n, mlp_sums, att_sums):
    model = mlp_sums.shape[1]
    rows = 3 * model // 4
    block = (1, rows // 2 + VECTOR_ROWS, model)
    out = jax.ShapeDtypeStruct((4,) + block[1:], BF16)
    others = (normed_n, mlp_sums, *att_sums)
    return pl.pallas_call(
        qkv_kernel,
        grid_spec=pltpu.PrefetchScalarGridSpec(
            num_scalar_prefetch=1,
            grid=(4,),
            in_specs=[pl.BlockSpec((rows, gproj_t.shape[1]), lambda c, info: (c, 0))]
            + [whole(o.shape) for o in others],
            out_specs=[pl.BlockSpec(block, lambda c, info: (c, 0, 0))] * 2,
            scratch_shapes=[pltpu.VMEM((rows, model), F32), pltpu.VMEM((2, VECTOR_ROWS, model), F32)],
        ),
        out_shape=[out, out],
        compiler_params=params(24),
        cost_estimate=cost(6),
        name="grad_qkv",
    )(info, in_hbm(gproj_t), in_hbm(normed_n), *others[1:])


def sum_core_kernel(info, *refs):
    for i in range(4):
        refs[8 + i][...] = add_low(refs[i][...], refs[4 + i][...])


def sum_core(info, keep, landed):
    rows, depth = keep.shape[1] // 2, keep.shape[2]
    block = (1, rows, depth)

    def by_x(i, info, flip, side):
        return (2 * i + lax.bitwise_xor(info[2], flip), side, 0)

    def by_y(i, info, flip, side):
        return (2 * lax.bitwise_xor(info[3], flip) + i, side, 0)

    specs = [
        pl.BlockSpec(block, functools.partial(lambda i, info, fn, flip, side: fn(i, info, flip, side), fn=fn, flip=flip, side=side))
        for side, fn in enumerate((by_x, by_y))
        for flip in (1, 0)
    ]
    out = jax.ShapeDtypeStruct((2, rows, depth), BF16)
    return pl.pallas_call(
        sum_core_kernel,
        grid_spec=pltpu.PrefetchScalarGridSpec(
            num_scalar_prefetch=1,
            grid=(2,),
            in_specs=specs * 2,
            out_specs=[pl.BlockSpec(block, lambda i, info: (i, 0, 0))] * 4,
        ),
        out_shape=[out] * 4,
        compiler_params=params(16),
        cost_estimate=cost(2),
        name="sum_core",
    )(info, *[keep] * 4, *[landed] * 4)


def sum_first_kernel(info, keep_a, land_a, keep_b, land_b, send_a, stay_a, send_b, stay_b):
    for keep, land, send, stay, mine in (
        (keep_a, land_a, send_a, stay_a, info[3]),
        (keep_b, land_b, send_b, stay_b, info[2]),
    ):
        send[...] = add_low(keep[1 - mine], land[1 - mine])
        stay[...] = add_low(keep[mine], land[mine])


def sum_first(info, keep_a, land_a, keep_b, land_b):
    rows, depth = keep_a.shape[1:]
    out = jax.ShapeDtypeStruct((rows, depth), BF16)
    return pl.pallas_call(
        sum_first_kernel,
        grid_spec=pltpu.PrefetchScalarGridSpec(
            num_scalar_prefetch=1,
            grid=(1,),
            in_specs=[whole(keep_a.shape)] * 4,
            out_specs=[whole((rows, depth))] * 4,
        ),
        out_shape=[out] * 4,
        compiler_params=params(16),
        cost_estimate=cost(1),
        name="sum_first",
    )(info, keep_a, land_a, keep_b, land_b)


def sum_second_kernel(info, stay_a, land_a, stay_b, land_b, own, send):
    low, high = add_low(stay_a[...], land_a[...]), add_low(stay_b[...], land_b[...])
    own[...] = jnp.where(info[4] == 0, low, high)
    send[...] = jnp.where(info[4] == 0, high, low)


def sum_second(info, stay_a, land_a, stay_b, land_b):
    shape = stay_a.shape
    return pl.pallas_call(
        sum_second_kernel,
        grid_spec=pltpu.PrefetchScalarGridSpec(
            num_scalar_prefetch=1, grid=(1,), in_specs=[whole(shape)] * 4, out_specs=[whole(shape)] * 2
        ),
        out_shape=[jax.ShapeDtypeStruct(shape, BF16)] * 2,
        compiler_params=params(16),
        cost_estimate=cost(1),
        name="sum_second",
    )(info, stay_a, land_a, stay_b, land_b)


def collect(info, parts, full):
    rows = parts[0].shape[0]
    for i, part in enumerate(parts):
        at = lax.bitwise_xor(info[4], i % 2) * rows
        full[lax.bitwise_xor(info[1], i // 2), pl.ds(pl.multiple_of(at, rows), rows), :] = part[...]


def finish_down_kernel(info, *refs):
    *parts, down_t, full = refs
    collect(info, parts, full)
    model, part = full.shape[2], down_t.shape[0]
    blocks = full.shape[1] // part
    for half in range(2):
        for j in range(blocks):
            at = (half * blocks + j) * model
            down_t[:, at : at + model] = full[half, j * part : (j + 1) * part].astype(F32)


def finish_up_kernel(info, *refs):
    *parts, up, out_t, full = refs
    collect(info, parts, full)
    model, chunk = up.shape[0], full.shape[2]
    for half in range(2):
        cut = slice(half * chunk, (half + 1) * chunk)
        up[:, cut] = full[half, :model].astype(F32)
        out_t[:, cut] = full[half, model:].astype(F32)


def finish_qkv_kernel(info, *refs):
    *parts, qkv_t, gain_one, shift_one, bias_qv, gain_two, shift_two, bias_out, bias_down, bias_up, full = refs
    collect(info, parts, full)
    rows = qkv_t.shape[0] // 2
    for half in range(2):
        qkv_t[half * rows : (half + 1) * rows] = full[half, :rows].astype(F32)
    mlp_rows = full[0, rows : rows + 16].astype(F32)
    att_rows = full[1, rows : rows + 16].astype(F32)
    for source, targets in ((mlp_rows, (gain_two, shift_two, bias_out, bias_down, bias_up)), (att_rows, (gain_one, shift_one, bias_qv))):
        for i, target in enumerate(targets):
            target[...] = source[i, : target.shape[0]]


def finish(kernel, name, info, parts, shapes):
    rows, depth = parts[0].shape
    return pl.pallas_call(
        kernel,
        grid_spec=pltpu.PrefetchScalarGridSpec(
            num_scalar_prefetch=1,
            grid=(1,),
            in_specs=[whole((rows, depth))] * 4,
            out_specs=[whole(s) for s in shapes],
            scratch_shapes=[pltpu.VMEM((2, 2 * rows, depth), BF16)],
        ),
        out_shape=[pltpu.HBM(s, F32) for s in shapes],
        compiler_params=params(24),
        cost_estimate=cost(2),
        name=name,
    )(info, *parts)


def wait_for(values, *others):
    flat, tree = jax.tree.flatten(values)
    held = lax.optimization_barrier((tuple(flat), others))[0]
    return jax.tree.unflatten(tree, held)


def join(*values):
    flat, tree = jax.tree.flatten(values)
    return jax.tree.unflatten(tree, lax.optimization_barrier(tuple(flat)))


def make(mesh):
    def on_device(
        frames,
        cotangent,
        frame_len,
        column_rank,
        gain_one,
        shift_one,
        w_qkv,
        bias_qv,
        w_out,
        bias_out,
        gain_two,
        shift_two,
        w_up,
        bias_up,
        w_down,
        bias_down,
    ):
        comm = Comm(mesh)
        ncol, me = comm.ncol, comm.me
        count, width, model = frames.shape
        hidden_size = w_down.shape[0]
        per = count // ncol
        size = ncol * width
        groups = 2 if per % 2 == 0 else 1
        part = per // groups
        middle_z = jnp.logical_or(comm.z == 1, comm.z == 2)
        info = jnp.stack([me, comm.core, lax.rem(me, 2), lax.div(me, 2), middle_z.astype(me.dtype)]).astype(jnp.int32)
        order = lax.bitwise_xor(me, jnp.arange(ncol, dtype=jnp.int32))
        ranks = column_rank.reshape(ncol, width)[order].reshape(size, 1)
        lens = pick(frame_len.reshape(ncol, per), me, 0)
        given = [gain_one, shift_one, bias_out, gain_two, shift_two, bias_down, bias_qv, bias_up]
        total, at, vecs = sum(v.size for v in given), 0, 0.0
        for v in given:
            vecs = vecs + jnp.pad(v.astype(F32), (at, total - at - v.size))
            at += v.size
        vecs = vecs.reshape(-1, model)

        def swap(pieces):
            return [comm.col_swap(p, k + 1) for k, p in enumerate(pieces)]

        paired = ncol == 4 and comm.nz == 4

        class Chunk:
            land = ()

            def core(self, keep, land):
                sa, self.ka, sb, self.kb = sum_core(info, keep, land)
                self.land = [comm.col_swap(sa, 1), comm.col_swap(sb, 2)]

            def first(self):
                sa, self.ka, sb, self.kb = sum_first(info, self.ka, self.land[0], self.kb, self.land[1])
                self.land = [comm.col_swap(sa, 2), comm.col_swap(sb, 1)]

            def second(self):
                self.own, send = sum_second(info, self.ka, self.land[0], self.kb, self.land[1])
                self.land = comm.z_swap(send, 1)

            def inner(self):
                self.own = add_low(self.own, self.land)
                self.land = comm.z_swap(self.own, 3)

            def outer(self):
                self.own = add_low(self.own, self.land)
                self.land = [comm.z_swap(self.own, 1), comm.core_swap(self.own)]

            def swap(self):
                self.parts = [self.own] + self.land
                self.land = comm.core_swap(self.parts[1])

            def last(self, kernel, name, shapes):
                return finish(kernel, name, info, self.parts + [self.land], shapes)

        landed = swap(take_frames(info, frames, ncol))
        cot_send = take_frames(info, cotangent, ncol)
        landed[0], cot_send, ranks, vecs, lens = join(landed[0], cot_send, ranks, vecs, lens)
        cot_land = swap(cot_send)
        rows = [frames, *join(*landed)]
        kept = attend_call(info, lens, rows, ranks, vecs, w_qkv, w_out, 0, per, per)
        kept, landed = join(kept, cot_land)
        qkv_t, mixed_t, middle_n, lse = kept
        cots = [cotangent, *landed]
        results = mlp_call(info, cots, middle_n, mixed_t, vecs, w_up, w_down)
        *outs, gmiddle_n, mlp_sums, down_keep, down_send, up_keep, up_send = join(*results)

        def back(gmiddle_n, g, earlier=()):
            return attend_back_call(
                info, lens, rows, ranks, vecs, w_qkv, w_out, qkv_t, lse, mixed_t, gmiddle_n, g * part, part, per, earlier
            )

        if not paired:
            out_land = swap(outs[1:])
            att_sums, earlier = 0.0, ()
            for g in range(groups):
                gproj_t, normed, sums, *gouts = back(gmiddle_n, g, earlier)
                att_sums, earlier = att_sums + sums, (gproj_t, normed, *gouts)
            output = place_frames(info, [outs[0]] + out_land, BF16)
            grad_input = place_frames(info, [gouts[0]] + swap(gouts[1:]), F32)
            first = comm.core == 0
            steps, part = hidden_size // model, model // 4

            def halves(keep, send):
                return jnp.stack([jnp.where(first, keep, send), jnp.where(first, send, keep)])

            def reduced(grad):
                return comm.reduce_rows(grad.astype(BF16)).astype(F32).T

            grad = halves(up_keep, up_send)
            grad_w_up = reduced(grad[:, :, :model].transpose(1, 0, 3, 2).reshape(hidden_size, model))
            grad_w_out = reduced(grad[:, :, model:].transpose(1, 2, 0, 3).reshape(model, model))
            grad = halves(down_keep, down_send).reshape(2, 4, steps // 2, part, model).transpose(1, 3, 0, 2, 4)
            grad_w_down = reduced(grad.reshape(model, hidden_size))
            grad_w_qkv = reduced(dot(gproj_t, normed))
            sums = jnp.concatenate([mlp_sums, att_sums])
            sums = reduced(jnp.concatenate([sums] * ncol)).T

            def own(row, rows=1):
                return pick(sums[row : row + rows].reshape(ncol, -1), me, 0)

            return (
                output, grad_input, own(16), own(17), grad_w_qkv, own(18, 2), grad_w_out, own(2), own(0), own(1),
                grad_w_up, own(4, steps), grad_w_down, own(3),
            )

        down, up, qkv = Chunk(), Chunk(), Chunk()
        down_land, up_land = comm.core_swap(down_send), comm.core_swap(up_send)
        down.core(down_keep, down_land)
        results = back(wait_for(gmiddle_n, down.ka), 0)
        down.land, up_land, results = join(down.land, up_land, results)
        gproj_t, normed, att_sums_a, *gouts = results

        down.first()
        up.core(up_keep, wait_for(up_land, down.ka))
        results = back(wait_for(gmiddle_n, up.ka), 1, (gproj_t, normed, *gouts))
        gproj_t, normed, att_sums_b, *gouts = results
        results_q = qkv_call(info, gproj_t, normed, mlp_sums, (att_sums_a, att_sums_b))
        down.land, up.land, gouts, results_q = join(down.land, up.land, gouts, results_q)
        qkv_keep, qkv_send = results_q

        qkv_land = comm.core_swap(qkv_send)
        up.land = wait_for(up.land, qkv_send)
        up.first()
        down.land = wait_for(down.land, up.ka)
        down.second()
        qkv_land, up.land, down.land, down.own, outs = join(qkv_land, up.land, down.land, down.own, outs)

        qkv.core(qkv_keep, qkv_land)
        down.land = wait_for(down.land, qkv.ka)
        down.inner()
        up.land = wait_for(up.land, down.own)
        up.second()
        qkv.land, up.land, down.own, up.own, outs = join(qkv.land, up.land, down.own, up.own, outs)

        qkv.first()
        up.land = wait_for(up.land, qkv.ka)
        up.inner()
        out_land = swap(outs[1:])
        qkv.land, down.land, down.own, up.own, gouts = join(qkv.land, down.land, down.own, up.own, gouts)

        qkv.second()
        gouts, down.land = wait_for((gouts, down.land), qkv.own)
        gin_land = swap(gouts[1:])
        down.outer()
        qkv.land, up.land, out_land, qkv.own, down.own = join(qkv.land, up.land, out_land, qkv.own, down.own)

        qkv.inner()
        up.land = wait_for(up.land, qkv.own)
        up.outer()
        down.land = wait_for(down.land, up.own)
        down.swap()
        output = place_frames(info, [outs[0], *wait_for(out_land, up.own)], BF16)
        qkv.land, up.land, down.land, gin_land, qkv.own, up.own, output = join(
            qkv.land, up.land, down.land, gin_land, qkv.own, up.own, output
        )

        qkv.outer()
        up.land = wait_for(up.land, qkv.own)
        up.swap()
        grad_input = place_frames(info, [gouts[0], *wait_for(gin_land, up.parts[1])], F32)
        down.parts, down.land = wait_for((down.parts, down.land), grad_input)
        (grad_w_down,) = down.last(finish_down_kernel, "finish_down", [(model // 4, hidden_size)])
        qkv.land, up.land, up.parts, qkv.own, grad_w_down = join(qkv.land, up.land, up.parts, qkv.own, grad_w_down)

        qkv.swap()
        up.parts, up.land = wait_for((up.parts, up.land), qkv.parts[0])
        grad_w_up, grad_w_out = up.last(
            finish_up_kernel, "finish_up", [(model, hidden_size // 4), (model // 4, model)]
        )
        qkv.land, qkv.parts, grad_w_up = join(qkv.land, qkv.parts, grad_w_up)
        part = model // 4
        vectors = [(part,), (part,), (2 * part,), (part,), (part,), (part,), (part,), (hidden_size // 4,)]
        grad_w_qkv, g_gain_one, g_shift_one, g_bias_qv, g_gain_two, g_shift_two, g_bias_out, g_bias_down, g_bias_up = qkv.last(
            finish_qkv_kernel, "finish_qkv", [(3 * model // 4, model)] + vectors
        )
        grad_w_qkv, grad_w_out, grad_w_down = grad_w_qkv.T, grad_w_out.T, grad_w_down.T
        return (
            output,
            grad_input,
            g_gain_one,
            g_shift_one,
            grad_w_qkv,
            g_bias_qv,
            grad_w_out,
            g_bias_out,
            g_gain_two,
            g_shift_two,
            grad_w_up,
            g_bias_up,
            grad_w_down,
            g_bias_down,
        )

    return on_device


def solution(mesh):
    return jax.shard_map(
        make(mesh),
        mesh=mesh,
        in_specs=(P("clip", "col", None), P("clip", "col", None), P("clip")) + (P(),) * 13,
        out_specs=(
            P("clip", "col", None),
            P("clip", "col", None),
            P("col"),
            P("col"),
            P(None, "col"),
            P("col"),
            P(None, "col"),
            P("col"),
            P("col"),
            P("col"),
            P(None, "col"),
            P("col"),
            P(None, "col"),
            P("col"),
        ),
        check_vma=False,
    )
```

profile of v0, /device:TPU:17, one launch (start us, length us, event | category | flops | bytes accessed | tf_op | source)
XLA Modules:
  0.0 232.4 jit_solution(3109554684699870885)
XLA Ops:
  0.8 2.8 %take_frames.2 = (bf16[4,64,768]{2,1,0:T(8,128)(2,1)}, bf16[4,64,768]{2,1,0:T(8,128)(2,1)}, bf16[4,64,768]{2,1,0:T(8,128)(2,1)}) custom-call(s32[5]{0:T(128)S(1)} %stack.27.info, bf16[16,64,768]{2,1,0:T(8,128)(2,1)} %refs_0_.11, bf16[16,64,768]{2,1,0:T(8,128)(2,1)} %refs_0_.11, bf16[16,64,768]{2,1,0:T(8,128)(2,1)} %refs_0_.11), custom_call_target="tpu_custom_call" | custom-call | bytes 1500000 | tf_op jit(solution)/shard_map/take_frames/pallas_call | solution.py:584
  3.7 1.2 collective-permute-start
  4.9 1.2 collective-permute-start.1
  7.3 2.8 %take_frames.3 = (bf16[4,64,768]{2,1,0:T(8,128)(2,1)}, bf16[4,64,768]{2,1,0:T(8,128)(2,1)}, bf16[4,64,768]{2,1,0:T(8,128)(2,1)}) custom-call(s32[5]{0:T(128)S(1)} %stack.27.info, bf16[16,64,768]{2,1,0:T(8,128)(2,1)} %refs_0_.9, bf16[16,64,768]{2,1,0:T(8,128)(2,1)} %refs_0_.9, bf16[16,64,768]{2,1,0:T(8,128)(2,1)} %refs_0_.9), custom_call_target="tpu_custom_call" | custom-call | bytes 1500000 | tf_op jit(solution)/shard_map/take_frames/pallas_call | solution.py:584
  10.1 3.8 %collective-permute-done.refs_1_ = bf16[4,64,768]{2,1,0:T(8,128)(2,1)S(1)} collective-permute-done((bf16[4,64,768]{2,1,0:T(8,128)(2,1)}, bf16[4,64,768]{2,1,0:T(8,128)(2,1)S(1)}, u32[]{:S(2)}, u32[]{:S(2)}) %collective-permute-start) | collective-permute-done | bytes 393248 | tf_op jit(solution)/shard_map/ppermute | solution.py:640
  13.9 1.2 collective-permute-start.3
  15.1 1.2 collective-permute-start.4
  16.7 6.6 %collective-permute-done.2.refs_3_ = bf16[4,64,768]{2,1,0:T(8,128)(2,1)S(1)} collective-permute-done((bf16[4,64,768]{2,1,0:T(8,128)(2,1)}, bf16[4,64,768]{2,1,0:T(8,128)(2,1)S(1)}, u32[]{:S(2)}, u32[]{:S(2)}) %collective-permute-start.2) | collective-permute-done | bytes 393248 | tf_op jit(solution)/shard_map/ppermute | solution.py:640
  23.3 15.8 %attend.1 = (bf16[2304,1024]{1,0:T(8,128)(2,1)}, bf16[768,1024]{1,0:T(8,128)(2,1)}, f32[1024,768]{1,0:T(8,128)}, f32[4,16,256]{2,1,0:T(8,128)}) custom-call(s32[5]{0:T(128)S(1)} %stack.27.info, s32[4]{0:T(128)S(1)} %dynamic-slice_bitcast_fusion.lens, bf16[16,64,768]{2,1,0:T(8,128)(2,1)S(1)} %copy-done, bf16[4,64,768]{2,1,0:T(8,128)(2,1)S(1)} %collective-permute-done.refs_1_, ...), custom_call_target="tpu_custom_call" | custom-call | bytes 15000000 | tf_op jit(solution)/shard_map/attend/pallas_call | solution.py:189
  39.1 2.5 %collective-permute-done.4.refs_2_ = bf16[4,64,768]{2,1,0:T(8,128)(2,1)} collective-permute-done((bf16[4,64,768]{2,1,0:T(8,128)(2,1)}, bf16[4,64,768]{2,1,0:T(8,128)(2,1)}, u32[]{:S(2)}, u32[]{:S(2)}) %collective-permute-start.4) | collective-permute-done | bytes 393248 | tf_op jit(solution)/shard_map/ppermute | solution.py:640
  41.5 44.2 %mlp.1 = (bf16[4,64,768]{2,1,0:T(8,128)(2,1)}, bf16[4,64,768]{2,1,0:T(8,128)(2,1)}, bf16[4,64,768]{2,1,0:T(8,128)(2,1)}, bf16[4,64,768]{2,1,0:T(8,128)(2,1)}, f3...) custom-call(s32[5]{0:T(128)} %copy-done.8, ...), custom_call_target="tpu_custom_call" | custom-call | bytes 60000000 | tf_op jit(solution)/shard_map/mlp/pallas_call | solution.py:375
  85.8 1.1 collective-permute-start.6
  86.9 4.3 %collective-permute-done.6.refs_4_.refs_5_.refs_6_.refs_7_ = bf16[4,384,768]{2,1,0:T(8,128)(2,1)S(1)} collective-permute-done((bf16[4,384,768]{2,1,0:T(8,128)(2,1)}, bf16[4,384,768]{2,1,0:T(8,128)(2,1)S(1)}, u32[]{:S(2)}, u32[]{:S(2)}) %collective-permute-start.6) | collective-permute-done | bytes 2359328 | tf_op jit(solution)/shard_map/ppermute | solution.py:643
  91.2 1.7 copy-done.2
  92.9 1.1 sum_core.3
  94.0 1.3 collective-permute-start.7
  95.6 13.9 %attend_back.2 = (bf16[2304,1024]{1,0:T(8,128)(2,1)}, bf16[1024,768]{1,0:T(8,128)(2,1)}, f32[16,768]{1,0:T(8,128)}, bf16[4,64,768]{2,1,0:T(8,128)(2,1)}, bf16[4,...) custom-call(s32[5]{0:T(128)S(1)} %copy-done.9, ...), custom_call_target="tpu_custom_call" | custom-call | bytes 22500000 | tf_op jit(solution)/shard_map/attend_back/pallas_call | solution.py:524
  109.6 0.8 sum_first.3
  110.4 1.3 sum_core.4
  111.7 1.5 collective-permute-start.12
  113.4 1.2 collective-permute-start.10
  114.7 13.3 %attend_back.3 = (bf16[2304,1024]{1,0:T(8,128)(2,1)}, bf16[1024,768]{1,0:T(8,128)(2,1)}, f32[16,768]{1,0:T(8,128)}, bf16[4,64,768]{2,1,0:T(8,128)(2,1)}, bf16[4,...) custom-call(s32[5]{0:T(128)S(1)} %copy-done.9, ...), custom_call_target="tpu_custom_call", output_to_operand_aliasing={{0}: (14, {}), {1}: (15, {}), {3}: (16, {}), {4}: (17, {}),... | custom-call | bytes 22500000 | tf_op jit(solution)/shard_map/attend_back/pallas_call | solution.py:524
  128.0 0.8 copy-done.12
  128.8 7.3 %grad_qkv.1 = (bf16[4,320,768]{2,1,0:T(8,128)(2,1)S(1)}, bf16[4,320,768]{2,1,0:T(8,128)(2,1)S(1)}) custom-call(s32[5]{0:T(128)S(1)} %copy-done.9, bf16[2304,1024]{1,0:T(8,128)(2,1)} %get-tuple-element.285.gproj_t, bf16[1024,768]{1,0:T(8,128)(2,1)} %get-tuple-element.286.normed_n, f32[16,768]{1,0:T(8,128)S(1)} %copy-done.10, f32[16,768]{1,0:T(8,128)S(1)} %copy-done.11, ...), custom_call_target="tpu_custom_call" | custom-call | bytes 9000000 | tf_op jit(solution)/shard_map/grad_qkv/pallas_call | solution.py:744
  136.2 2.7 %collective-permute-start.14 = (bf16[4,320,768]{2,1,0:T(8,128)(2,1)S(1)}, bf16[4,320,768]{2,1,0:T(8,128)(2,1)S(1)}, u32[]{:S(2)}, u32[]{:S(2)}) collective-permute-start(bf16[4,320,768]{2,1,0:T(8,128)(2,1)S(1)} %get-tuple-element.293), channel_id=1, source_target_pairs={{0,4},{4,0},{8,12},{12,8},{16,20},{20,16},{24,28},{28,24},{1,5},{5... | collective-permute-start | bytes 5898248 | tf_op jit(solution)/shard_map/ppermute | solution.py:643
  138.9 0.9 sum_first.4
  139.8 0.7 collective-permute-start.15
  140.5 1.1 collective-permute-start.16
  141.6 0.7 sum_second.3
  142.3 1.4 collective-permute-start.17
  143.6 6.7 %collective-permute-done.17 = bf16[192,768]{1,0:T(8,128)(2,1)S(1)} collective-permute-done((bf16[192,768]{1,0:T(8,128)(2,1)S(1)}, bf16[192,768]{1,0:T(8,128)(2,1)S(1)}, u32[]{:S(2)}, u32[]{:S(2)}) %collective-permute-start.17) | collective-permute-done | bytes 294944 | tf_op jit(solution)/shard_map/ppermute | solution.py:650
  150.4 1.3 sum_core.5
  151.7 1.1 collective-permute-start.18
  153.5 0.8 sum_second.4
  154.3 1.4 collective-permute-start.20
  155.7 7.1 %collective-permute-done.20 = bf16[480,384]{1,0:T(8,128)(2,1)S(1)} collective-permute-done((bf16[480,384]{1,0:T(8,128)(2,1)S(1)}, bf16[480,384]{1,0:T(8,128)(2,1)S(1)}, u32[]{:S(2)}, u32[]{:S(2)}) %collective-permute-start.20) | collective-permute-done | bytes 368672 | tf_op jit(solution)/shard_map/ppermute | solution.py:650
  163.1 1.1 collective-permute-done.19.land_b
  164.2 0.8 sum_first.5
  166.2 0.9 collective-permute-start.26
  167.1 0.9 collective-permute-start.27
  168.0 0.9 collective-permute-start.28
  169.0 1.1 collective-permute-done.21.land_a
  170.7 0.7 sum_second.5
  171.4 2.6 %collective-permute-start.24 = (bf16[160,768]{1,0:T(8,128)(2,1)S(1)}, bf16[160,768]{1,0:T(8,128)(2,1)S(1)}, u32[]{:S(2)}, u32[]{:S(2)}) collective-permute-start(bf16[160,768]{1,0:T(8,128)(2,1)S(1)} %get-tuple-element.348), channel_id=1, source_target_pairs={{0,8},{4,12},{8,0},{12,4},{16,24},{20,28},{24,16},{28,20},{1,9},{5... | collective-permute-start | bytes 737288 | tf_op jit(solution)/shard_map/ppermute | solution.py:650
  174.1 6.7 %collective-permute-done.25 = bf16[480,384]{1,0:T(8,128)(2,1)S(1)} collective-permute-done((bf16[480,384]{1,0:T(8,128)(2,1)S(1)}, bf16[480,384]{1,0:T(8,128)(2,1)S(1)}, u32[]{:S(2)}, u32[]{:S(2)}) %collective-permute-start.25) | collective-permute-done | bytes 368672 | tf_op jit(solution)/shard_map/ppermute | solution.py:650
  180.8 4.6 %collective-permute-start.33 = (bf16[192,768]{1,0:T(8,128)(2,1)S(1)}, bf16[192,768]{1,0:T(8,128)(2,1)S(1)}, u32[]{:S(2)}, u32[]{:S(2)}) collective-permute-start(bf16[192,768]{1,0:T(8,128)(2,1)S(1)} %add_convert_fusion.2.refs_0_), channel_id=1, source_target_pairs={{0,4},{4,0},{8,12},{12,8},{16,20},{20,16},{24,28},{28,24},{1,5},{5... | collective-permute-start | bytes 884744 | tf_op jit(solution)/shard_map/ppermute | solution.py:643
  185.3 8.2 %collective-permute-start.32 = (bf16[192,768]{1,0:T(8,128)(2,1)S(1)}, bf16[192,768]{1,0:T(8,128)(2,1)S(1)}, u32[]{:S(2)}, u32[]{:S(2)}) collective-permute-start(bf16[192,768]{1,0:T(8,128)(2,1)S(1)} %add_convert_fusion.2.refs_0_), channel_id=1, source_target_pairs={{0,8},{4,12},{8,0},{12,4},{16,24},{20,28},{24,16},{28,20},{1,9},{5... | collective-permute-start | bytes 884744 | tf_op jit(solution)/shard_map/ppermute | solution.py:650
  194.0 0.9 collective-permute-start.36
  194.9 1.3 collective-permute-start.37
  196.4 1.2 collective-permute-start.31
  197.6 3.3 %collective-permute-done.32.refs_1_ = bf16[192,768]{1,0:T(8,128)(2,1)S(1)} collective-permute-done((bf16[192,768]{1,0:T(8,128)(2,1)S(1)}, bf16[192,768]{1,0:T(8,128)(2,1)S(1)}, u32[]{:S(2)}, u32[]{:S(2)}) %collective-permute-start.32) | collective-permute-done | bytes 294944 | tf_op jit(solution)/shard_map/ppermute | solution.py:650
  201.0 1.3 collective-permute-start.30
  202.2 1.8 collective-permute-done.35.refs_1_
  204.0 1.8 collective-permute-start.34
  205.8 2.3 place_frames.2
  208.1 4.8 %collective-permute-done.37.refs_3_ = bf16[4,64,768]{2,1,0:T(8,128)(2,1)S(1)} collective-permute-done((bf16[4,64,768]{2,1,0:T(8,128)(2,1)S(1)}, bf16[4,64,768]{2,1,0:T(8,128)(2,1)S(1)}, u32[]{:S(2)}, u32[]{:S(2)}) %collective-permute-start.37) | collective-permute-done | bytes 393248 | tf_op jit(solution)/shard_map/ppermute | solution.py:640
  212.9 5.5 %collective-permute-done.29 = bf16[160,768]{1,0:T(8,128)(2,1)S(1)} collective-permute-done((bf16[160,768]{1,0:T(8,128)(2,1)S(1)}, bf16[160,768]{1,0:T(8,128)(2,1)S(1)}, u32[]{:S(2)}, u32[]{:S(2)}) %collective-permute-start.29) | collective-permute-done | bytes 245792 | tf_op jit(solution)/shard_map/ppermute | solution.py:650
  218.5 1.1 collective-permute-start.40
  219.7 2.7 %place_frames.3 = f32[16,64,768]{2,1,0:T(8,128)} custom-call(s32[5]{0:T(128)S(1)} %copy-done.9, bf16[4,64,768]{2,1,0:T(8,128)(2,1)S(1)} %copy-done.3, bf16[4,64,768]{2,1,0:T(8,128)(2,1)S(1)} %collective-permute-done.35.refs_1_, bf16[4,64,768]{2,1,0:T(8,128)(2,1)S(1)} %collective-permute-done.36.refs_2_, bf16[4,64,768]{2,1,0:T(8,128)(2,1)S(1)} %collective-permute-done.37.refs_3_), custom_call_target="tpu_custom_call" | custom-call | bytes 3000000 | tf_op jit(solution)/shard_map/place_frames/pallas_call | solution.py:610
  222.4 2.2 finish_down.1
  224.6 2.2 collective-permute-done.38.refs_1_
  226.8 1.3 collective-permute-start.41
  228.1 2.4 %finish_up.1 = (f32[768,768]{1,0:T(8,128)}, f32[192,768]{1,0:T(8,128)}) custom-call(s32[5]{0:T(128)S(1)} %copy-done.9, bf16[480,384]{1,0:T(8,128)(2,1)S(1)} %add_convert_fusion.refs_0_, bf16[480,384]{1,0:T(8,128)(2,1)S(1)} %collective-permute-done.30.refs_1_, bf16[480,384]{1,0:T(8,128)(2,1)S(1)} %collective-permute-done.31.refs_2_, ...), custom_call_target="tpu_custom_call" | custom-call | bytes 3000000 | tf_op jit(solution)/shard_map/finish_up/pallas_call | solution.py:887
  230.5 1.9 finish_qkv.1
  (118 shorter events, 6.2 us)
Async XLA Ops:
  0.7 22.5 %copy-start.8 = (s32[5]{0:T(128)}, s32[5]{0:T(128)S(1)}, u32[]{:S(2)}) copy-start(s32[5]{0:T(128)S(1)} %stack.27.info) | copy-start | bytes 64
  0.8 6.3 %copy-start.17 = (bf16[3072]{0:T(1024)(128)(2,1)S(1)}, bf16[3072]{0:T(1024)(128)(2,1)}, u32[]{:S(2)}) copy-start(bf16[3072]{0:T(1024)(128)(2,1)} %param.29) | copy-start | bytes 18436
  0.8 6.3 %copy-start.18 = (bf16[1536]{0:T(1024)(128)(2,1)S(1)}, bf16[1536]{0:T(1024)(128)(2,1)}, u32[]{:S(2)}) copy-start(bf16[1536]{0:T(1024)(128)(2,1)} %param.23) | copy-start | bytes 9220
  0.8 6.3 %copy-start.19 = (bf16[768]{0:T(1024)(128)(2,1)S(1)}, bf16[768]{0:T(1024)(128)(2,1)}, u32[]{:S(2)}) copy-start(bf16[768]{0:T(1024)(128)(2,1)} %param.31) | copy-start | bytes 4612
  0.8 6.3 %copy-start.20 = (bf16[768]{0:T(1024)(128)(2,1)S(1)}, bf16[768]{0:T(1024)(128)(2,1)}, u32[]{:S(2)}) copy-start(bf16[768]{0:T(1024)(128)(2,1)} %param.27) | copy-start | bytes 4612
  0.8 6.3 %copy-start.21 = (bf16[768]{0:T(1024)(128)(2,1)S(1)}, bf16[768]{0:T(1024)(128)(2,1)}, u32[]{:S(2)}) copy-start(bf16[768]{0:T(1024)(128)(2,1)} %param.26) | copy-start | bytes 4612
  0.8 6.3 %copy-start.22 = (bf16[768]{0:T(1024)(128)(2,1)S(1)}, bf16[768]{0:T(1024)(128)(2,1)}, u32[]{:S(2)}) copy-start(bf16[768]{0:T(1024)(128)(2,1)} %param.25) | copy-start | bytes 4612
  0.8 6.3 %copy-start.23 = (bf16[768]{0:T(1024)(128)(2,1)S(1)}, bf16[768]{0:T(1024)(128)(2,1)}, u32[]{:S(2)}) copy-start(bf16[768]{0:T(1024)(128)(2,1)} %param.21) | copy-start | bytes 4612
  3.7 10.2 %collective-permute-start = (bf16[4,64,768]{2,1,0:T(8,128)(2,1)}, bf16[4,64,768]{2,1,0:T(8,128)(2,1)S(1)}, u32[]{:S(2)}, u32[]{:S(2)}) collective-permute-start(bf16[4,64,768]{2,1,0:T(8,128)(2,1)} %get-tuple-element.220), channel_id=1, source_target_pairs={{0,1},{1,0},{2,3},{3,2},{4,5},{5,4},{6,7},{7,6},{8,9},{9,8},{10,11... | collective-permute-start | bytes 1179656 | tf_op jit(solution)/shard_map/ppermute | solution.py:640
  4.9 11.8 %collective-permute-start.1 = (bf16[4,64,768]{2,1,0:T(8,128)(2,1)}, bf16[4,64,768]{2,1,0:T(8,128)(2,1)S(1)}, u32[]{:S(2)}, u32[]{:S(2)}) collective-permute-start(bf16[4,64,768]{2,1,0:T(8,128)(2,1)} %get-tuple-element.226), channel_id=1, source_target_pairs={{0,2},{1,3},{2,0},{3,1},{4,6},{5,7},{6,4},{7,5},{8,10},{9,11},{10,... | collective-permute-start | bytes 1179656 | tf_op jit(solution)/shard_map/ppermute | solution.py:640
  6.1 17.2 %collective-permute-start.2 = (bf16[4,64,768]{2,1,0:T(8,128)(2,1)}, bf16[4,64,768]{2,1,0:T(8,128)(2,1)S(1)}, u32[]{:S(2)}, u32[]{:S(2)}) collective-permute-start(bf16[4,64,768]{2,1,0:T(8,128)(2,1)} %get-tuple-element.227), channel_id=1, source_target_pairs={{0,3},{1,2},{2,1},{3,0},{4,7},{5,6},{6,5},{7,4},{8,11},{9,10},{10,... | collective-permute-start | bytes 1179656 | tf_op jit(solution)/shard_map/ppermute | solution.py:640
  7.3 16.0 %copy-start.4 = (f32[12,768]{1,0:T(8,128)}, f32[12,768]{1,0:T(8,128)S(1)}, u32[]{:S(2)}) copy-start(f32[12,768]{1,0:T(8,128)S(1)} %reshape.58.refs_5_.refs_6_) | copy-start | bytes 110596
  7.3 16.0 %copy-start = (bf16[16,64,768]{2,1,0:T(8,128)(2,1)S(1)}, bf16[16,64,768]{2,1,0:T(8,128)(2,1)}, u32[]{:S(2)}) copy-start(bf16[16,64,768]{2,1,0:T(8,128)(2,1)} %refs_0_.11) | copy-start | bytes 4718596
  13.9 25.2 %collective-permute-start.3 = (bf16[4,64,768]{2,1,0:T(8,128)(2,1)}, bf16[4,64,768]{2,1,0:T(8,128)(2,1)S(1)}, u32[]{:S(2)}, u32[]{:S(2)}) collective-permute-start(bf16[4,64,768]{2,1,0:T(8,128)(2,1)} %get-tuple-element.237), channel_id=1, source_target_pairs={{0,1},{1,0},{2,3},{3,2},{4,5},{5,4},{6,7},{7,6},{8,9},{9,8},{10,11... | collective-permute-start | bytes 1179656 | tf_op jit(solution)/shard_map/ppermute | solution.py:640
  15.1 26.4 %collective-permute-start.4 = (bf16[4,64,768]{2,1,0:T(8,128)(2,1)}, bf16[4,64,768]{2,1,0:T(8,128)(2,1)}, u32[]{:S(2)}, u32[]{:S(2)}) collective-permute-start(bf16[4,64,768]{2,1,0:T(8,128)(2,1)} %get-tuple-element.238), channel_id=1, source_target_pairs={{0,2},{1,3},{2,0},{3,1},{4,6},{5,7},{6,4},{7,5},{8,10},{9,11},{10,... | collective-permute-start | bytes 1179656 | tf_op jit(solution)/shard_map/ppermute | solution.py:640
  16.3 25.2 %collective-permute-start.5 = (bf16[4,64,768]{2,1,0:T(8,128)(2,1)}, bf16[4,64,768]{2,1,0:T(8,128)(2,1)}, u32[]{:S(2)}, u32[]{:S(2)}) collective-permute-start(bf16[4,64,768]{2,1,0:T(8,128)(2,1)} %get-tuple-element.239), channel_id=1, source_target_pairs={{0,3},{1,2},{2,1},{3,0},{4,7},{5,6},{6,5},{7,4},{8,11},{9,10},{10,... | collective-permute-start | bytes 1179656 | tf_op jit(solution)/shard_map/ppermute | solution.py:640
  41.5 49.7 %copy-start.9 = (s32[5]{0:T(128)S(1)}, s32[5]{0:T(128)}, u32[]{:S(2)}) copy-start(s32[5]{0:T(128)} %copy-done.8) | copy-start | bytes 64
  85.8 5.5 %collective-permute-start.6 = (bf16[4,384,768]{2,1,0:T(8,128)(2,1)}, bf16[4,384,768]{2,1,0:T(8,128)(2,1)S(1)}, u32[]{:S(2)}, u32[]{:S(2)}) collective-permute-start(bf16[4,384,768]{2,1,0:T(8,128)(2,1)} %get-tuple-element.246), channel_id=1, source_target_pairs={{0,4},{4,0},{8,12},{12,8},{16,20},{20,16},{24,28},{28,24},{1,5},{5... | collective-permute-start | bytes 7077896 | tf_op jit(solution)/shard_map/ppermute | solution.py:643
  86.9 22.7 %collective-permute-start.9 = (bf16[4,960,384]{2,1,0:T(8,128)(2,1)}, bf16[4,960,384]{2,1,0:T(8,128)(2,1)S(1)}, u32[]{:S(2)}, u32[]{:S(2)}) collective-permute-start(bf16[4,960,384]{2,1,0:T(8,128)(2,1)} %get-tuple-element.250), channel_id=1, source_target_pairs={{0,4},{4,0},{8,12},{12,8},{16,20},{20,16},{24,28},{28,24},{1,5},{5... | collective-permute-start | bytes 8847368 | tf_op jit(solution)/shard_map/ppermute | solution.py:643
  94.0 15.5 %collective-permute-start.7 = (bf16[2,192,768]{2,1,0:T(8,128)(2,1)S(1)}, bf16[2,192,768]{2,1,0:T(8,128)(2,1)S(1)}, u32[]{:S(2)}, u32[]{:S(2)}) collective-permute-start(bf16[2,192,768]{2,1,0:T(8,128)(2,1)S(1)} %get-tuple-element.248), channel_id=1, source_target_pairs={{0,1},{1,0},{2,3},{3,2},{4,5},{5,4},{6,7},{7,6},{8,9},{9,8},{10,11... | collective-permute-start | bytes 1769480 | tf_op jit(solution)/shard_map/ppermute | solution.py:640
  95.3 14.2 %collective-permute-start.8 = (bf16[2,192,768]{2,1,0:T(8,128)(2,1)S(1)}, bf16[2,192,768]{2,1,0:T(8,128)(2,1)S(1)}, u32[]{:S(2)}, u32[]{:S(2)}) collective-permute-start(bf16[2,192,768]{2,1,0:T(8,128)(2,1)S(1)} %get-tuple-element.249), channel_id=1, source_target_pairs={{0,2},{1,3},{2,0},{3,1},{4,6},{5,7},{6,4},{7,5},{8,10},{9,11},{10,... | collective-permute-start | bytes 1769480 | tf_op jit(solution)/shard_map/ppermute | solution.py:640
  95.6 14.8 %copy-start.1 = (bf16[4,960,384]{2,1,0:T(8,128)(2,1)S(1)}, bf16[4,960,384]{2,1,0:T(8,128)(2,1)}, u32[]{:S(2)}) copy-start(bf16[4,960,384]{2,1,0:T(8,128)(2,1)} %get-tuple-element.267.refs_0_.refs_1_.refs_2_.refs_3_) | copy-start | bytes 8847364
  111.7 24.5 %collective-permute-start.12 = (bf16[2,480,384]{2,1,0:T(8,128)(2,1)S(1)}, bf16[2,480,384]{2,1,0:T(8,128)(2,1)S(1)}, u32[]{:S(2)}, u32[]{:S(2)}) collective-permute-start(bf16[2,480,384]{2,1,0:T(8,128)(2,1)S(1)} %get-tuple-element.271), channel_id=1, source_target_pairs={{0,1},{1,0},{2,3},{3,2},{4,5},{5,4},{6,7},{7,6},{8,9},{9,8},{10,11... | collective-permute-start | bytes 2211848 | tf_op jit(solution)/shard_map/ppermute | solution.py:640
  113.2 23.1 %collective-permute-start.13 = (bf16[2,480,384]{2,1,0:T(8,128)(2,1)S(1)}, bf16[2,480,384]{2,1,0:T(8,128)(2,1)S(1)}, u32[]{:S(2)}, u32[]{:S(2)}) collective-permute-start(bf16[2,480,384]{2,1,0:T(8,128)(2,1)S(1)} %get-tuple-element.272), channel_id=1, source_target_pairs={{0,2},{1,3},{2,0},{3,1},{4,6},{5,7},{6,4},{7,5},{8,10},{9,11},{10,... | collective-permute-start | bytes 2211848 | tf_op jit(solution)/shard_map/ppermute | solution.py:640
  113.4 22.8 %collective-permute-start.10 = (bf16[192,768]{1,0:T(8,128)(2,1)S(1)}, bf16[192,768]{1,0:T(8,128)(2,1)S(1)}, u32[]{:S(2)}, u32[]{:S(2)}) collective-permute-start(bf16[192,768]{1,0:T(8,128)(2,1)S(1)} %get-tuple-element.265), channel_id=1, source_target_pairs={{0,2},{1,3},{2,0},{3,1},{4,6},{5,7},{6,4},{7,5},{8,10},{9,11},{10,... | collective-permute-start | bytes 884744 | tf_op jit(solution)/shard_map/ppermute | solution.py:640
  114.6 21.6 %collective-permute-start.11 = (bf16[192,768]{1,0:T(8,128)(2,1)S(1)}, bf16[192,768]{1,0:T(8,128)(2,1)S(1)}, u32[]{:S(2)}, u32[]{:S(2)}) collective-permute-start(bf16[192,768]{1,0:T(8,128)(2,1)S(1)} %get-tuple-element.266), channel_id=1, source_target_pairs={{0,1},{1,0},{2,3},{3,2},{4,5},{5,4},{6,7},{7,6},{8,9},{9,8},{10,11... | collective-permute-start | bytes 884744 | tf_op jit(solution)/shard_map/ppermute | solution.py:640
  114.7 13.3 %copy-start.10 = (f32[16,768]{1,0:T(8,128)S(1)}, f32[16,768]{1,0:T(8,128)}, u32[]{:S(2)}) copy-start(f32[16,768]{1,0:T(8,128)} %get-tuple-element.287.mlp_sums) | copy-start | bytes 147460
  114.7 13.3 %copy-start.11 = (f32[16,768]{1,0:T(8,128)S(1)}, f32[16,768]{1,0:T(8,128)}, u32[]{:S(2)}) copy-start(f32[16,768]{1,0:T(8,128)} %get-tuple-element.288.refs_0_) | copy-start | bytes 147460
  136.2 14.1 %collective-permute-start.14 = (bf16[4,320,768]{2,1,0:T(8,128)(2,1)S(1)}, bf16[4,320,768]{2,1,0:T(8,128)(2,1)S(1)}, u32[]{:S(2)}, u32[]{:S(2)}) collective-permute-start(bf16[4,320,768]{2,1,0:T(8,128)(2,1)S(1)} %get-tuple-element.293), channel_id=1, source_target_pairs={{0,4},{4,0},{8,12},{12,8},{16,20},{20,16},{24,28},{28,24},{1,5},{5... | collective-permute-start | bytes 5898248 | tf_op jit(solution)/shard_map/ppermute | solution.py:643
  139.8 10.5 %collective-permute-start.15 = (bf16[480,384]{1,0:T(8,128)(2,1)S(1)}, bf16[480,384]{1,0:T(8,128)(2,1)S(1)}, u32[]{:S(2)}, u32[]{:S(2)}) collective-permute-start(bf16[480,384]{1,0:T(8,128)(2,1)S(1)} %get-tuple-element.299), channel_id=1, source_target_pairs={{0,2},{1,3},{2,0},{3,1},{4,6},{5,7},{6,4},{7,5},{8,10},{9,11},{10,... | collective-permute-start | bytes 1105928 | tf_op jit(solution)/shard_map/ppermute | solution.py:640
  140.5 9.9 %collective-permute-start.16 = (bf16[480,384]{1,0:T(8,128)(2,1)S(1)}, bf16[480,384]{1,0:T(8,128)(2,1)S(1)}, u32[]{:S(2)}, u32[]{:S(2)}) collective-permute-start(bf16[480,384]{1,0:T(8,128)(2,1)S(1)} %get-tuple-element.300), channel_id=1, source_target_pairs={{0,1},{1,0},{2,3},{3,2},{4,5},{5,4},{6,7},{7,6},{8,9},{9,8},{10,11... | collective-permute-start | bytes 1105928 | tf_op jit(solution)/shard_map/ppermute | solution.py:640
  142.3 8.0 %collective-permute-start.17 = (bf16[192,768]{1,0:T(8,128)(2,1)S(1)}, bf16[192,768]{1,0:T(8,128)(2,1)S(1)}, u32[]{:S(2)}, u32[]{:S(2)}) collective-permute-start(bf16[192,768]{1,0:T(8,128)(2,1)S(1)} %get-tuple-element.307), channel_id=1, source_target_pairs={{0,8},{4,12},{8,0},{12,4},{16,24},{20,28},{24,16},{28,20},{1,9},{5... | collective-permute-start | bytes 884744 | tf_op jit(solution)/shard_map/ppermute | solution.py:650
  151.7 14.6 %copy-start.29 = (bf16[4,64,768]{2,1,0:T(8,128)(2,1)S(1)}, bf16[4,64,768]{2,1,0:T(8,128)(2,1)}, u32[]{:S(2)}) copy-start(bf16[4,64,768]{2,1,0:T(8,128)(2,1)} %get-tuple-element.349) | copy-start | bytes 1179652
  151.7 15.4 %copy-start.28 = (bf16[4,64,768]{2,1,0:T(8,128)(2,1)S(1)}, bf16[4,64,768]{2,1,0:T(8,128)(2,1)}, u32[]{:S(2)}) copy-start(bf16[4,64,768]{2,1,0:T(8,128)(2,1)} %get-tuple-element.350) | copy-start | bytes 1179652
  151.7 16.3 %copy-start.27 = (bf16[4,64,768]{2,1,0:T(8,128)(2,1)S(1)}, bf16[4,64,768]{2,1,0:T(8,128)(2,1)}, u32[]{:S(2)}) copy-start(bf16[4,64,768]{2,1,0:T(8,128)(2,1)} %get-tuple-element.351) | copy-start | bytes 1179652
  151.7 11.4 %collective-permute-start.18 = (bf16[2,160,768]{2,1,0:T(8,128)(2,1)S(1)}, bf16[2,160,768]{2,1,0:T(8,128)(2,1)S(1)}, u32[]{:S(2)}, u32[]{:S(2)}) collective-permute-start(bf16[2,160,768]{2,1,0:T(8,128)(2,1)S(1)} %get-tuple-element.315), channel_id=1, source_target_pairs={{0,1},{1,0},{2,3},{3,2},{4,5},{5,4},{6,7},{7,6},{8,9},{9,8},{10,11... | collective-permute-start | bytes 1474568 | tf_op jit(solution)/shard_map/ppermute | solution.py:640
  152.9 11.3 %collective-permute-start.19 = (bf16[2,160,768]{2,1,0:T(8,128)(2,1)S(1)}, bf16[2,160,768]{2,1,0:T(8,128)(2,1)S(1)}, u32[]{:S(2)}, u32[]{:S(2)}) collective-permute-start(bf16[2,160,768]{2,1,0:T(8,128)(2,1)S(1)} %get-tuple-element.316), channel_id=1, source_target_pairs={{0,2},{1,3},{2,0},{3,1},{4,6},{5,7},{6,4},{7,5},{8,10},{9,11},{10,... | collective-permute-start | bytes 1474568 | tf_op jit(solution)/shard_map/ppermute | solution.py:640
  154.3 8.5 %collective-permute-start.20 = (bf16[480,384]{1,0:T(8,128)(2,1)S(1)}, bf16[480,384]{1,0:T(8,128)(2,1)S(1)}, u32[]{:S(2)}, u32[]{:S(2)}) collective-permute-start(bf16[480,384]{1,0:T(8,128)(2,1)S(1)} %get-tuple-element.325), channel_id=1, source_target_pairs={{0,8},{4,12},{8,0},{12,4},{16,24},{20,28},{24,16},{28,20},{1,9},{5... | collective-permute-start | bytes 1105928 | tf_op jit(solution)/shard_map/ppermute | solution.py:650
  155.7 12.3 %collective-permute-start.23 = (bf16[192,768]{1,0:T(8,128)(2,1)S(1)}, bf16[192,768]{1,0:T(8,128)(2,1)S(1)}, u32[]{:S(2)}, u32[]{:S(2)}) collective-permute-start(bf16[192,768]{1,0:T(8,128)(2,1)S(1)} %add_convert_fusion.3), channel_id=1, source_target_pairs={{0,24},{4,28},{8,16},{12,20},{16,8},{20,12},{24,0},{28,4},{1,25},{... | collective-permute-start | bytes 884744 | tf_op jit(solution)/shard_map/ppermute | solution.py:650
  164.2 29.4 %copy-start.13 = (bf16[4,64,768]{2,1,0:T(8,128)(2,1)S(1)}, bf16[4,64,768]{2,1,0:T(8,128)(2,1)}, u32[]{:S(2)}) copy-start(bf16[4,64,768]{2,1,0:T(8,128)(2,1)} %get-tuple-element.366) | copy-start | bytes 1179652
  164.2 29.9 %copy-start.14 = (bf16[4,64,768]{2,1,0:T(8,128)(2,1)S(1)}, bf16[4,64,768]{2,1,0:T(8,128)(2,1)}, u32[]{:S(2)}) copy-start(bf16[4,64,768]{2,1,0:T(8,128)(2,1)} %get-tuple-element.367) | copy-start | bytes 1179652
  164.2 30.8 %copy-start.15 = (bf16[4,64,768]{2,1,0:T(8,128)(2,1)S(1)}, bf16[4,64,768]{2,1,0:T(8,128)(2,1)}, u32[]{:S(2)}) copy-start(bf16[4,64,768]{2,1,0:T(8,128)(2,1)} %get-tuple-element.368) | copy-start | bytes 1179652
  165.0 5.1 %collective-permute-start.21 = (bf16[160,768]{1,0:T(8,128)(2,1)S(1)}, bf16[160,768]{1,0:T(8,128)(2,1)S(1)}, u32[]{:S(2)}, u32[]{:S(2)}) collective-permute-start(bf16[160,768]{1,0:T(8,128)(2,1)S(1)} %get-tuple-element.335), channel_id=1, source_target_pairs={{0,2},{1,3},{2,0},{3,1},{4,6},{5,7},{6,4},{7,5},{8,10},{9,11},{10,... | collective-permute-start | bytes 737288 | tf_op jit(solution)/shard_map/ppermute | solution.py:640
  165.6 40.2 %copy-start.6 = (bf16[4,64,768]{2,1,0:T(8,128)(2,1)S(1)}, bf16[4,64,768]{2,1,0:T(8,128)(2,1)}, u32[]{:S(2)}) copy-start(bf16[4,64,768]{2,1,0:T(8,128)(2,1)} %get-tuple-element.369.refs_0_) | copy-start | bytes 1179652
  165.6 5.0 %collective-permute-start.22 = (bf16[160,768]{1,0:T(8,128)(2,1)S(1)}, bf16[160,768]{1,0:T(8,128)(2,1)S(1)}, u32[]{:S(2)}, u32[]{:S(2)}) collective-permute-start(bf16[160,768]{1,0:T(8,128)(2,1)S(1)} %get-tuple-element.336), channel_id=1, source_target_pairs={{0,1},{1,0},{2,3},{3,2},{4,5},{5,4},{6,7},{7,6},{8,9},{9,8},{10,11... | collective-permute-start | bytes 737288 | tf_op jit(solution)/shard_map/ppermute | solution.py:640
  166.2 19.1 %collective-permute-start.26 = (bf16[4,64,768]{2,1,0:T(8,128)(2,1)S(1)}, bf16[4,64,768]{2,1,0:T(8,128)(2,1)S(1)}, u32[]{:S(2)}, u32[]{:S(2)}) collective-permute-start(bf16[4,64,768]{2,1,0:T(8,128)(2,1)S(1)} %copy-done.29), channel_id=1, source_target_pairs={{0,1},{1,0},{2,3},{3,2},{4,5},{5,4},{6,7},{7,6},{8,9},{9,8},{10,11... | collective-permute-start | bytes 1179656 | tf_op jit(solution)/shard_map/ppermute | solution.py:640
  167.1 26.5 %collective-permute-start.27 = (bf16[4,64,768]{2,1,0:T(8,128)(2,1)S(1)}, bf16[4,64,768]{2,1,0:T(8,128)(2,1)S(1)}, u32[]{:S(2)}, u32[]{:S(2)}) collective-permute-start(bf16[4,64,768]{2,1,0:T(8,128)(2,1)S(1)} %copy-done.28), channel_id=1, source_target_pairs={{0,2},{1,3},{2,0},{3,1},{4,6},{5,7},{6,4},{7,5},{8,10},{9,11},{10,... | collective-permute-start | bytes 1179656 | tf_op jit(solution)/shard_map/ppermute | solution.py:640
  168.0 26.1 %collective-permute-start.28 = (bf16[4,64,768]{2,1,0:T(8,128)(2,1)S(1)}, bf16[4,64,768]{2,1,0:T(8,128)(2,1)S(1)}, u32[]{:S(2)}, u32[]{:S(2)}) collective-permute-start(bf16[4,64,768]{2,1,0:T(8,128)(2,1)S(1)} %copy-done.27), channel_id=1, source_target_pairs={{0,3},{1,2},{2,1},{3,0},{4,7},{5,6},{6,5},{7,4},{8,11},{9,10},{10,... | collective-permute-start | bytes 1179656 | tf_op jit(solution)/shard_map/ppermute | solution.py:640
  170.1 10.7 %collective-permute-start.25 = (bf16[480,384]{1,0:T(8,128)(2,1)S(1)}, bf16[480,384]{1,0:T(8,128)(2,1)S(1)}, u32[]{:S(2)}, u32[]{:S(2)}) collective-permute-start(bf16[480,384]{1,0:T(8,128)(2,1)S(1)} %add_convert_fusion.1), channel_id=1, source_target_pairs={{0,24},{4,28},{8,16},{12,20},{16,8},{20,12},{24,0},{28,4},{1,25},{... | collective-permute-start | bytes 1105928 | tf_op jit(solution)/shard_map/ppermute | solution.py:650
  171.4 23.6 %collective-permute-start.24 = (bf16[160,768]{1,0:T(8,128)(2,1)S(1)}, bf16[160,768]{1,0:T(8,128)(2,1)S(1)}, u32[]{:S(2)}, u32[]{:S(2)}) collective-permute-start(bf16[160,768]{1,0:T(8,128)(2,1)S(1)} %get-tuple-element.348), channel_id=1, source_target_pairs={{0,8},{4,12},{8,0},{12,4},{16,24},{20,28},{24,16},{28,20},{1,9},{5... | collective-permute-start | bytes 737288 | tf_op jit(solution)/shard_map/ppermute | solution.py:650
  180.8 15.7 %collective-permute-start.33 = (bf16[192,768]{1,0:T(8,128)(2,1)S(1)}, bf16[192,768]{1,0:T(8,128)(2,1)S(1)}, u32[]{:S(2)}, u32[]{:S(2)}) collective-permute-start(bf16[192,768]{1,0:T(8,128)(2,1)S(1)} %add_convert_fusion.2.refs_0_), channel_id=1, source_target_pairs={{0,4},{4,0},{8,12},{12,8},{16,20},{20,16},{24,28},{28,24},{1,5},{5... | collective-permute-start | bytes 884744 | tf_op jit(solution)/shard_map/ppermute | solution.py:643
  185.3 15.6 %collective-permute-start.32 = (bf16[192,768]{1,0:T(8,128)(2,1)S(1)}, bf16[192,768]{1,0:T(8,128)(2,1)S(1)}, u32[]{:S(2)}, u32[]{:S(2)}) collective-permute-start(bf16[192,768]{1,0:T(8,128)(2,1)S(1)} %add_convert_fusion.2.refs_0_), channel_id=1, source_target_pairs={{0,8},{4,12},{8,0},{12,4},{16,24},{20,28},{24,16},{28,20},{1,9},{5... | collective-permute-start | bytes 884744 | tf_op jit(solution)/shard_map/ppermute | solution.py:650
  193.6 10.4 %collective-permute-start.35 = (bf16[4,64,768]{2,1,0:T(8,128)(2,1)S(1)}, bf16[4,64,768]{2,1,0:T(8,128)(2,1)S(1)}, u32[]{:S(2)}, u32[]{:S(2)}) collective-permute-start(bf16[4,64,768]{2,1,0:T(8,128)(2,1)S(1)} %copy-done.13), channel_id=1, source_target_pairs={{0,1},{1,0},{2,3},{3,2},{4,5},{5,4},{6,7},{7,6},{8,9},{9,8},{10,11... | collective-permute-start | bytes 1179656 | tf_op jit(solution)/shard_map/ppermute | solution.py:640
  194.0 11.8 %collective-permute-start.36 = (bf16[4,64,768]{2,1,0:T(8,128)(2,1)S(1)}, bf16[4,64,768]{2,1,0:T(8,128)(2,1)S(1)}, u32[]{:S(2)}, u32[]{:S(2)}) collective-permute-start(bf16[4,64,768]{2,1,0:T(8,128)(2,1)S(1)} %copy-done.14), channel_id=1, source_target_pairs={{0,2},{1,3},{2,0},{3,1},{4,6},{5,7},{6,4},{7,5},{8,10},{9,11},{10,... | collective-permute-start | bytes 1179656 | tf_op jit(solution)/shard_map/ppermute | solution.py:640
  194.9 18.0 %collective-permute-start.37 = (bf16[4,64,768]{2,1,0:T(8,128)(2,1)S(1)}, bf16[4,64,768]{2,1,0:T(8,128)(2,1)S(1)}, u32[]{:S(2)}, u32[]{:S(2)}) collective-permute-start(bf16[4,64,768]{2,1,0:T(8,128)(2,1)S(1)} %copy-done.15), channel_id=1, source_target_pairs={{0,3},{1,2},{2,1},{3,0},{4,7},{5,6},{6,5},{7,4},{8,11},{9,10},{10,... | collective-permute-start | bytes 1179656 | tf_op jit(solution)/shard_map/ppermute | solution.py:640
  196.3 23.4 %copy-start.3 = (bf16[4,64,768]{2,1,0:T(8,128)(2,1)S(1)}, bf16[4,64,768]{2,1,0:T(8,128)(2,1)}, u32[]{:S(2)}) copy-start(bf16[4,64,768]{2,1,0:T(8,128)(2,1)} %get-tuple-element.377.refs_0_) | copy-start | bytes 1179652
  196.4 22.0 %collective-permute-start.31 = (bf16[480,384]{1,0:T(8,128)(2,1)S(1)}, bf16[480,384]{1,0:T(8,128)(2,1)S(1)}, u32[]{:S(2)}, u32[]{:S(2)}) collective-permute-start(bf16[480,384]{1,0:T(8,128)(2,1)S(1)} %add_convert_fusion.refs_0_), channel_id=1, source_target_pairs={{0,4},{4,0},{8,12},{12,8},{16,20},{20,16},{24,28},{28,24},{1,5},{5... | collective-permute-start | bytes 1105928 | tf_op jit(solution)/shard_map/ppermute | solution.py:643
  201.0 17.5 %collective-permute-start.30 = (bf16[480,384]{1,0:T(8,128)(2,1)S(1)}, bf16[480,384]{1,0:T(8,128)(2,1)S(1)}, u32[]{:S(2)}, u32[]{:S(2)}) collective-permute-start(bf16[480,384]{1,0:T(8,128)(2,1)S(1)} %add_convert_fusion.refs_0_), channel_id=1, source_target_pairs={{0,8},{4,12},{8,0},{12,4},{16,24},{20,28},{24,16},{28,20},{1,9},{5... | collective-permute-start | bytes 1105928 | tf_op jit(solution)/shard_map/ppermute | solution.py:650
  204.0 14.4 %collective-permute-start.34 = (bf16[192,768]{1,0:T(8,128)(2,1)S(1)}, bf16[192,768]{1,0:T(8,128)(2,1)S(1)}, u32[]{:S(2)}, u32[]{:S(2)}) collective-permute-start(bf16[192,768]{1,0:T(8,128)(2,1)S(1)} %collective-permute-done.32.refs_1_), channel_id=1, source_target_pairs={{0,4},{4,0},{8,12},{12,8},{16,20},{20,16},{24,28},{28,24},{1,5},{5... | collective-permute-start | bytes 884744 | tf_op jit(solution)/shard_map/ppermute | solution.py:643
  205.8 12.6 %collective-permute-start.29 = (bf16[160,768]{1,0:T(8,128)(2,1)S(1)}, bf16[160,768]{1,0:T(8,128)(2,1)S(1)}, u32[]{:S(2)}, u32[]{:S(2)}) collective-permute-start(bf16[160,768]{1,0:T(8,128)(2,1)S(1)} %add_convert_fusion.5), channel_id=1, source_target_pairs={{0,24},{4,28},{8,16},{12,20},{16,8},{20,12},{24,0},{28,4},{1,25},{... | collective-permute-start | bytes 737288 | tf_op jit(solution)/shard_map/ppermute | solution.py:650
  218.5 8.3 %collective-permute-start.40 = (bf16[480,384]{1,0:T(8,128)(2,1)S(1)}, bf16[480,384]{1,0:T(8,128)(2,1)S(1)}, u32[]{:S(2)}, u32[]{:S(2)}) collective-permute-start(bf16[480,384]{1,0:T(8,128)(2,1)S(1)} %collective-permute-done.30.refs_1_), channel_id=1, source_target_pairs={{0,4},{4,0},{8,12},{12,8},{16,20},{20,16},{24,28},{28,24},{1,5},{5... | collective-permute-start | bytes 1105928 | tf_op jit(solution)/shard_map/ppermute | solution.py:643
  219.6 5.0 %collective-permute-start.39 = (bf16[160,768]{1,0:T(8,128)(2,1)S(1)}, bf16[160,768]{1,0:T(8,128)(2,1)S(1)}, u32[]{:S(2)}, u32[]{:S(2)}) collective-permute-start(bf16[160,768]{1,0:T(8,128)(2,1)S(1)} %add_convert_fusion.4.refs_0_), channel_id=1, source_target_pairs={{0,4},{4,0},{8,12},{12,8},{16,20},{20,16},{24,28},{28,24},{1,5},{5... | collective-permute-start | bytes 737288 | tf_op jit(solution)/shard_map/ppermute | solution.py:643
  219.7 7.1 %collective-permute-start.38 = (bf16[160,768]{1,0:T(8,128)(2,1)S(1)}, bf16[160,768]{1,0:T(8,128)(2,1)S(1)}, u32[]{:S(2)}, u32[]{:S(2)}) collective-permute-start(bf16[160,768]{1,0:T(8,128)(2,1)S(1)} %add_convert_fusion.4.refs_0_), channel_id=1, source_target_pairs={{0,8},{4,12},{8,0},{12,4},{16,24},{20,28},{24,16},{28,20},{1,9},{5... | collective-permute-start | bytes 737288 | tf_op jit(solution)/shard_map/ppermute | solution.py:650
  226.8 3.7 %collective-permute-start.41 = (bf16[160,768]{1,0:T(8,128)(2,1)S(1)}, bf16[160,768]{1,0:T(8,128)(2,1)S(1)}, u32[]{:S(2)}, u32[]{:S(2)}) collective-permute-start(bf16[160,768]{1,0:T(8,128)(2,1)S(1)} %collective-permute-done.38.refs_1_), channel_id=1, source_target_pairs={{0,4},{4,0},{8,12},{12,8},{16,20},{20,16},{24,28},{28,24},{1,5},{5... | collective-permute-start | bytes 737288 | tf_op jit(solution)/shard_map/ppermute | solution.py:643
  (8 other events, 27.9 us)
where the time goes:
time: 236 us; the launch traced here: 232 us
  Pallas kernels  120 us (51%)
  waiting for transfers between devices  58.3 us (25%)
  starting transfers between devices  48.8 us (21%)
  local copies, waits for them, and re-layouts  3.63 us (2%)
    pallas_call x1, Pallas kernels, mlp_call(): pl.pallas_call(functools.partial(mlp_kernel, ncol), grid_spec=pltpu.Prefe...  44.2 us
    ppermute x9, waiting for transfers between devices, z_swap(): lax.ppermute(array, 'clip', [(i, i ^ 2 * distance) for i in range(self.nc...  31.5 us
    pallas_call x2, Pallas kernels, attend_back_call(): pl.pallas_call(functools.partial(attend_back_kernel, ncol, block, first),...  27.2 us
    ppermute x24, waiting for transfers between devices, col_swap(): lax.ppermute(array, 'col', [(i, i ^ distance) for i in range(self.ncol)])  22.5 us
    ppermute x24, starting transfers between devices, col_swap(): lax.ppermute(array, 'col', [(i, i ^ distance) for i in range(self.ncol)])  19.9 us
    pallas_call x1, Pallas kernels, attend_call(): pl.pallas_call(functools.partial(attend_kernel, ncol, block, first), grid...  15.8 us
    ppermute x9, starting transfers between devices, z_swap(): lax.ppermute(array, 'clip', [(i, i ^ 2 * distance) for i in range(self.nc...  15 us
    ppermute x9, starting transfers between devices, core_swap(): return lax.ppermute(array, 'clip', [(i, i ^ 1) for i in range(self.nclip)])  13.9 us
  transfers between devices with their start and end apart: 42, of which 16 were waited for; matrix products, arithmetic and copies ran while one was open for 1% of the time, Pallas kernels for 29%

commit v1 on v0

--- a/solution.py
+++ b/solution.py
@@ -1080,22 +1080,20 @@
         qkv.inner()
         up.land = wait_for(up.land, qkv.own)
         up.outer()
-        down.land = wait_for(down.land, up.own)
-        down.swap()
-        output = place_frames(info, [outs[0], *wait_for(out_land, up.own)], BF16)
-        qkv.land, up.land, down.land, gin_land, qkv.own, up.own, output = join(
-            qkv.land, up.land, down.land, gin_land, qkv.own, up.own, output
-        )
+        qkv.land, down.land, gin_land, qkv.own, up.own = join(qkv.land, down.land, gin_land, qkv.own, up.own)
 
         qkv.outer()
         up.land = wait_for(up.land, qkv.own)
         up.swap()
+        down.land = wait_for(down.land, up.parts[1])
+        down.swap()
+        output = place_frames(info, [outs[0], *wait_for(out_land, up.parts[1])], BF16)
         grad_input = place_frames(info, [gouts[0], *wait_for(gin_land, up.parts[1])], F32)
-        down.parts, down.land = wait_for((down.parts, down.land), grad_input)
+        qkv.land, up.land, down.land, up.parts, down.parts, qkv.own, output, grad_input = join(qkv.land, up.land, down.land, up.parts, down.parts, qkv.own, output, grad_input)
+
+        qkv.swap()
+        down.parts, down.land = wait_for((down.parts, down.land), qkv.parts[0])
         (grad_w_down,) = down.last(finish_down_kernel, "finish_down", [(model // 4, hidden_size)])
-        qkv.land, up.land, up.parts, qkv.own, grad_w_down = join(qkv.land, up.land, up.parts, qkv.own, grad_w_down)
-
-        qkv.swap()
         up.parts, up.land = wait_for((up.parts, up.land), qkv.parts[0])
         grad_w_up, grad_w_out = up.last(
             finish_up_kernel, "finish_up", [(model, hidden_size // 4), (model // 4, model)]

time: 236 us -> 231 us (0.979)
  starting transfers between devices: 48.8 us -> 40.5 us
  waiting for transfers between devices: 58.3 us -> 63.2 us
    ppermute x9, starting transfers between devices: 15 us -> 9.39 us  [z_swap(): lax.ppermute(array, 'clip', [(i, i ^ 2 * distance) for i in range(self.nc...]
    ppermute x9, waiting for transfers between devices: 31.5 us -> 34.7 us  [z_swap(): lax.ppermute(array, 'clip', [(i, i ^ 2 * distance) for i in range(self.nc...]
    ppermute x9, starting transfers between devices: 13.9 us -> 10.9 us  [core_swap(): return lax.ppermute(array, 'clip', [(i, i ^ 1) for i in range(self.nclip)])]
  transfers between devices with their start and end apart: 42 -> 42, of which waited for: 16 -> 15; matrix products, arithmetic and copies ran while one was open for 1% -> 1% of each run, Pallas kernels for 29% -> 30%
where the time goes in v1:
time: 231 us; the launch traced here: 229 us
  Pallas kernels  120 us (52%)
  waiting for transfers between devices  63.2 us (27%)
  starting transfers between devices  40.5 us (18%)
  local copies, waits for them, and re-layouts  3.63 us (2%)
    pallas_call x1, Pallas kernels, mlp_call(): pl.pallas_call(functools.partial(mlp_kernel, ncol), grid_spec=pltpu.Prefe...  44.2 us
    ppermute x9, waiting for transfers between devices, z_swap(): lax.ppermute(array, 'clip', [(i, i ^ 2 * distance) for i in range(self.nc...  34.7 us
    pallas_call x2, Pallas kernels, attend_back_call(): pl.pallas_call(functools.partial(attend_back_kernel, ncol, block, first),...  27.2 us
    ppermute x24, waiting for transfers between devices, col_swap(): lax.ppermute(array, 'col', [(i, i ^ distance) for i in range(self.ncol)])  24.2 us
    ppermute x24, starting transfers between devices, col_swap(): lax.ppermute(array, 'col', [(i, i ^ distance) for i in range(self.ncol)])  20.2 us
    pallas_call x1, Pallas kernels, attend_call(): pl.pallas_call(functools.partial(attend_kernel, ncol, block, first), grid...  15.8 us
    ppermute x9, starting transfers between devices, core_swap(): return lax.ppermute(array, 'clip', [(i, i ^ 1) for i in range(self.nclip)])  10.9 us
    ppermute x9, starting transfers between devices, z_swap(): lax.ppermute(array, 'clip', [(i, i ^ 2 * distance) for i in range(self.nc...  9.39 us
  transfers between devices with their start and end apart: 42, of which 15 were waited for; matrix products, arithmetic and copies ran while one was open for 1% of the time, Pallas kernels for 30%

profile of v1, /device:TPU:17, one launch (start us, length us, event | category | flops | bytes accessed | tf_op | source)
XLA Modules:
  0.0 229.1 jit_solution(7272832621185909010)
XLA Ops:
  0.8 2.8 %take_frames.2 = (bf16[4,64,768]{2,1,0:T(8,128)(2,1)}, bf16[4,64,768]{2,1,0:T(8,128)(2,1)}, bf16[4,64,768]{2,1,0:T(8,128)(2,1)}) custom-call(s32[5]{0:T(128)S(1)} %stack.27.info, bf16[16,64,768]{2,1,0:T(8,128)(2,1)} %refs_0_.11, bf16[16,64,768]{2,1,0:T(8,128)(2,1)} %refs_0_.11, bf16[16,64,768]{2,1,0:T(8,128)(2,1)} %refs_0_.11), custom_call_target="tpu_custom_call" | custom-call | bytes 1500000 | tf_op jit(solution)/shard_map/take_frames/pallas_call | solution.py:584
  3.7 1.2 collective-permute-start
  4.9 1.2 collective-permute-start.1
  7.3 2.8 %take_frames.3 = (bf16[4,64,768]{2,1,0:T(8,128)(2,1)}, bf16[4,64,768]{2,1,0:T(8,128)(2,1)}, bf16[4,64,768]{2,1,0:T(8,128)(2,1)}) custom-call(s32[5]{0:T(128)S(1)} %stack.27.info, bf16[16,64,768]{2,1,0:T(8,128)(2,1)} %refs_0_.9, bf16[16,64,768]{2,1,0:T(8,128)(2,1)} %refs_0_.9, bf16[16,64,768]{2,1,0:T(8,128)(2,1)} %refs_0_.9), custom_call_target="tpu_custom_call" | custom-call | bytes 1500000 | tf_op jit(solution)/shard_map/take_frames/pallas_call | solution.py:584
  10.1 3.8 %collective-permute-done.refs_1_ = bf16[4,64,768]{2,1,0:T(8,128)(2,1)S(1)} collective-permute-done((bf16[4,64,768]{2,1,0:T(8,128)(2,1)}, bf16[4,64,768]{2,1,0:T(8,128)(2,1)S(1)}, u32[]{:S(2)}, u32[]{:S(2)}) %collective-permute-start) | collective-permute-done | bytes 393248 | tf_op jit(solution)/shard_map/ppermute | solution.py:640
  13.9 1.2 collective-permute-start.3
  15.1 1.2 collective-permute-start.4
  16.7 6.6 %collective-permute-done.2.refs_3_ = bf16[4,64,768]{2,1,0:T(8,128)(2,1)S(1)} collective-permute-done((bf16[4,64,768]{2,1,0:T(8,128)(2,1)}, bf16[4,64,768]{2,1,0:T(8,128)(2,1)S(1)}, u32[]{:S(2)}, u32[]{:S(2)}) %collective-permute-start.2) | collective-permute-done | bytes 393248 | tf_op jit(solution)/shard_map/ppermute | solution.py:640
  23.3 15.8 %attend.1 = (bf16[2304,1024]{1,0:T(8,128)(2,1)}, bf16[768,1024]{1,0:T(8,128)(2,1)}, f32[1024,768]{1,0:T(8,128)}, f32[4,16,256]{2,1,0:T(8,128)}) custom-call(s32[5]{0:T(128)S(1)} %stack.27.info, s32[4]{0:T(128)S(1)} %dynamic-slice_bitcast_fusion.lens, bf16[16,64,768]{2,1,0:T(8,128)(2,1)S(1)} %copy-done, bf16[4,64,768]{2,1,0:T(8,128)(2,1)S(1)} %collective-permute-done.refs_1_, ...), custom_call_target="tpu_custom_call" | custom-call | bytes 15000000 | tf_op jit(solution)/shard_map/attend/pallas_call | solution.py:189
  39.1 2.5 %collective-permute-done.4.refs_2_ = bf16[4,64,768]{2,1,0:T(8,128)(2,1)} collective-permute-done((bf16[4,64,768]{2,1,0:T(8,128)(2,1)}, bf16[4,64,768]{2,1,0:T(8,128)(2,1)}, u32[]{:S(2)}, u32[]{:S(2)}) %collective-permute-start.4) | collective-permute-done | bytes 393248 | tf_op jit(solution)/shard_map/ppermute | solution.py:640
  41.5 44.2 %mlp.1 = (bf16[4,64,768]{2,1,0:T(8,128)(2,1)}, bf16[4,64,768]{2,1,0:T(8,128)(2,1)}, bf16[4,64,768]{2,1,0:T(8,128)(2,1)}, bf16[4,64,768]{2,1,0:T(8,128)(2,1)}, f3...) custom-call(s32[5]{0:T(128)} %copy-done.8, ...), custom_call_target="tpu_custom_call" | custom-call | bytes 60000000 | tf_op jit(solution)/shard_map/mlp/pallas_call | solution.py:375
  85.8 1.1 collective-permute-start.6
  86.9 4.3 %collective-permute-done.6.refs_4_.refs_5_.refs_6_.refs_7_ = bf16[4,384,768]{2,1,0:T(8,128)(2,1)S(1)} collective-permute-done((bf16[4,384,768]{2,1,0:T(8,128)(2,1)}, bf16[4,384,768]{2,1,0:T(8,128)(2,1)S(1)}, u32[]{:S(2)}, u32[]{:S(2)}) %collective-permute-start.6) | collective-permute-done | bytes 2359328 | tf_op jit(solution)/shard_map/ppermute | solution.py:643
  91.2 1.7 copy-done.2
  92.9 1.1 sum_core.3
  94.0 1.3 collective-permute-start.7
  95.6 13.9 %attend_back.2 = (bf16[2304,1024]{1,0:T(8,128)(2,1)}, bf16[1024,768]{1,0:T(8,128)(2,1)}, f32[16,768]{1,0:T(8,128)}, bf16[4,64,768]{2,1,0:T(8,128)(2,1)}, bf16[4,...) custom-call(s32[5]{0:T(128)S(1)} %copy-done.9, ...), custom_call_target="tpu_custom_call" | custom-call | bytes 22500000 | tf_op jit(solution)/shard_map/attend_back/pallas_call | solution.py:524
  109.6 0.8 sum_first.3
  110.4 1.3 sum_core.4
  111.7 1.5 collective-permute-start.12
  113.4 1.2 collective-permute-start.10
  114.7 13.3 %attend_back.3 = (bf16[2304,1024]{1,0:T(8,128)(2,1)}, bf16[1024,768]{1,0:T(8,128)(2,1)}, f32[16,768]{1,0:T(8,128)}, bf16[4,64,768]{2,1,0:T(8,128)(2,1)}, bf16[4,...) custom-call(s32[5]{0:T(128)S(1)} %copy-done.9, ...), custom_call_target="tpu_custom_call", output_to_operand_aliasing={{0}: (14, {}), {1}: (15, {}), {3}: (16, {}), {4}: (17, {}),... | custom-call | bytes 22500000 | tf_op jit(solution)/shard_map/attend_back/pallas_call | solution.py:524
  128.0 0.8 copy-done.12
  128.8 7.3 %grad_qkv.1 = (bf16[4,320,768]{2,1,0:T(8,128)(2,1)S(1)}, bf16[4,320,768]{2,1,0:T(8,128)(2,1)S(1)}) custom-call(s32[5]{0:T(128)S(1)} %copy-done.9, bf16[2304,1024]{1,0:T(8,128)(2,1)} %get-tuple-element.288.gproj_t, bf16[1024,768]{1,0:T(8,128)(2,1)} %get-tuple-element.289.normed_n, f32[16,768]{1,0:T(8,128)S(1)} %copy-done.10, f32[16,768]{1,0:T(8,128)S(1)} %copy-done.11, ...), custom_call_target="tpu_custom_call" | custom-call | bytes 9000000 | tf_op jit(solution)/shard_map/grad_qkv/pallas_call | solution.py:744
  136.2 2.7 %collective-permute-start.14 = (bf16[4,320,768]{2,1,0:T(8,128)(2,1)S(1)}, bf16[4,320,768]{2,1,0:T(8,128)(2,1)S(1)}, u32[]{:S(2)}, u32[]{:S(2)}) collective-permute-start(bf16[4,320,768]{2,1,0:T(8,128)(2,1)S(1)} %get-tuple-element.296), channel_id=1, source_target_pairs={{0,4},{4,0},{8,12},{12,8},{16,20},{20,16},{24,28},{28,24},{1,5},{5... | collective-permute-start | bytes 5898248 | tf_op jit(solution)/shard_map/ppermute | solution.py:643
  138.9 0.9 sum_first.4
  139.8 0.7 collective-permute-start.15
  140.5 1.1 collective-permute-start.16
  141.6 0.7 sum_second.3
  142.3 1.4 collective-permute-start.17
  143.6 6.7 %collective-permute-done.17 = bf16[192,768]{1,0:T(8,128)(2,1)S(1)} collective-permute-done((bf16[192,768]{1,0:T(8,128)(2,1)S(1)}, bf16[192,768]{1,0:T(8,128)(2,1)S(1)}, u32[]{:S(2)}, u32[]{:S(2)}) %collective-permute-start.17) | collective-permute-done | bytes 294944 | tf_op jit(solution)/shard_map/ppermute | solution.py:650
  150.4 1.3 sum_core.5
  151.7 1.1 collective-permute-start.18
  153.5 0.8 sum_second.4
  154.3 1.4 collective-permute-start.20
  155.7 7.1 %collective-permute-done.20 = bf16[480,384]{1,0:T(8,128)(2,1)S(1)} collective-permute-done((bf16[480,384]{1,0:T(8,128)(2,1)S(1)}, bf16[480,384]{1,0:T(8,128)(2,1)S(1)}, u32[]{:S(2)}, u32[]{:S(2)}) %collective-permute-start.20) | collective-permute-done | bytes 368672 | tf_op jit(solution)/shard_map/ppermute | solution.py:650
  163.1 1.1 collective-permute-done.19.land_b
  164.1 0.8 sum_first.5
  164.9 0.7 collective-permute-start.21
  166.6 0.9 collective-permute-start.26
  167.4 0.9 collective-permute-start.27
  168.3 1.8 collective-permute-done.21.land_a
  170.0 0.9 collective-permute-start.28
  171.0 0.7 sum_second.5
  171.7 1.7 collective-permute-start.24
  173.4 12.6 %collective-permute-done.25 = bf16[480,384]{1,0:T(8,128)(2,1)S(1)} collective-permute-done((bf16[480,384]{1,0:T(8,128)(2,1)S(1)}, bf16[480,384]{1,0:T(8,128)(2,1)S(1)}, u32[]{:S(2)}, u32[]{:S(2)}) %collective-permute-start.25) | collective-permute-done | bytes 368672 | tf_op jit(solution)/shard_map/ppermute | solution.py:650
  186.0 1.4 collective-permute-start.31
  187.4 1.1 collective-permute-start.30
  188.6 1.6 collective-permute-start.32
  190.8 0.7 collective-permute-start.34
  191.8 4.4 %collective-permute-done.30.refs_1_ = bf16[192,768]{1,0:T(8,128)(2,1)S(1)} collective-permute-done((bf16[192,768]{1,0:T(8,128)(2,1)S(1)}, bf16[192,768]{1,0:T(8,128)(2,1)S(1)}, u32[]{:S(2)}, u32[]{:S(2)}) %collective-permute-start.30) | collective-permute-done | bytes 294944 | tf_op jit(solution)/shard_map/ppermute | solution.py:650
  196.2 1.3 collective-permute-start.38
  197.5 1.0 collective-permute-done.32.refs_1_
  198.5 3.0 %collective-permute-start.37 = (bf16[480,384]{1,0:T(8,128)(2,1)S(1)}, bf16[480,384]{1,0:T(8,128)(2,1)S(1)}, u32[]{:S(2)}, u32[]{:S(2)}) collective-permute-start(bf16[480,384]{1,0:T(8,128)(2,1)S(1)} %add_convert_fusion.refs_0_), channel_id=1, source_target_pairs={{0,8},{4,12},{8,0},{12,4},{16,24},{20,28},{24,16},{28,20},{1,9},{5... | collective-permute-start | bytes 1105928 | tf_op jit(solution)/shard_map/ppermute | solution.py:650
  201.4 7.2 %collective-permute-done.34.refs_3_ = bf16[4,64,768]{2,1,0:T(8,128)(2,1)S(1)} collective-permute-done((bf16[4,64,768]{2,1,0:T(8,128)(2,1)S(1)}, bf16[4,64,768]{2,1,0:T(8,128)(2,1)S(1)}, u32[]{:S(2)}, u32[]{:S(2)}) %collective-permute-start.34) | collective-permute-done | bytes 393248 | tf_op jit(solution)/shard_map/ppermute | solution.py:640
  208.7 1.9 collective-permute-done.37.refs_1_
  210.6 3.0 %collective-permute-start.39 = (bf16[480,384]{1,0:T(8,128)(2,1)S(1)}, bf16[480,384]{1,0:T(8,128)(2,1)S(1)}, u32[]{:S(2)}, u32[]{:S(2)}) collective-permute-start(bf16[480,384]{1,0:T(8,128)(2,1)S(1)} %collective-permute-done.37.refs_1_), channel_id=1, source_target_pairs={{0,4},{4,0},{8,12},{12,8},{16,20},{20,16},{24,28},{28,24},{1,5},{5... | collective-permute-start | bytes 1105928 | tf_op jit(solution)/shard_map/ppermute | solution.py:643
  214.7 2.3 place_frames.2
  217.0 2.7 %place_frames.3 = f32[16,64,768]{2,1,0:T(8,128)} custom-call(s32[5]{0:T(128)S(1)} %copy-done.9, bf16[4,64,768]{2,1,0:T(8,128)(2,1)S(1)} %copy-done.3, bf16[4,64,768]{2,1,0:T(8,128)(2,1)S(1)} %collective-permute-done.32.refs_1_, bf16[4,64,768]{2,1,0:T(8,128)(2,1)S(1)} %collective-permute-done.33.refs_2_, bf16[4,64,768]{2,1,0:T(8,128)(2,1)S(1)} %collective-permute-done.34.refs_3_), custom_call_target="tpu_custom_call" | custom-call | bytes 3000000 | tf_op jit(solution)/shard_map/place_frames/pallas_call | solution.py:610
  219.7 2.0 collective-permute-done.35.refs_1_
  221.7 0.8 collective-permute-start.41
  222.5 2.2 finish_down.1
  224.7 2.4 %finish_up.1 = (f32[768,768]{1,0:T(8,128)}, f32[192,768]{1,0:T(8,128)}) custom-call(s32[5]{0:T(128)S(1)} %copy-done.9, bf16[480,384]{1,0:T(8,128)(2,1)S(1)} %add_convert_fusion.refs_0_, bf16[480,384]{1,0:T(8,128)(2,1)S(1)} %collective-permute-done.37.refs_1_, bf16[480,384]{1,0:T(8,128)(2,1)S(1)} %collective-permute-done.38.refs_2_, ...), custom_call_target="tpu_custom_call" | custom-call | bytes 3000000 | tf_op jit(solution)/shard_map/finish_up/pallas_call | solution.py:887
  227.1 1.9 finish_qkv.1
  (118 shorter events, 6.4 us)
Async XLA Ops:
  0.7 22.5 %copy-start.8 = (s32[5]{0:T(128)}, s32[5]{0:T(128)S(1)}, u32[]{:S(2)}) copy-start(s32[5]{0:T(128)S(1)} %stack.27.info) | copy-start | bytes 64
  0.8 6.3 %copy-start.17 = (bf16[3072]{0:T(1024)(128)(2,1)S(1)}, bf16[3072]{0:T(1024)(128)(2,1)}, u32[]{:S(2)}) copy-start(bf16[3072]{0:T(1024)(128)(2,1)} %param.29) | copy-start | bytes 18436
  0.8 6.3 %copy-start.18 = (bf16[1536]{0:T(1024)(128)(2,1)S(1)}, bf16[1536]{0:T(1024)(128)(2,1)}, u32[]{:S(2)}) copy-start(bf16[1536]{0:T(1024)(128)(2,1)} %param.23) | copy-start | bytes 9220
  0.8 6.3 %copy-start.19 = (bf16[768]{0:T(1024)(128)(2,1)S(1)}, bf16[768]{0:T(1024)(128)(2,1)}, u32[]{:S(2)}) copy-start(bf16[768]{0:T(1024)(128)(2,1)} %param.31) | copy-start | bytes 4612
  0.8 6.3 %copy-start.20 = (bf16[768]{0:T(1024)(128)(2,1)S(1)}, bf16[768]{0:T(1024)(128)(2,1)}, u32[]{:S(2)}) copy-start(bf16[768]{0:T(1024)(128)(2,1)} %param.27) | copy-start | bytes 4612
  0.8 6.3 %copy-start.21 = (bf16[768]{0:T(1024)(128)(2,1)S(1)}, bf16[768]{0:T(1024)(128)(2,1)}, u32[]{:S(2)}) copy-start(bf16[768]{0:T(1024)(128)(2,1)} %param.26) | copy-start | bytes 4612
  0.8 6.3 %copy-start.22 = (bf16[768]{0:T(1024)(128)(2,1)S(1)}, bf16[768]{0:T(1024)(128)(2,1)}, u32[]{:S(2)}) copy-start(bf16[768]{0:T(1024)(128)(2,1)} %param.25) | copy-start | bytes 4612
  0.8 6.3 %copy-start.23 = (bf16[768]{0:T(1024)(128)(2,1)S(1)}, bf16[768]{0:T(1024)(128)(2,1)}, u32[]{:S(2)}) copy-start(bf16[768]{0:T(1024)(128)(2,1)} %param.21) | copy-start | bytes 4612
  3.7 10.2 %collective-permute-start = (bf16[4,64,768]{2,1,0:T(8,128)(2,1)}, bf16[4,64,768]{2,1,0:T(8,128)(2,1)S(1)}, u32[]{:S(2)}, u32[]{:S(2)}) collective-permute-start(bf16[4,64,768]{2,1,0:T(8,128)(2,1)} %get-tuple-element.223), channel_id=1, source_target_pairs={{0,1},{1,0},{2,3},{3,2},{4,5},{5,4},{6,7},{7,6},{8,9},{9,8},{10,11... | collective-permute-start | bytes 1179656 | tf_op jit(solution)/shard_map/ppermute | solution.py:640
  4.9 11.8 %collective-permute-start.1 = (bf16[4,64,768]{2,1,0:T(8,128)(2,1)}, bf16[4,64,768]{2,1,0:T(8,128)(2,1)S(1)}, u32[]{:S(2)}, u32[]{:S(2)}) collective-permute-start(bf16[4,64,768]{2,1,0:T(8,128)(2,1)} %get-tuple-element.229), channel_id=1, source_target_pairs={{0,2},{1,3},{2,0},{3,1},{4,6},{5,7},{6,4},{7,5},{8,10},{9,11},{10,... | collective-permute-start | bytes 1179656 | tf_op jit(solution)/shard_map/ppermute | solution.py:640
  6.1 17.2 %collective-permute-start.2 = (bf16[4,64,768]{2,1,0:T(8,128)(2,1)}, bf16[4,64,768]{2,1,0:T(8,128)(2,1)S(1)}, u32[]{:S(2)}, u32[]{:S(2)}) collective-permute-start(bf16[4,64,768]{2,1,0:T(8,128)(2,1)} %get-tuple-element.230), channel_id=1, source_target_pairs={{0,3},{1,2},{2,1},{3,0},{4,7},{5,6},{6,5},{7,4},{8,11},{9,10},{10,... | collective-permute-start | bytes 1179656 | tf_op jit(solution)/shard_map/ppermute | solution.py:640
  7.3 16.0 %copy-start.4 = (f32[12,768]{1,0:T(8,128)}, f32[12,768]{1,0:T(8,128)S(1)}, u32[]{:S(2)}) copy-start(f32[12,768]{1,0:T(8,128)S(1)} %reshape.58.refs_5_.refs_6_) | copy-start | bytes 110596
  7.3 16.0 %copy-start = (bf16[16,64,768]{2,1,0:T(8,128)(2,1)S(1)}, bf16[16,64,768]{2,1,0:T(8,128)(2,1)}, u32[]{:S(2)}) copy-start(bf16[16,64,768]{2,1,0:T(8,128)(2,1)} %refs_0_.11) | copy-start | bytes 4718596
  13.9 25.2 %collective-permute-start.3 = (bf16[4,64,768]{2,1,0:T(8,128)(2,1)}, bf16[4,64,768]{2,1,0:T(8,128)(2,1)S(1)}, u32[]{:S(2)}, u32[]{:S(2)}) collective-permute-start(bf16[4,64,768]{2,1,0:T(8,128)(2,1)} %get-tuple-element.240), channel_id=1, source_target_pairs={{0,1},{1,0},{2,3},{3,2},{4,5},{5,4},{6,7},{7,6},{8,9},{9,8},{10,11... | collective-permute-start | bytes 1179656 | tf_op jit(solution)/shard_map/ppermute | solution.py:640
  15.1 26.4 %collective-permute-start.4 = (bf16[4,64,768]{2,1,0:T(8,128)(2,1)}, bf16[4,64,768]{2,1,0:T(8,128)(2,1)}, u32[]{:S(2)}, u32[]{:S(2)}) collective-permute-start(bf16[4,64,768]{2,1,0:T(8,128)(2,1)} %get-tuple-element.241), channel_id=1, source_target_pairs={{0,2},{1,3},{2,0},{3,1},{4,6},{5,7},{6,4},{7,5},{8,10},{9,11},{10,... | collective-permute-start | bytes 1179656 | tf_op jit(solution)/shard_map/ppermute | solution.py:640
  16.3 25.2 %collective-permute-start.5 = (bf16[4,64,768]{2,1,0:T(8,128)(2,1)}, bf16[4,64,768]{2,1,0:T(8,128)(2,1)}, u32[]{:S(2)}, u32[]{:S(2)}) collective-permute-start(bf16[4,64,768]{2,1,0:T(8,128)(2,1)} %get-tuple-element.242), channel_id=1, source_target_pairs={{0,3},{1,2},{2,1},{3,0},{4,7},{5,6},{6,5},{7,4},{8,11},{9,10},{10,... | collective-permute-start | bytes 1179656 | tf_op jit(solution)/shard_map/ppermute | solution.py:640
  41.5 49.7 %copy-start.9 = (s32[5]{0:T(128)S(1)}, s32[5]{0:T(128)}, u32[]{:S(2)}) copy-start(s32[5]{0:T(128)} %copy-done.8) | copy-start | bytes 64
  85.8 5.5 %collective-permute-start.6 = (bf16[4,384,768]{2,1,0:T(8,128)(2,1)}, bf16[4,384,768]{2,1,0:T(8,128)(2,1)S(1)}, u32[]{:S(2)}, u32[]{:S(2)}) collective-permute-start(bf16[4,384,768]{2,1,0:T(8,128)(2,1)} %get-tuple-element.249), channel_id=1, source_target_pairs={{0,4},{4,0},{8,12},{12,8},{16,20},{20,16},{24,28},{28,24},{1,5},{5... | collective-permute-start | bytes 7077896 | tf_op jit(solution)/shard_map/ppermute | solution.py:643
  86.9 22.7 %collective-permute-start.9 = (bf16[4,960,384]{2,1,0:T(8,128)(2,1)}, bf16[4,960,384]{2,1,0:T(8,128)(2,1)S(1)}, u32[]{:S(2)}, u32[]{:S(2)}) collective-permute-start(bf16[4,960,384]{2,1,0:T(8,128)(2,1)} %get-tuple-element.253), channel_id=1, source_target_pairs={{0,4},{4,0},{8,12},{12,8},{16,20},{20,16},{24,28},{28,24},{1,5},{5... | collective-permute-start | bytes 8847368 | tf_op jit(solution)/shard_map/ppermute | solution.py:643
  94.0 15.5 %collective-permute-start.7 = (bf16[2,192,768]{2,1,0:T(8,128)(2,1)S(1)}, bf16[2,192,768]{2,1,0:T(8,128)(2,1)S(1)}, u32[]{:S(2)}, u32[]{:S(2)}) collective-permute-start(bf16[2,192,768]{2,1,0:T(8,128)(2,1)S(1)} %get-tuple-element.251), channel_id=1, source_target_pairs={{0,1},{1,0},{2,3},{3,2},{4,5},{5,4},{6,7},{7,6},{8,9},{9,8},{10,11... | collective-permute-start | bytes 1769480 | tf_op jit(solution)/shard_map/ppermute | solution.py:640
  95.3 14.2 %collective-permute-start.8 = (bf16[2,192,768]{2,1,0:T(8,128)(2,1)S(1)}, bf16[2,192,768]{2,1,0:T(8,128)(2,1)S(1)}, u32[]{:S(2)}, u32[]{:S(2)}) collective-permute-start(bf16[2,192,768]{2,1,0:T(8,128)(2,1)S(1)} %get-tuple-element.252), channel_id=1, source_target_pairs={{0,2},{1,3},{2,0},{3,1},{4,6},{5,7},{6,4},{7,5},{8,10},{9,11},{10,... | collective-permute-start | bytes 1769480 | tf_op jit(solution)/shard_map/ppermute | solution.py:640
  95.6 14.8 %copy-start.1 = (bf16[4,960,384]{2,1,0:T(8,128)(2,1)S(1)}, bf16[4,960,384]{2,1,0:T(8,128)(2,1)}, u32[]{:S(2)}) copy-start(bf16[4,960,384]{2,1,0:T(8,128)(2,1)} %get-tuple-element.270.refs_0_.refs_1_.refs_2_.refs_3_) | copy-start | bytes 8847364
  111.7 24.5 %collective-permute-start.12 = (bf16[2,480,384]{2,1,0:T(8,128)(2,1)S(1)}, bf16[2,480,384]{2,1,0:T(8,128)(2,1)S(1)}, u32[]{:S(2)}, u32[]{:S(2)}) collective-permute-start(bf16[2,480,384]{2,1,0:T(8,128)(2,1)S(1)} %get-tuple-element.274), channel_id=1, source_target_pairs={{0,1},{1,0},{2,3},{3,2},{4,5},{5,4},{6,7},{7,6},{8,9},{9,8},{10,11... | collective-permute-start | bytes 2211848 | tf_op jit(solution)/shard_map/ppermute | solution.py:640
  113.2 23.1 %collective-permute-start.13 = (bf16[2,480,384]{2,1,0:T(8,128)(2,1)S(1)}, bf16[2,480,384]{2,1,0:T(8,128)(2,1)S(1)}, u32[]{:S(2)}, u32[]{:S(2)}) collective-permute-start(bf16[2,480,384]{2,1,0:T(8,128)(2,1)S(1)} %get-tuple-element.275), channel_id=1, source_target_pairs={{0,2},{1,3},{2,0},{3,1},{4,6},{5,7},{6,4},{7,5},{8,10},{9,11},{10,... | collective-permute-start | bytes 2211848 | tf_op jit(solution)/shard_map/ppermute | solution.py:640
  113.4 22.8 %collective-permute-start.10 = (bf16[192,768]{1,0:T(8,128)(2,1)S(1)}, bf16[192,768]{1,0:T(8,128)(2,1)S(1)}, u32[]{:S(2)}, u32[]{:S(2)}) collective-permute-start(bf16[192,768]{1,0:T(8,128)(2,1)S(1)} %get-tuple-element.268), channel_id=1, source_target_pairs={{0,2},{1,3},{2,0},{3,1},{4,6},{5,7},{6,4},{7,5},{8,10},{9,11},{10,... | collective-permute-start | bytes 884744 | tf_op jit(solution)/shard_map/ppermute | solution.py:640
  114.6 21.6 %collective-permute-start.11 = (bf16[192,768]{1,0:T(8,128)(2,1)S(1)}, bf16[192,768]{1,0:T(8,128)(2,1)S(1)}, u32[]{:S(2)}, u32[]{:S(2)}) collective-permute-start(bf16[192,768]{1,0:T(8,128)(2,1)S(1)} %get-tuple-element.269), channel_id=1, source_target_pairs={{0,1},{1,0},{2,3},{3,2},{4,5},{5,4},{6,7},{7,6},{8,9},{9,8},{10,11... | collective-permute-start | bytes 884744 | tf_op jit(solution)/shard_map/ppermute | solution.py:640
  114.7 13.3 %copy-start.10 = (f32[16,768]{1,0:T(8,128)S(1)}, f32[16,768]{1,0:T(8,128)}, u32[]{:S(2)}) copy-start(f32[16,768]{1,0:T(8,128)} %get-tuple-element.290.mlp_sums) | copy-start | bytes 147460
  114.7 13.3 %copy-start.11 = (f32[16,768]{1,0:T(8,128)S(1)}, f32[16,768]{1,0:T(8,128)}, u32[]{:S(2)}) copy-start(f32[16,768]{1,0:T(8,128)} %get-tuple-element.291.refs_0_) | copy-start | bytes 147460
  136.2 14.1 %collective-permute-start.14 = (bf16[4,320,768]{2,1,0:T(8,128)(2,1)S(1)}, bf16[4,320,768]{2,1,0:T(8,128)(2,1)S(1)}, u32[]{:S(2)}, u32[]{:S(2)}) collective-permute-start(bf16[4,320,768]{2,1,0:T(8,128)(2,1)S(1)} %get-tuple-element.296), channel_id=1, source_target_pairs={{0,4},{4,0},{8,12},{12,8},{16,20},{20,16},{24,28},{28,24},{1,5},{5... | collective-permute-start | bytes 5898248 | tf_op jit(solution)/shard_map/ppermute | solution.py:643
  139.8 10.5 %collective-permute-start.15 = (bf16[480,384]{1,0:T(8,128)(2,1)S(1)}, bf16[480,384]{1,0:T(8,128)(2,1)S(1)}, u32[]{:S(2)}, u32[]{:S(2)}) collective-permute-start(bf16[480,384]{1,0:T(8,128)(2,1)S(1)} %get-tuple-element.302), channel_id=1, source_target_pairs={{0,2},{1,3},{2,0},{3,1},{4,6},{5,7},{6,4},{7,5},{8,10},{9,11},{10,... | collective-permute-start | bytes 1105928 | tf_op jit(solution)/shard_map/ppermute | solution.py:640
  140.5 9.9 %collective-permute-start.16 = (bf16[480,384]{1,0:T(8,128)(2,1)S(1)}, bf16[480,384]{1,0:T(8,128)(2,1)S(1)}, u32[]{:S(2)}, u32[]{:S(2)}) collective-permute-start(bf16[480,384]{1,0:T(8,128)(2,1)S(1)} %get-tuple-element.303), channel_id=1, source_target_pairs={{0,1},{1,0},{2,3},{3,2},{4,5},{5,4},{6,7},{7,6},{8,9},{9,8},{10,11... | collective-permute-start | bytes 1105928 | tf_op jit(solution)/shard_map/ppermute | solution.py:640
  142.3 8.0 %collective-permute-start.17 = (bf16[192,768]{1,0:T(8,128)(2,1)S(1)}, bf16[192,768]{1,0:T(8,128)(2,1)S(1)}, u32[]{:S(2)}, u32[]{:S(2)}) collective-permute-start(bf16[192,768]{1,0:T(8,128)(2,1)S(1)} %get-tuple-element.310), channel_id=1, source_target_pairs={{0,8},{4,12},{8,0},{12,4},{16,24},{20,28},{24,16},{28,20},{1,9},{5... | collective-permute-start | bytes 884744 | tf_op jit(solution)/shard_map/ppermute | solution.py:650
  151.7 11.4 %collective-permute-start.18 = (bf16[2,160,768]{2,1,0:T(8,128)(2,1)S(1)}, bf16[2,160,768]{2,1,0:T(8,128)(2,1)S(1)}, u32[]{:S(2)}, u32[]{:S(2)}) collective-permute-start(bf16[2,160,768]{2,1,0:T(8,128)(2,1)S(1)} %get-tuple-element.318), channel_id=1, source_target_pairs={{0,1},{1,0},{2,3},{3,2},{4,5},{5,4},{6,7},{7,6},{8,9},{9,8},{10,11... | collective-permute-start | bytes 1474568 | tf_op jit(solution)/shard_map/ppermute | solution.py:640
  152.8 11.3 %collective-permute-start.19 = (bf16[2,160,768]{2,1,0:T(8,128)(2,1)S(1)}, bf16[2,160,768]{2,1,0:T(8,128)(2,1)S(1)}, u32[]{:S(2)}, u32[]{:S(2)}) collective-permute-start(bf16[2,160,768]{2,1,0:T(8,128)(2,1)S(1)} %get-tuple-element.319), channel_id=1, source_target_pairs={{0,2},{1,3},{2,0},{3,1},{4,6},{5,7},{6,4},{7,5},{8,10},{9,11},{10,... | collective-permute-start | bytes 1474568 | tf_op jit(solution)/shard_map/ppermute | solution.py:640
  153.5 13.0 %copy-start.29 = (bf16[4,64,768]{2,1,0:T(8,128)(2,1)S(1)}, bf16[4,64,768]{2,1,0:T(8,128)(2,1)}, u32[]{:S(2)}) copy-start(bf16[4,64,768]{2,1,0:T(8,128)(2,1)} %get-tuple-element.352) | copy-start | bytes 1179652
  153.5 13.9 %copy-start.28 = (bf16[4,64,768]{2,1,0:T(8,128)(2,1)S(1)}, bf16[4,64,768]{2,1,0:T(8,128)(2,1)}, u32[]{:S(2)}) copy-start(bf16[4,64,768]{2,1,0:T(8,128)(2,1)} %get-tuple-element.353) | copy-start | bytes 1179652
  153.5 16.5 %copy-start.27 = (bf16[4,64,768]{2,1,0:T(8,128)(2,1)S(1)}, bf16[4,64,768]{2,1,0:T(8,128)(2,1)}, u32[]{:S(2)}) copy-start(bf16[4,64,768]{2,1,0:T(8,128)(2,1)} %get-tuple-element.354) | copy-start | bytes 1179652
  154.3 8.5 %collective-permute-start.20 = (bf16[480,384]{1,0:T(8,128)(2,1)S(1)}, bf16[480,384]{1,0:T(8,128)(2,1)S(1)}, u32[]{:S(2)}, u32[]{:S(2)}) collective-permute-start(bf16[480,384]{1,0:T(8,128)(2,1)S(1)} %get-tuple-element.328), channel_id=1, source_target_pairs={{0,8},{4,12},{8,0},{12,4},{16,24},{20,28},{24,16},{28,20},{1,9},{5... | collective-permute-start | bytes 1105928 | tf_op jit(solution)/shard_map/ppermute | solution.py:650
  155.7 11.7 %collective-permute-start.23 = (bf16[192,768]{1,0:T(8,128)(2,1)S(1)}, bf16[192,768]{1,0:T(8,128)(2,1)S(1)}, u32[]{:S(2)}, u32[]{:S(2)}) collective-permute-start(bf16[192,768]{1,0:T(8,128)(2,1)S(1)} %add_convert_fusion.3), channel_id=1, source_target_pairs={{0,24},{4,28},{8,16},{12,20},{16,8},{20,12},{24,0},{28,4},{1,25},{... | collective-permute-start | bytes 884744 | tf_op jit(solution)/shard_map/ppermute | solution.py:650
  164.1 24.4 %copy-start.13 = (bf16[4,64,768]{2,1,0:T(8,128)(2,1)S(1)}, bf16[4,64,768]{2,1,0:T(8,128)(2,1)}, u32[]{:S(2)}) copy-start(bf16[4,64,768]{2,1,0:T(8,128)(2,1)} %get-tuple-element.365) | copy-start | bytes 1179652
  164.1 26.1 %copy-start.14 = (bf16[4,64,768]{2,1,0:T(8,128)(2,1)S(1)}, bf16[4,64,768]{2,1,0:T(8,128)(2,1)}, u32[]{:S(2)}) copy-start(bf16[4,64,768]{2,1,0:T(8,128)(2,1)} %get-tuple-element.366) | copy-start | bytes 1179652
  164.1 26.7 %copy-start.15 = (bf16[4,64,768]{2,1,0:T(8,128)(2,1)S(1)}, bf16[4,64,768]{2,1,0:T(8,128)(2,1)}, u32[]{:S(2)}) copy-start(bf16[4,64,768]{2,1,0:T(8,128)(2,1)} %get-tuple-element.367) | copy-start | bytes 1179652
  164.9 5.1 %collective-permute-start.21 = (bf16[160,768]{1,0:T(8,128)(2,1)S(1)}, bf16[160,768]{1,0:T(8,128)(2,1)S(1)}, u32[]{:S(2)}, u32[]{:S(2)}) collective-permute-start(bf16[160,768]{1,0:T(8,128)(2,1)S(1)} %get-tuple-element.338), channel_id=1, source_target_pairs={{0,2},{1,3},{2,0},{3,1},{4,6},{5,7},{6,4},{7,5},{8,10},{9,11},{10,... | collective-permute-start | bytes 737288 | tf_op jit(solution)/shard_map/ppermute | solution.py:640
  165.6 5.4 %collective-permute-start.22 = (bf16[160,768]{1,0:T(8,128)(2,1)S(1)}, bf16[160,768]{1,0:T(8,128)(2,1)S(1)}, u32[]{:S(2)}, u32[]{:S(2)}) collective-permute-start(bf16[160,768]{1,0:T(8,128)(2,1)S(1)} %get-tuple-element.339), channel_id=1, source_target_pairs={{0,1},{1,0},{2,3},{3,2},{4,5},{5,4},{6,7},{7,6},{8,9},{9,8},{10,11... | collective-permute-start | bytes 737288 | tf_op jit(solution)/shard_map/ppermute | solution.py:640
  166.3 48.4 %copy-start.6 = (bf16[4,64,768]{2,1,0:T(8,128)(2,1)S(1)}, bf16[4,64,768]{2,1,0:T(8,128)(2,1)}, u32[]{:S(2)}) copy-start(bf16[4,64,768]{2,1,0:T(8,128)(2,1)} %get-tuple-element.381.refs_0_) | copy-start | bytes 1179652
  166.3 19.7 %collective-permute-start.25 = (bf16[480,384]{1,0:T(8,128)(2,1)S(1)}, bf16[480,384]{1,0:T(8,128)(2,1)S(1)}, u32[]{:S(2)}, u32[]{:S(2)}) collective-permute-start(bf16[480,384]{1,0:T(8,128)(2,1)S(1)} %add_convert_fusion.1), channel_id=1, source_target_pairs={{0,24},{4,28},{8,16},{12,20},{16,8},{20,12},{24,0},{28,4},{1,25},{... | collective-permute-start | bytes 1105928 | tf_op jit(solution)/shard_map/ppermute | solution.py:650
  166.6 20.9 %collective-permute-start.26 = (bf16[4,64,768]{2,1,0:T(8,128)(2,1)S(1)}, bf16[4,64,768]{2,1,0:T(8,128)(2,1)S(1)}, u32[]{:S(2)}, u32[]{:S(2)}) collective-permute-start(bf16[4,64,768]{2,1,0:T(8,128)(2,1)S(1)} %copy-done.29), channel_id=1, source_target_pairs={{0,1},{1,0},{2,3},{3,2},{4,5},{5,4},{6,7},{7,6},{8,9},{9,8},{10,11... | collective-permute-start | bytes 1179656 | tf_op jit(solution)/shard_map/ppermute | solution.py:640
  167.4 21.2 %collective-permute-start.27 = (bf16[4,64,768]{2,1,0:T(8,128)(2,1)S(1)}, bf16[4,64,768]{2,1,0:T(8,128)(2,1)S(1)}, u32[]{:S(2)}, u32[]{:S(2)}) collective-permute-start(bf16[4,64,768]{2,1,0:T(8,128)(2,1)S(1)} %copy-done.28), channel_id=1, source_target_pairs={{0,2},{1,3},{2,0},{3,1},{4,6},{5,7},{6,4},{7,5},{8,10},{9,11},{10,... | collective-permute-start | bytes 1179656 | tf_op jit(solution)/shard_map/ppermute | solution.py:640
  170.0 20.2 %collective-permute-start.28 = (bf16[4,64,768]{2,1,0:T(8,128)(2,1)S(1)}, bf16[4,64,768]{2,1,0:T(8,128)(2,1)S(1)}, u32[]{:S(2)}, u32[]{:S(2)}) collective-permute-start(bf16[4,64,768]{2,1,0:T(8,128)(2,1)S(1)} %copy-done.27), channel_id=1, source_target_pairs={{0,3},{1,2},{2,1},{3,0},{4,7},{5,6},{6,5},{7,4},{8,11},{9,10},{10,... | collective-permute-start | bytes 1179656 | tf_op jit(solution)/shard_map/ppermute | solution.py:640
  171.7 19.2 %collective-permute-start.24 = (bf16[160,768]{1,0:T(8,128)(2,1)S(1)}, bf16[160,768]{1,0:T(8,128)(2,1)S(1)}, u32[]{:S(2)}, u32[]{:S(2)}) collective-permute-start(bf16[160,768]{1,0:T(8,128)(2,1)S(1)} %get-tuple-element.351), channel_id=1, source_target_pairs={{0,8},{4,12},{8,0},{12,4},{16,24},{20,28},{24,16},{28,20},{1,9},{5... | collective-permute-start | bytes 737288 | tf_op jit(solution)/shard_map/ppermute | solution.py:650
  186.0 5.6 %collective-permute-start.31 = (bf16[192,768]{1,0:T(8,128)(2,1)S(1)}, bf16[192,768]{1,0:T(8,128)(2,1)S(1)}, u32[]{:S(2)}, u32[]{:S(2)}) collective-permute-start(bf16[192,768]{1,0:T(8,128)(2,1)S(1)} %add_convert_fusion.2.refs_0_), channel_id=1, source_target_pairs={{0,4},{4,0},{8,12},{12,8},{16,20},{20,16},{24,28},{28,24},{1,5},{5... | collective-permute-start | bytes 884744 | tf_op jit(solution)/shard_map/ppermute | solution.py:643
  187.4 8.7 %collective-permute-start.30 = (bf16[192,768]{1,0:T(8,128)(2,1)S(1)}, bf16[192,768]{1,0:T(8,128)(2,1)S(1)}, u32[]{:S(2)}, u32[]{:S(2)}) collective-permute-start(bf16[192,768]{1,0:T(8,128)(2,1)S(1)} %add_convert_fusion.2.refs_0_), channel_id=1, source_target_pairs={{0,8},{4,12},{8,0},{12,4},{16,24},{20,28},{24,16},{28,20},{1,9},{5... | collective-permute-start | bytes 884744 | tf_op jit(solution)/shard_map/ppermute | solution.py:650
  188.6 9.9 %collective-permute-start.32 = (bf16[4,64,768]{2,1,0:T(8,128)(2,1)S(1)}, bf16[4,64,768]{2,1,0:T(8,128)(2,1)S(1)}, u32[]{:S(2)}, u32[]{:S(2)}) collective-permute-start(bf16[4,64,768]{2,1,0:T(8,128)(2,1)S(1)} %copy-done.13), channel_id=1, source_target_pairs={{0,1},{1,0},{2,3},{3,2},{4,5},{5,4},{6,7},{7,6},{8,9},{9,8},{10,11... | collective-permute-start | bytes 1179656 | tf_op jit(solution)/shard_map/ppermute | solution.py:640
  190.2 11.2 %collective-permute-start.33 = (bf16[4,64,768]{2,1,0:T(8,128)(2,1)S(1)}, bf16[4,64,768]{2,1,0:T(8,128)(2,1)S(1)}, u32[]{:S(2)}, u32[]{:S(2)}) collective-permute-start(bf16[4,64,768]{2,1,0:T(8,128)(2,1)S(1)} %copy-done.14), channel_id=1, source_target_pairs={{0,2},{1,3},{2,0},{3,1},{4,6},{5,7},{6,4},{7,5},{8,10},{9,11},{10,... | collective-permute-start | bytes 1179656 | tf_op jit(solution)/shard_map/ppermute | solution.py:640
  190.8 17.8 %collective-permute-start.34 = (bf16[4,64,768]{2,1,0:T(8,128)(2,1)S(1)}, bf16[4,64,768]{2,1,0:T(8,128)(2,1)S(1)}, u32[]{:S(2)}, u32[]{:S(2)}) collective-permute-start(bf16[4,64,768]{2,1,0:T(8,128)(2,1)S(1)} %copy-done.15), channel_id=1, source_target_pairs={{0,3},{1,2},{2,1},{3,0},{4,7},{5,6},{6,5},{7,4},{8,11},{9,10},{10,... | collective-permute-start | bytes 1179656 | tf_op jit(solution)/shard_map/ppermute | solution.py:640
  191.6 25.4 %copy-start.3 = (bf16[4,64,768]{2,1,0:T(8,128)(2,1)S(1)}, bf16[4,64,768]{2,1,0:T(8,128)(2,1)}, u32[]{:S(2)}) copy-start(bf16[4,64,768]{2,1,0:T(8,128)(2,1)} %get-tuple-element.388.refs_0_) | copy-start | bytes 1179652
  191.6 17.0 %collective-permute-start.29 = (bf16[160,768]{1,0:T(8,128)(2,1)S(1)}, bf16[160,768]{1,0:T(8,128)(2,1)S(1)}, u32[]{:S(2)}, u32[]{:S(2)}) collective-permute-start(bf16[160,768]{1,0:T(8,128)(2,1)S(1)} %add_convert_fusion.5), channel_id=1, source_target_pairs={{0,24},{4,28},{8,16},{12,20},{16,8},{20,12},{24,0},{28,4},{1,25},{... | collective-permute-start | bytes 737288 | tf_op jit(solution)/shard_map/ppermute | solution.py:650
  196.2 12.5 %collective-permute-start.38 = (bf16[480,384]{1,0:T(8,128)(2,1)S(1)}, bf16[480,384]{1,0:T(8,128)(2,1)S(1)}, u32[]{:S(2)}, u32[]{:S(2)}) collective-permute-start(bf16[480,384]{1,0:T(8,128)(2,1)S(1)} %add_convert_fusion.refs_0_), channel_id=1, source_target_pairs={{0,4},{4,0},{8,12},{12,8},{16,20},{20,16},{24,28},{28,24},{1,5},{5... | collective-permute-start | bytes 1105928 | tf_op jit(solution)/shard_map/ppermute | solution.py:643
  198.5 12.1 %collective-permute-start.37 = (bf16[480,384]{1,0:T(8,128)(2,1)S(1)}, bf16[480,384]{1,0:T(8,128)(2,1)S(1)}, u32[]{:S(2)}, u32[]{:S(2)}) collective-permute-start(bf16[480,384]{1,0:T(8,128)(2,1)S(1)} %add_convert_fusion.refs_0_), channel_id=1, source_target_pairs={{0,8},{4,12},{8,0},{12,4},{16,24},{20,28},{24,16},{28,20},{1,9},{5... | collective-permute-start | bytes 1105928 | tf_op jit(solution)/shard_map/ppermute | solution.py:650
  210.6 11.1 %collective-permute-start.39 = (bf16[480,384]{1,0:T(8,128)(2,1)S(1)}, bf16[480,384]{1,0:T(8,128)(2,1)S(1)}, u32[]{:S(2)}, u32[]{:S(2)}) collective-permute-start(bf16[480,384]{1,0:T(8,128)(2,1)S(1)} %collective-permute-done.37.refs_1_), channel_id=1, source_target_pairs={{0,4},{4,0},{8,12},{12,8},{16,20},{20,16},{24,28},{28,24},{1,5},{5... | collective-permute-start | bytes 1105928 | tf_op jit(solution)/shard_map/ppermute | solution.py:643
  213.6 8.1 %collective-permute-start.40 = (bf16[192,768]{1,0:T(8,128)(2,1)S(1)}, bf16[192,768]{1,0:T(8,128)(2,1)S(1)}, u32[]{:S(2)}, u32[]{:S(2)}) collective-permute-start(bf16[192,768]{1,0:T(8,128)(2,1)S(1)} %collective-permute-done.30.refs_1_), channel_id=1, source_target_pairs={{0,4},{4,0},{8,12},{12,8},{16,20},{20,16},{24,28},{28,24},{1,5},{5... | collective-permute-start | bytes 884744 | tf_op jit(solution)/shard_map/ppermute | solution.py:643
  213.6 6.1 %collective-permute-start.36 = (bf16[160,768]{1,0:T(8,128)(2,1)S(1)}, bf16[160,768]{1,0:T(8,128)(2,1)S(1)}, u32[]{:S(2)}, u32[]{:S(2)}) collective-permute-start(bf16[160,768]{1,0:T(8,128)(2,1)S(1)} %add_convert_fusion.4.refs_0_), channel_id=1, source_target_pairs={{0,4},{4,0},{8,12},{12,8},{16,20},{20,16},{24,28},{28,24},{1,5},{5... | collective-permute-start | bytes 737288 | tf_op jit(solution)/shard_map/ppermute | solution.py:643
  214.1 7.6 %collective-permute-start.35 = (bf16[160,768]{1,0:T(8,128)(2,1)S(1)}, bf16[160,768]{1,0:T(8,128)(2,1)S(1)}, u32[]{:S(2)}, u32[]{:S(2)}) collective-permute-start(bf16[160,768]{1,0:T(8,128)(2,1)S(1)} %add_convert_fusion.4.refs_0_), channel_id=1, source_target_pairs={{0,8},{4,12},{8,0},{12,4},{16,24},{20,28},{24,16},{28,20},{1,9},{5... | collective-permute-start | bytes 737288 | tf_op jit(solution)/shard_map/ppermute | solution.py:650
  221.7 5.4 %collective-permute-start.41 = (bf16[160,768]{1,0:T(8,128)(2,1)S(1)}, bf16[160,768]{1,0:T(8,128)(2,1)S(1)}, u32[]{:S(2)}, u32[]{:S(2)}) collective-permute-start(bf16[160,768]{1,0:T(8,128)(2,1)S(1)} %collective-permute-done.35.refs_1_), channel_id=1, source_target_pairs={{0,4},{4,0},{8,12},{12,8},{16,20},{20,16},{24,28},{28,24},{1,5},{5... | collective-permute-start | bytes 737288 | tf_op jit(solution)/shard_map/ppermute | solution.py:643
  (8 other events, 27.9 us)

commit v2 on v1

--- a/solution.py
+++ b/solution.py
@@ -1075,12 +1075,12 @@
         gouts, down.land = wait_for((gouts, down.land), qkv.own)
         gin_land = swap(gouts[1:])
         down.outer()
-        qkv.land, up.land, out_land, qkv.own, down.own = join(qkv.land, up.land, out_land, qkv.own, down.own)
+        qkv.land, up.land, qkv.own, down.own = join(qkv.land, up.land, qkv.own, down.own)
 
         qkv.inner()
         up.land = wait_for(up.land, qkv.own)
         up.outer()
-        qkv.land, down.land, gin_land, qkv.own, up.own = join(qkv.land, down.land, gin_land, qkv.own, up.own)
+        qkv.land, down.land, out_land, gin_land, qkv.own, up.own = join(qkv.land, down.land, out_land, gin_land, qkv.own, up.own)
 
         qkv.outer()
         up.land = wait_for(up.land, qkv.own)
@@ -1089,11 +1089,11 @@
         down.swap()
         output = place_frames(info, [outs[0], *wait_for(out_land, up.parts[1])], BF16)
         grad_input = place_frames(info, [gouts[0], *wait_for(gin_land, up.parts[1])], F32)
-        qkv.land, up.land, down.land, up.parts, down.parts, qkv.own, output, grad_input = join(qkv.land, up.land, down.land, up.parts, down.parts, qkv.own, output, grad_input)
+        down.parts, down.land = wait_for((down.parts, down.land), grad_input)
+        (grad_w_down,) = down.last(finish_down_kernel, "finish_down", [(model // 4, hidden_size)])
+        qkv.land, up.land, up.parts, qkv.own, output, grad_w_down = join(qkv.land, up.land, up.parts, qkv.own, output, grad_w_down)
 
         qkv.swap()
-        down.parts, down.land = wait_for((down.parts, down.land), qkv.parts[0])
-        (grad_w_down,) = down.last(finish_down_kernel, "finish_down", [(model // 4, hidden_size)])
         up.parts, up.land = wait_for((up.parts, up.land), qkv.parts[0])
         grad_w_up, grad_w_out = up.last(
             finish_up_kernel, "finish_up", [(model, hidden_size // 4), (model // 4, model)]

time: 231 us -> 229 us (level)
  waiting for transfers between devices: 63.2 us -> 55.8 us
  starting transfers between devices: 40.5 us -> 47.3 us
    ppermute x24, waiting for transfers between devices: 24.2 us -> 16.1 us  [col_swap(): lax.ppermute(array, 'col', [(i, i ^ distance) for i in range(self.ncol)])]
    ppermute x9, starting transfers between devices: 10.9 us -> 15.6 us  [core_swap(): return lax.ppermute(array, 'clip', [(i, i ^ 1) for i in range(self.nclip)])]
  transfers between devices with their start and end apart: 42 -> 42, of which waited for: 15 -> 12; matrix products, arithmetic and copies ran while one was open for 1% -> 1% of each run, Pallas kernels for 30% -> 30%
where the time goes in v2:
time: 229 us; the launch traced here: 228 us
  Pallas kernels  120 us (52%)
  waiting for transfers between devices  55.8 us (24%)
  starting transfers between devices  47.3 us (21%)
  local copies, waits for them, and re-layouts  3.63 us (2%)
    pallas_call x1, Pallas kernels, mlp_call(): pl.pallas_call(functools.partial(mlp_kernel, ncol), grid_spec=pltpu.Prefe...  44.2 us
    ppermute x9, waiting for transfers between devices, z_swap(): lax.ppermute(array, 'clip', [(i, i ^ 2 * distance) for i in range(self.nc...  35.4 us
    pallas_call x2, Pallas kernels, attend_back_call(): pl.pallas_call(functools.partial(attend_back_kernel, ncol, block, first),...  27.2 us
    ppermute x24, starting transfers between devices, col_swap(): lax.ppermute(array, 'col', [(i, i ^ distance) for i in range(self.ncol)])  20.2 us
    ppermute x24, waiting for transfers between devices, col_swap(): lax.ppermute(array, 'col', [(i, i ^ distance) for i in range(self.ncol)])  16.1 us
    pallas_call x1, Pallas kernels, attend_call(): pl.pallas_call(functools.partial(attend_kernel, ncol, block, first), grid...  15.8 us
    ppermute x9, starting transfers between devices, core_swap(): return lax.ppermute(array, 'clip', [(i, i ^ 1) for i in range(self.nclip)])  15.6 us
    ppermute x9, starting transfers between devices, z_swap(): lax.ppermute(array, 'clip', [(i, i ^ 2 * distance) for i in range(self.nc...  11.5 us
  transfers between devices with their start and end apart: 42, of which 12 were waited for; matrix products, arithmetic and copies ran while one was open for 1% of the time, Pallas kernels for 30%

profile of v2, /device:TPU:17, one launch (start us, length us, event | category | flops | bytes accessed | tf_op | source)
XLA Modules:
  0.0 228.4 jit_solution(3850857272293374529)
XLA Ops:
  0.8 2.8 %take_frames.2 = (bf16[4,64,768]{2,1,0:T(8,128)(2,1)}, bf16[4,64,768]{2,1,0:T(8,128)(2,1)}, bf16[4,64,768]{2,1,0:T(8,128)(2,1)}) custom-call(s32[5]{0:T(128)S(1)} %stack.27.info, bf16[16,64,768]{2,1,0:T(8,128)(2,1)} %refs_0_.11, bf16[16,64,768]{2,1,0:T(8,128)(2,1)} %refs_0_.11, bf16[16,64,768]{2,1,0:T(8,128)(2,1)} %refs_0_.11), custom_call_target="tpu_custom_call" | custom-call | bytes 1500000 | tf_op jit(solution)/shard_map/take_frames/pallas_call | solution.py:584
  3.7 1.2 collective-permute-start
  4.9 1.2 collective-permute-start.1
  7.3 2.8 %take_frames.3 = (bf16[4,64,768]{2,1,0:T(8,128)(2,1)}, bf16[4,64,768]{2,1,0:T(8,128)(2,1)}, bf16[4,64,768]{2,1,0:T(8,128)(2,1)}) custom-call(s32[5]{0:T(128)S(1)} %stack.27.info, bf16[16,64,768]{2,1,0:T(8,128)(2,1)} %refs_0_.9, bf16[16,64,768]{2,1,0:T(8,128)(2,1)} %refs_0_.9, bf16[16,64,768]{2,1,0:T(8,128)(2,1)} %refs_0_.9), custom_call_target="tpu_custom_call" | custom-call | bytes 1500000 | tf_op jit(solution)/shard_map/take_frames/pallas_call | solution.py:584
  10.1 3.8 %collective-permute-done.refs_1_ = bf16[4,64,768]{2,1,0:T(8,128)(2,1)S(1)} collective-permute-done((bf16[4,64,768]{2,1,0:T(8,128)(2,1)}, bf16[4,64,768]{2,1,0:T(8,128)(2,1)S(1)}, u32[]{:S(2)}, u32[]{:S(2)}) %collective-permute-start) | collective-permute-done | bytes 393248 | tf_op jit(solution)/shard_map/ppermute | solution.py:640
  13.9 1.2 collective-permute-start.3
  15.1 1.2 collective-permute-start.4
  16.7 6.6 %collective-permute-done.2.refs_3_ = bf16[4,64,768]{2,1,0:T(8,128)(2,1)S(1)} collective-permute-done((bf16[4,64,768]{2,1,0:T(8,128)(2,1)}, bf16[4,64,768]{2,1,0:T(8,128)(2,1)S(1)}, u32[]{:S(2)}, u32[]{:S(2)}) %collective-permute-start.2) | collective-permute-done | bytes 393248 | tf_op jit(solution)/shard_map/ppermute | solution.py:640
  23.3 15.8 %attend.1 = (bf16[2304,1024]{1,0:T(8,128)(2,1)}, bf16[768,1024]{1,0:T(8,128)(2,1)}, f32[1024,768]{1,0:T(8,128)}, f32[4,16,256]{2,1,0:T(8,128)}) custom-call(s32[5]{0:T(128)S(1)} %stack.27.info, s32[4]{0:T(128)S(1)} %dynamic-slice_bitcast_fusion.lens, bf16[16,64,768]{2,1,0:T(8,128)(2,1)S(1)} %copy-done, bf16[4,64,768]{2,1,0:T(8,128)(2,1)S(1)} %collective-permute-done.refs_1_, ...), custom_call_target="tpu_custom_call" | custom-call | bytes 15000000 | tf_op jit(solution)/shard_map/attend/pallas_call | solution.py:189
  39.1 2.5 %collective-permute-done.4.refs_2_ = bf16[4,64,768]{2,1,0:T(8,128)(2,1)} collective-permute-done((bf16[4,64,768]{2,1,0:T(8,128)(2,1)}, bf16[4,64,768]{2,1,0:T(8,128)(2,1)}, u32[]{:S(2)}, u32[]{:S(2)}) %collective-permute-start.4) | collective-permute-done | bytes 393248 | tf_op jit(solution)/shard_map/ppermute | solution.py:640
  41.5 44.2 %mlp.1 = (bf16[4,64,768]{2,1,0:T(8,128)(2,1)}, bf16[4,64,768]{2,1,0:T(8,128)(2,1)}, bf16[4,64,768]{2,1,0:T(8,128)(2,1)}, bf16[4,64,768]{2,1,0:T(8,128)(2,1)}, f3...) custom-call(s32[5]{0:T(128)} %copy-done.8, ...), custom_call_target="tpu_custom_call" | custom-call | bytes 60000000 | tf_op jit(solution)/shard_map/mlp/pallas_call | solution.py:375
  85.8 1.1 collective-permute-start.6
  86.9 4.3 %collective-permute-done.6.refs_4_.refs_5_.refs_6_.refs_7_ = bf16[4,384,768]{2,1,0:T(8,128)(2,1)S(1)} collective-permute-done((bf16[4,384,768]{2,1,0:T(8,128)(2,1)}, bf16[4,384,768]{2,1,0:T(8,128)(2,1)S(1)}, u32[]{:S(2)}, u32[]{:S(2)}) %collective-permute-start.6) | collective-permute-done | bytes 2359328 | tf_op jit(solution)/shard_map/ppermute | solution.py:643
  91.2 1.7 copy-done.2
  92.9 1.1 sum_core.3
  94.0 1.3 collective-permute-start.7
  95.6 13.9 %attend_back.2 = (bf16[2304,1024]{1,0:T(8,128)(2,1)}, bf16[1024,768]{1,0:T(8,128)(2,1)}, f32[16,768]{1,0:T(8,128)}, bf16[4,64,768]{2,1,0:T(8,128)(2,1)}, bf16[4,...) custom-call(s32[5]{0:T(128)S(1)} %copy-done.9, ...), custom_call_target="tpu_custom_call" | custom-call | bytes 22500000 | tf_op jit(solution)/shard_map/attend_back/pallas_call | solution.py:524
  109.6 0.8 sum_first.3
  110.4 1.3 sum_core.4
  111.7 1.5 collective-permute-start.12
  113.4 1.2 collective-permute-start.10
  114.7 13.3 %attend_back.3 = (bf16[2304,1024]{1,0:T(8,128)(2,1)}, bf16[1024,768]{1,0:T(8,128)(2,1)}, f32[16,768]{1,0:T(8,128)}, bf16[4,64,768]{2,1,0:T(8,128)(2,1)}, bf16[4,...) custom-call(s32[5]{0:T(128)S(1)} %copy-done.9, ...), custom_call_target="tpu_custom_call", output_to_operand_aliasing={{0}: (14, {}), {1}: (15, {}), {3}: (16, {}), {4}: (17, {}),... | custom-call | bytes 22500000 | tf_op jit(solution)/shard_map/attend_back/pallas_call | solution.py:524
  128.0 0.8 copy-done.12
  128.8 7.3 %grad_qkv.1 = (bf16[4,320,768]{2,1,0:T(8,128)(2,1)S(1)}, bf16[4,320,768]{2,1,0:T(8,128)(2,1)S(1)}) custom-call(s32[5]{0:T(128)S(1)} %copy-done.9, bf16[2304,1024]{1,0:T(8,128)(2,1)} %get-tuple-element.284.gproj_t, bf16[1024,768]{1,0:T(8,128)(2,1)} %get-tuple-element.285.normed_n, f32[16,768]{1,0:T(8,128)S(1)} %copy-done.10, f32[16,768]{1,0:T(8,128)S(1)} %copy-done.11, ...), custom_call_target="tpu_custom_call" | custom-call | bytes 9000000 | tf_op jit(solution)/shard_map/grad_qkv/pallas_call | solution.py:744
  136.2 2.7 %collective-permute-start.14 = (bf16[4,320,768]{2,1,0:T(8,128)(2,1)S(1)}, bf16[4,320,768]{2,1,0:T(8,128)(2,1)S(1)}, u32[]{:S(2)}, u32[]{:S(2)}) collective-permute-start(bf16[4,320,768]{2,1,0:T(8,128)(2,1)S(1)} %get-tuple-element.292), channel_id=1, source_target_pairs={{0,4},{4,0},{8,12},{12,8},{16,20},{20,16},{24,28},{28,24},{1,5},{5... | collective-permute-start | bytes 5898248 | tf_op jit(solution)/shard_map/ppermute | solution.py:643
  138.9 0.9 sum_first.4
  139.8 0.7 collective-permute-start.15
  140.5 1.1 collective-permute-start.16
  141.6 0.7 sum_second.3
  142.3 1.4 collective-permute-start.17
  143.6 6.7 %collective-permute-done.17 = bf16[192,768]{1,0:T(8,128)(2,1)S(1)} collective-permute-done((bf16[192,768]{1,0:T(8,128)(2,1)S(1)}, bf16[192,768]{1,0:T(8,128)(2,1)S(1)}, u32[]{:S(2)}, u32[]{:S(2)}) %collective-permute-start.17) | collective-permute-done | bytes 294944 | tf_op jit(solution)/shard_map/ppermute | solution.py:650
  150.4 1.3 sum_core.5
  151.7 1.1 collective-permute-start.18
  152.8 0.6 collective-permute-start.19
  153.5 0.8 sum_second.4
  154.3 1.4 collective-permute-start.20
  155.7 7.1 %collective-permute-done.20 = bf16[480,384]{1,0:T(8,128)(2,1)S(1)} collective-permute-done((bf16[480,384]{1,0:T(8,128)(2,1)S(1)}, bf16[480,384]{1,0:T(8,128)(2,1)S(1)}, u32[]{:S(2)}, u32[]{:S(2)}) %collective-permute-start.20) | collective-permute-done | bytes 368672 | tf_op jit(solution)/shard_map/ppermute | solution.py:650
  163.1 1.1 collective-permute-done.19.land_b
  164.1 0.8 sum_first.5
  164.9 0.7 collective-permute-start.21
  165.6 0.6 collective-permute-start.22
  166.6 0.9 collective-permute-start.29
  167.4 0.9 collective-permute-start.30
  168.3 1.8 collective-permute-done.21.land_a
  170.0 0.9 collective-permute-start.31
  171.0 0.7 sum_second.5
  171.7 1.7 collective-permute-start.24
  173.4 12.6 %collective-permute-done.25 = bf16[480,384]{1,0:T(8,128)(2,1)S(1)} collective-permute-done((bf16[480,384]{1,0:T(8,128)(2,1)S(1)}, bf16[480,384]{1,0:T(8,128)(2,1)S(1)}, u32[]{:S(2)}, u32[]{:S(2)}) %collective-permute-start.25) | collective-permute-done | bytes 368672 | tf_op jit(solution)/shard_map/ppermute | solution.py:650
  186.0 1.4 collective-permute-start.28
  187.4 1.1 collective-permute-start.27
  188.6 1.6 collective-permute-start.32
  190.2 0.6 collective-permute-start.33
  190.8 0.7 collective-permute-start.34
  191.8 1.4 collective-permute-done.27.refs_1_
  193.2 7.6 %collective-permute-start.38 = (bf16[480,384]{1,0:T(8,128)(2,1)S(1)}, bf16[480,384]{1,0:T(8,128)(2,1)S(1)}, u32[]{:S(2)}, u32[]{:S(2)}) collective-permute-start(bf16[480,384]{1,0:T(8,128)(2,1)S(1)} %add_convert_fusion.refs_0_), channel_id=1, source_target_pairs={{0,4},{4,0},{8,12},{12,8},{16,20},{20,16},{24,28},{28,24},{1,5},{5... | collective-permute-start | bytes 1105928 | tf_op jit(solution)/shard_map/ppermute | solution.py:643
  200.8 4.2 %collective-permute-start.37 = (bf16[480,384]{1,0:T(8,128)(2,1)S(1)}, bf16[480,384]{1,0:T(8,128)(2,1)S(1)}, u32[]{:S(2)}, u32[]{:S(2)}) collective-permute-start(bf16[480,384]{1,0:T(8,128)(2,1)S(1)} %add_convert_fusion.refs_0_), channel_id=1, source_target_pairs={{0,8},{4,12},{8,0},{12,4},{16,24},{20,28},{24,16},{28,20},{1,9},{5... | collective-permute-start | bytes 1105928 | tf_op jit(solution)/shard_map/ppermute | solution.py:650
  205.0 7.5 %collective-permute-done.37.refs_1_ = bf16[480,384]{1,0:T(8,128)(2,1)S(1)} collective-permute-done((bf16[480,384]{1,0:T(8,128)(2,1)S(1)}, bf16[480,384]{1,0:T(8,128)(2,1)S(1)}, u32[]{:S(2)}, u32[]{:S(2)}) %collective-permute-start.37) | collective-permute-done | bytes 368672 | tf_op jit(solution)/shard_map/ppermute | solution.py:650
  212.6 1.9 collective-permute-start.39
  215.0 1.5 collective-permute-start.35
  216.5 2.3 place_frames.2
  218.7 2.7 %place_frames.3 = f32[16,64,768]{2,1,0:T(8,128)} custom-call(s32[5]{0:T(128)S(1)} %copy-done.9, bf16[4,64,768]{2,1,0:T(8,128)(2,1)S(1)} %copy-done.3, bf16[4,64,768]{2,1,0:T(8,128)(2,1)S(1)} %collective-permute-done.32.refs_1_, bf16[4,64,768]{2,1,0:T(8,128)(2,1)S(1)} %collective-permute-done.33.refs_2_, bf16[4,64,768]{2,1,0:T(8,128)(2,1)S(1)} %collective-permute-done.34.refs_3_), custom_call_target="tpu_custom_call" | custom-call | bytes 3000000 | tf_op jit(solution)/shard_map/place_frames/pallas_call | solution.py:610
  221.4 2.2 finish_down.1
  224.0 2.4 %finish_up.1 = (f32[768,768]{1,0:T(8,128)}, f32[192,768]{1,0:T(8,128)}) custom-call(s32[5]{0:T(128)S(1)} %copy-done.9, bf16[480,384]{1,0:T(8,128)(2,1)S(1)} %add_convert_fusion.refs_0_, bf16[480,384]{1,0:T(8,128)(2,1)S(1)} %collective-permute-done.37.refs_1_, bf16[480,384]{1,0:T(8,128)(2,1)S(1)} %collective-permute-done.38.refs_2_, ...), custom_call_target="tpu_custom_call" | custom-call | bytes 3000000 | tf_op jit(solution)/shard_map/finish_up/pallas_call | solution.py:887
  226.4 1.9 finish_qkv.1
  (118 shorter events, 4.4 us)
Async XLA Ops:
  0.7 22.5 %copy-start.8 = (s32[5]{0:T(128)}, s32[5]{0:T(128)S(1)}, u32[]{:S(2)}) copy-start(s32[5]{0:T(128)S(1)} %stack.27.info) | copy-start | bytes 64
  0.8 6.3 %copy-start.17 = (bf16[3072]{0:T(1024)(128)(2,1)S(1)}, bf16[3072]{0:T(1024)(128)(2,1)}, u32[]{:S(2)}) copy-start(bf16[3072]{0:T(1024)(128)(2,1)} %param.29) | copy-start | bytes 18436
  0.8 6.3 %copy-start.18 = (bf16[1536]{0:T(1024)(128)(2,1)S(1)}, bf16[1536]{0:T(1024)(128)(2,1)}, u32[]{:S(2)}) copy-start(bf16[1536]{0:T(1024)(128)(2,1)} %param.23) | copy-start | bytes 9220
  0.8 6.3 %copy-start.19 = (bf16[768]{0:T(1024)(128)(2,1)S(1)}, bf16[768]{0:T(1024)(128)(2,1)}, u32[]{:S(2)}) copy-start(bf16[768]{0:T(1024)(128)(2,1)} %param.31) | copy-start | bytes 4612
  0.8 6.3 %copy-start.20 = (bf16[768]{0:T(1024)(128)(2,1)S(1)}, bf16[768]{0:T(1024)(128)(2,1)}, u32[]{:S(2)}) copy-start(bf16[768]{0:T(1024)(128)(2,1)} %param.27) | copy-start | bytes 4612
  0.8 6.3 %copy-start.21 = (bf16[768]{0:T(1024)(128)(2,1)S(1)}, bf16[768]{0:T(1024)(128)(2,1)}, u32[]{:S(2)}) copy-start(bf16[768]{0:T(1024)(128)(2,1)} %param.26) | copy-start | bytes 4612
  0.8 6.3 %copy-start.22 = (bf16[768]{0:T(1024)(128)(2,1)S(1)}, bf16[768]{0:T(1024)(128)(2,1)}, u32[]{:S(2)}) copy-start(bf16[768]{0:T(1024)(128)(2,1)} %param.25) | copy-start | bytes 4612
  0.8 6.3 %copy-start.23 = (bf16[768]{0:T(1024)(128)(2,1)S(1)}, bf16[768]{0:T(1024)(128)(2,1)}, u32[]{:S(2)}) copy-start(bf16[768]{0:T(1024)(128)(2,1)} %param.21) | copy-start | bytes 4612
  3.7 10.2 %collective-permute-start = (bf16[4,64,768]{2,1,0:T(8,128)(2,1)}, bf16[4,64,768]{2,1,0:T(8,128)(2,1)S(1)}, u32[]{:S(2)}, u32[]{:S(2)}) collective-permute-start(bf16[4,64,768]{2,1,0:T(8,128)(2,1)} %get-tuple-element.219), channel_id=1, source_target_pairs={{0,1},{1,0},{2,3},{3,2},{4,5},{5,4},{6,7},{7,6},{8,9},{9,8},{10,11... | collective-permute-start | bytes 1179656 | tf_op jit(solution)/shard_map/ppermute | solution.py:640
  4.9 11.8 %collective-permute-start.1 = (bf16[4,64,768]{2,1,0:T(8,128)(2,1)}, bf16[4,64,768]{2,1,0:T(8,128)(2,1)S(1)}, u32[]{:S(2)}, u32[]{:S(2)}) collective-permute-start(bf16[4,64,768]{2,1,0:T(8,128)(2,1)} %get-tuple-element.225), channel_id=1, source_target_pairs={{0,2},{1,3},{2,0},{3,1},{4,6},{5,7},{6,4},{7,5},{8,10},{9,11},{10,... | collective-permute-start | bytes 1179656 | tf_op jit(solution)/shard_map/ppermute | solution.py:640
  6.1 17.2 %collective-permute-start.2 = (bf16[4,64,768]{2,1,0:T(8,128)(2,1)}, bf16[4,64,768]{2,1,0:T(8,128)(2,1)S(1)}, u32[]{:S(2)}, u32[]{:S(2)}) collective-permute-start(bf16[4,64,768]{2,1,0:T(8,128)(2,1)} %get-tuple-element.226), channel_id=1, source_target_pairs={{0,3},{1,2},{2,1},{3,0},{4,7},{5,6},{6,5},{7,4},{8,11},{9,10},{10,... | collective-permute-start | bytes 1179656 | tf_op jit(solution)/shard_map/ppermute | solution.py:640
  7.3 16.0 %copy-start.4 = (f32[12,768]{1,0:T(8,128)}, f32[12,768]{1,0:T(8,128)S(1)}, u32[]{:S(2)}) copy-start(f32[12,768]{1,0:T(8,128)S(1)} %reshape.58.refs_5_.refs_6_) | copy-start | bytes 110596
  7.3 16.0 %copy-start = (bf16[16,64,768]{2,1,0:T(8,128)(2,1)S(1)}, bf16[16,64,768]{2,1,0:T(8,128)(2,1)}, u32[]{:S(2)}) copy-start(bf16[16,64,768]{2,1,0:T(8,128)(2,1)} %refs_0_.11) | copy-start | bytes 4718596
  13.9 25.2 %collective-permute-start.3 = (bf16[4,64,768]{2,1,0:T(8,128)(2,1)}, bf16[4,64,768]{2,1,0:T(8,128)(2,1)S(1)}, u32[]{:S(2)}, u32[]{:S(2)}) collective-permute-start(bf16[4,64,768]{2,1,0:T(8,128)(2,1)} %get-tuple-element.236), channel_id=1, source_target_pairs={{0,1},{1,0},{2,3},{3,2},{4,5},{5,4},{6,7},{7,6},{8,9},{9,8},{10,11... | collective-permute-start | bytes 1179656 | tf_op jit(solution)/shard_map/ppermute | solution.py:640
  15.1 26.4 %collective-permute-start.4 = (bf16[4,64,768]{2,1,0:T(8,128)(2,1)}, bf16[4,64,768]{2,1,0:T(8,128)(2,1)}, u32[]{:S(2)}, u32[]{:S(2)}) collective-permute-start(bf16[4,64,768]{2,1,0:T(8,128)(2,1)} %get-tuple-element.237), channel_id=1, source_target_pairs={{0,2},{1,3},{2,0},{3,1},{4,6},{5,7},{6,4},{7,5},{8,10},{9,11},{10,... | collective-permute-start | bytes 1179656 | tf_op jit(solution)/shard_map/ppermute | solution.py:640
  16.3 25.2 %collective-permute-start.5 = (bf16[4,64,768]{2,1,0:T(8,128)(2,1)}, bf16[4,64,768]{2,1,0:T(8,128)(2,1)}, u32[]{:S(2)}, u32[]{:S(2)}) collective-permute-start(bf16[4,64,768]{2,1,0:T(8,128)(2,1)} %get-tuple-element.238), channel_id=1, source_target_pairs={{0,3},{1,2},{2,1},{3,0},{4,7},{5,6},{6,5},{7,4},{8,11},{9,10},{10,... | collective-permute-start | bytes 1179656 | tf_op jit(solution)/shard_map/ppermute | solution.py:640
  41.5 49.7 %copy-start.9 = (s32[5]{0:T(128)S(1)}, s32[5]{0:T(128)}, u32[]{:S(2)}) copy-start(s32[5]{0:T(128)} %copy-done.8) | copy-start | bytes 64
  85.8 5.5 %collective-permute-start.6 = (bf16[4,384,768]{2,1,0:T(8,128)(2,1)}, bf16[4,384,768]{2,1,0:T(8,128)(2,1)S(1)}, u32[]{:S(2)}, u32[]{:S(2)}) collective-permute-start(bf16[4,384,768]{2,1,0:T(8,128)(2,1)} %get-tuple-element.245), channel_id=1, source_target_pairs={{0,4},{4,0},{8,12},{12,8},{16,20},{20,16},{24,28},{28,24},{1,5},{5... | collective-permute-start | bytes 7077896 | tf_op jit(solution)/shard_map/ppermute | solution.py:643
  86.9 22.7 %collective-permute-start.9 = (bf16[4,960,384]{2,1,0:T(8,128)(2,1)}, bf16[4,960,384]{2,1,0:T(8,128)(2,1)S(1)}, u32[]{:S(2)}, u32[]{:S(2)}) collective-permute-start(bf16[4,960,384]{2,1,0:T(8,128)(2,1)} %get-tuple-element.249), channel_id=1, source_target_pairs={{0,4},{4,0},{8,12},{12,8},{16,20},{20,16},{24,28},{28,24},{1,5},{5... | collective-permute-start | bytes 8847368 | tf_op jit(solution)/shard_map/ppermute | solution.py:643
  94.0 15.5 %collective-permute-start.7 = (bf16[2,192,768]{2,1,0:T(8,128)(2,1)S(1)}, bf16[2,192,768]{2,1,0:T(8,128)(2,1)S(1)}, u32[]{:S(2)}, u32[]{:S(2)}) collective-permute-start(bf16[2,192,768]{2,1,0:T(8,128)(2,1)S(1)} %get-tuple-element.247), channel_id=1, source_target_pairs={{0,1},{1,0},{2,3},{3,2},{4,5},{5,4},{6,7},{7,6},{8,9},{9,8},{10,11... | collective-permute-start | bytes 1769480 | tf_op jit(solution)/shard_map/ppermute | solution.py:640
  95.3 14.2 %collective-permute-start.8 = (bf16[2,192,768]{2,1,0:T(8,128)(2,1)S(1)}, bf16[2,192,768]{2,1,0:T(8,128)(2,1)S(1)}, u32[]{:S(2)}, u32[]{:S(2)}) collective-permute-start(bf16[2,192,768]{2,1,0:T(8,128)(2,1)S(1)} %get-tuple-element.248), channel_id=1, source_target_pairs={{0,2},{1,3},{2,0},{3,1},{4,6},{5,7},{6,4},{7,5},{8,10},{9,11},{10,... | collective-permute-start | bytes 1769480 | tf_op jit(solution)/shard_map/ppermute | solution.py:640
  95.6 14.8 %copy-start.1 = (bf16[4,960,384]{2,1,0:T(8,128)(2,1)S(1)}, bf16[4,960,384]{2,1,0:T(8,128)(2,1)}, u32[]{:S(2)}) copy-start(bf16[4,960,384]{2,1,0:T(8,128)(2,1)} %get-tuple-element.266.refs_0_.refs_1_.refs_2_.refs_3_) | copy-start | bytes 8847364
  111.7 24.5 %collective-permute-start.12 = (bf16[2,480,384]{2,1,0:T(8,128)(2,1)S(1)}, bf16[2,480,384]{2,1,0:T(8,128)(2,1)S(1)}, u32[]{:S(2)}, u32[]{:S(2)}) collective-permute-start(bf16[2,480,384]{2,1,0:T(8,128)(2,1)S(1)} %get-tuple-element.270), channel_id=1, source_target_pairs={{0,1},{1,0},{2,3},{3,2},{4,5},{5,4},{6,7},{7,6},{8,9},{9,8},{10,11... | collective-permute-start | bytes 2211848 | tf_op jit(solution)/shard_map/ppermute | solution.py:640
  113.2 23.1 %collective-permute-start.13 = (bf16[2,480,384]{2,1,0:T(8,128)(2,1)S(1)}, bf16[2,480,384]{2,1,0:T(8,128)(2,1)S(1)}, u32[]{:S(2)}, u32[]{:S(2)}) collective-permute-start(bf16[2,480,384]{2,1,0:T(8,128)(2,1)S(1)} %get-tuple-element.271), channel_id=1, source_target_pairs={{0,2},{1,3},{2,0},{3,1},{4,6},{5,7},{6,4},{7,5},{8,10},{9,11},{10,... | collective-permute-start | bytes 2211848 | tf_op jit(solution)/shard_map/ppermute | solution.py:640
  113.4 22.8 %collective-permute-start.10 = (bf16[192,768]{1,0:T(8,128)(2,1)S(1)}, bf16[192,768]{1,0:T(8,128)(2,1)S(1)}, u32[]{:S(2)}, u32[]{:S(2)}) collective-permute-start(bf16[192,768]{1,0:T(8,128)(2,1)S(1)} %get-tuple-element.264), channel_id=1, source_target_pairs={{0,2},{1,3},{2,0},{3,1},{4,6},{5,7},{6,4},{7,5},{8,10},{9,11},{10,... | collective-permute-start | bytes 884744 | tf_op jit(solution)/shard_map/ppermute | solution.py:640
  114.6 21.6 %collective-permute-start.11 = (bf16[192,768]{1,0:T(8,128)(2,1)S(1)}, bf16[192,768]{1,0:T(8,128)(2,1)S(1)}, u32[]{:S(2)}, u32[]{:S(2)}) collective-permute-start(bf16[192,768]{1,0:T(8,128)(2,1)S(1)} %get-tuple-element.265), channel_id=1, source_target_pairs={{0,1},{1,0},{2,3},{3,2},{4,5},{5,4},{6,7},{7,6},{8,9},{9,8},{10,11... | collective-permute-start | bytes 884744 | tf_op jit(solution)/shard_map/ppermute | solution.py:640
  114.7 13.3 %copy-start.10 = (f32[16,768]{1,0:T(8,128)S(1)}, f32[16,768]{1,0:T(8,128)}, u32[]{:S(2)}) copy-start(f32[16,768]{1,0:T(8,128)} %get-tuple-element.286.mlp_sums) | copy-start | bytes 147460
  114.7 13.3 %copy-start.11 = (f32[16,768]{1,0:T(8,128)S(1)}, f32[16,768]{1,0:T(8,128)}, u32[]{:S(2)}) copy-start(f32[16,768]{1,0:T(8,128)} %get-tuple-element.287.refs_0_) | copy-start | bytes 147460
  136.2 14.1 %collective-permute-start.14 = (bf16[4,320,768]{2,1,0:T(8,128)(2,1)S(1)}, bf16[4,320,768]{2,1,0:T(8,128)(2,1)S(1)}, u32[]{:S(2)}, u32[]{:S(2)}) collective-permute-start(bf16[4,320,768]{2,1,0:T(8,128)(2,1)S(1)} %get-tuple-element.292), channel_id=1, source_target_pairs={{0,4},{4,0},{8,12},{12,8},{16,20},{20,16},{24,28},{28,24},{1,5},{5... | collective-permute-start | bytes 5898248 | tf_op jit(solution)/shard_map/ppermute | solution.py:643
  139.8 10.5 %collective-permute-start.15 = (bf16[480,384]{1,0:T(8,128)(2,1)S(1)}, bf16[480,384]{1,0:T(8,128)(2,1)S(1)}, u32[]{:S(2)}, u32[]{:S(2)}) collective-permute-start(bf16[480,384]{1,0:T(8,128)(2,1)S(1)} %get-tuple-element.298), channel_id=1, source_target_pairs={{0,2},{1,3},{2,0},{3,1},{4,6},{5,7},{6,4},{7,5},{8,10},{9,11},{10,... | collective-permute-start | bytes 1105928 | tf_op jit(solution)/shard_map/ppermute | solution.py:640
  140.5 9.9 %collective-permute-start.16 = (bf16[480,384]{1,0:T(8,128)(2,1)S(1)}, bf16[480,384]{1,0:T(8,128)(2,1)S(1)}, u32[]{:S(2)}, u32[]{:S(2)}) collective-permute-start(bf16[480,384]{1,0:T(8,128)(2,1)S(1)} %get-tuple-element.299), channel_id=1, source_target_pairs={{0,1},{1,0},{2,3},{3,2},{4,5},{5,4},{6,7},{7,6},{8,9},{9,8},{10,11... | collective-permute-start | bytes 1105928 | tf_op jit(solution)/shard_map/ppermute | solution.py:640
  142.3 8.0 %collective-permute-start.17 = (bf16[192,768]{1,0:T(8,128)(2,1)S(1)}, bf16[192,768]{1,0:T(8,128)(2,1)S(1)}, u32[]{:S(2)}, u32[]{:S(2)}) collective-permute-start(bf16[192,768]{1,0:T(8,128)(2,1)S(1)} %get-tuple-element.306), channel_id=1, source_target_pairs={{0,8},{4,12},{8,0},{12,4},{16,24},{20,28},{24,16},{28,20},{1,9},{5... | collective-permute-start | bytes 884744 | tf_op jit(solution)/shard_map/ppermute | solution.py:650
  151.7 11.4 %collective-permute-start.18 = (bf16[2,160,768]{2,1,0:T(8,128)(2,1)S(1)}, bf16[2,160,768]{2,1,0:T(8,128)(2,1)S(1)}, u32[]{:S(2)}, u32[]{:S(2)}) collective-permute-start(bf16[2,160,768]{2,1,0:T(8,128)(2,1)S(1)} %get-tuple-element.314), channel_id=1, source_target_pairs={{0,1},{1,0},{2,3},{3,2},{4,5},{5,4},{6,7},{7,6},{8,9},{9,8},{10,11... | collective-permute-start | bytes 1474568 | tf_op jit(solution)/shard_map/ppermute | solution.py:640
  152.8 11.3 %collective-permute-start.19 = (bf16[2,160,768]{2,1,0:T(8,128)(2,1)S(1)}, bf16[2,160,768]{2,1,0:T(8,128)(2,1)S(1)}, u32[]{:S(2)}, u32[]{:S(2)}) collective-permute-start(bf16[2,160,768]{2,1,0:T(8,128)(2,1)S(1)} %get-tuple-element.315), channel_id=1, source_target_pairs={{0,2},{1,3},{2,0},{3,1},{4,6},{5,7},{6,4},{7,5},{8,10},{9,11},{10,... | collective-permute-start | bytes 1474568 | tf_op jit(solution)/shard_map/ppermute | solution.py:640
  153.5 13.0 %copy-start.29 = (bf16[4,64,768]{2,1,0:T(8,128)(2,1)S(1)}, bf16[4,64,768]{2,1,0:T(8,128)(2,1)}, u32[]{:S(2)}) copy-start(bf16[4,64,768]{2,1,0:T(8,128)(2,1)} %get-tuple-element.358) | copy-start | bytes 1179652
  153.5 13.9 %copy-start.28 = (bf16[4,64,768]{2,1,0:T(8,128)(2,1)S(1)}, bf16[4,64,768]{2,1,0:T(8,128)(2,1)}, u32[]{:S(2)}) copy-start(bf16[4,64,768]{2,1,0:T(8,128)(2,1)} %get-tuple-element.359) | copy-start | bytes 1179652
  153.5 16.5 %copy-start.27 = (bf16[4,64,768]{2,1,0:T(8,128)(2,1)S(1)}, bf16[4,64,768]{2,1,0:T(8,128)(2,1)}, u32[]{:S(2)}) copy-start(bf16[4,64,768]{2,1,0:T(8,128)(2,1)} %get-tuple-element.360) | copy-start | bytes 1179652
  154.3 8.5 %collective-permute-start.20 = (bf16[480,384]{1,0:T(8,128)(2,1)S(1)}, bf16[480,384]{1,0:T(8,128)(2,1)S(1)}, u32[]{:S(2)}, u32[]{:S(2)}) collective-permute-start(bf16[480,384]{1,0:T(8,128)(2,1)S(1)} %get-tuple-element.324), channel_id=1, source_target_pairs={{0,8},{4,12},{8,0},{12,4},{16,24},{20,28},{24,16},{28,20},{1,9},{5... | collective-permute-start | bytes 1105928 | tf_op jit(solution)/shard_map/ppermute | solution.py:650
  155.7 11.7 %collective-permute-start.23 = (bf16[192,768]{1,0:T(8,128)(2,1)S(1)}, bf16[192,768]{1,0:T(8,128)(2,1)S(1)}, u32[]{:S(2)}, u32[]{:S(2)}) collective-permute-start(bf16[192,768]{1,0:T(8,128)(2,1)S(1)} %add_convert_fusion.3), channel_id=1, source_target_pairs={{0,24},{4,28},{8,16},{12,20},{16,8},{20,12},{24,0},{28,4},{1,25},{... | collective-permute-start | bytes 884744 | tf_op jit(solution)/shard_map/ppermute | solution.py:650
  164.1 24.4 %copy-start.13 = (bf16[4,64,768]{2,1,0:T(8,128)(2,1)S(1)}, bf16[4,64,768]{2,1,0:T(8,128)(2,1)}, u32[]{:S(2)}) copy-start(bf16[4,64,768]{2,1,0:T(8,128)(2,1)} %get-tuple-element.361) | copy-start | bytes 1179652
  164.1 26.1 %copy-start.14 = (bf16[4,64,768]{2,1,0:T(8,128)(2,1)S(1)}, bf16[4,64,768]{2,1,0:T(8,128)(2,1)}, u32[]{:S(2)}) copy-start(bf16[4,64,768]{2,1,0:T(8,128)(2,1)} %get-tuple-element.362) | copy-start | bytes 1179652
  164.1 26.7 %copy-start.15 = (bf16[4,64,768]{2,1,0:T(8,128)(2,1)S(1)}, bf16[4,64,768]{2,1,0:T(8,128)(2,1)}, u32[]{:S(2)}) copy-start(bf16[4,64,768]{2,1,0:T(8,128)(2,1)} %get-tuple-element.363) | copy-start | bytes 1179652
  164.9 5.1 %collective-permute-start.21 = (bf16[160,768]{1,0:T(8,128)(2,1)S(1)}, bf16[160,768]{1,0:T(8,128)(2,1)S(1)}, u32[]{:S(2)}, u32[]{:S(2)}) collective-permute-start(bf16[160,768]{1,0:T(8,128)(2,1)S(1)} %get-tuple-element.334), channel_id=1, source_target_pairs={{0,2},{1,3},{2,0},{3,1},{4,6},{5,7},{6,4},{7,5},{8,10},{9,11},{10,... | collective-permute-start | bytes 737288 | tf_op jit(solution)/shard_map/ppermute | solution.py:640
  165.6 5.4 %collective-permute-start.22 = (bf16[160,768]{1,0:T(8,128)(2,1)S(1)}, bf16[160,768]{1,0:T(8,128)(2,1)S(1)}, u32[]{:S(2)}, u32[]{:S(2)}) collective-permute-start(bf16[160,768]{1,0:T(8,128)(2,1)S(1)} %get-tuple-element.335), channel_id=1, source_target_pairs={{0,1},{1,0},{2,3},{3,2},{4,5},{5,4},{6,7},{7,6},{8,9},{9,8},{10,11... | collective-permute-start | bytes 737288 | tf_op jit(solution)/shard_map/ppermute | solution.py:640
  166.3 50.2 %copy-start.6 = (bf16[4,64,768]{2,1,0:T(8,128)(2,1)S(1)}, bf16[4,64,768]{2,1,0:T(8,128)(2,1)}, u32[]{:S(2)}) copy-start(bf16[4,64,768]{2,1,0:T(8,128)(2,1)} %get-tuple-element.372.refs_0_) | copy-start | bytes 1179652
  166.3 19.7 %collective-permute-start.25 = (bf16[480,384]{1,0:T(8,128)(2,1)S(1)}, bf16[480,384]{1,0:T(8,128)(2,1)S(1)}, u32[]{:S(2)}, u32[]{:S(2)}) collective-permute-start(bf16[480,384]{1,0:T(8,128)(2,1)S(1)} %add_convert_fusion.1), channel_id=1, source_target_pairs={{0,24},{4,28},{8,16},{12,20},{16,8},{20,12},{24,0},{28,4},{1,25},{... | collective-permute-start | bytes 1105928 | tf_op jit(solution)/shard_map/ppermute | solution.py:650
  166.6 22.0 %collective-permute-start.29 = (bf16[4,64,768]{2,1,0:T(8,128)(2,1)S(1)}, bf16[4,64,768]{2,1,0:T(8,128)(2,1)S(1)}, u32[]{:S(2)}, u32[]{:S(2)}) collective-permute-start(bf16[4,64,768]{2,1,0:T(8,128)(2,1)S(1)} %copy-done.29), channel_id=1, source_target_pairs={{0,1},{1,0},{2,3},{3,2},{4,5},{5,4},{6,7},{7,6},{8,9},{9,8},{10,11... | collective-permute-start | bytes 1179656 | tf_op jit(solution)/shard_map/ppermute | solution.py:640
  167.4 22.8 %collective-permute-start.30 = (bf16[4,64,768]{2,1,0:T(8,128)(2,1)S(1)}, bf16[4,64,768]{2,1,0:T(8,128)(2,1)S(1)}, u32[]{:S(2)}, u32[]{:S(2)}) collective-permute-start(bf16[4,64,768]{2,1,0:T(8,128)(2,1)S(1)} %copy-done.28), channel_id=1, source_target_pairs={{0,2},{1,3},{2,0},{3,1},{4,6},{5,7},{6,4},{7,5},{8,10},{9,11},{10,... | collective-permute-start | bytes 1179656 | tf_op jit(solution)/shard_map/ppermute | solution.py:640
  170.0 20.8 %collective-permute-start.31 = (bf16[4,64,768]{2,1,0:T(8,128)(2,1)S(1)}, bf16[4,64,768]{2,1,0:T(8,128)(2,1)S(1)}, u32[]{:S(2)}, u32[]{:S(2)}) collective-permute-start(bf16[4,64,768]{2,1,0:T(8,128)(2,1)S(1)} %copy-done.27), channel_id=1, source_target_pairs={{0,3},{1,2},{2,1},{3,0},{4,7},{5,6},{6,5},{7,4},{8,11},{9,10},{10,... | collective-permute-start | bytes 1179656 | tf_op jit(solution)/shard_map/ppermute | solution.py:640
  171.7 15.8 %collective-permute-start.24 = (bf16[160,768]{1,0:T(8,128)(2,1)S(1)}, bf16[160,768]{1,0:T(8,128)(2,1)S(1)}, u32[]{:S(2)}, u32[]{:S(2)}) collective-permute-start(bf16[160,768]{1,0:T(8,128)(2,1)S(1)} %get-tuple-element.347), channel_id=1, source_target_pairs={{0,8},{4,12},{8,0},{12,4},{16,24},{20,28},{24,16},{28,20},{1,9},{5... | collective-permute-start | bytes 737288 | tf_op jit(solution)/shard_map/ppermute | solution.py:650
  186.0 5.6 %collective-permute-start.28 = (bf16[192,768]{1,0:T(8,128)(2,1)S(1)}, bf16[192,768]{1,0:T(8,128)(2,1)S(1)}, u32[]{:S(2)}, u32[]{:S(2)}) collective-permute-start(bf16[192,768]{1,0:T(8,128)(2,1)S(1)} %add_convert_fusion.2.refs_0_), channel_id=1, source_target_pairs={{0,4},{4,0},{8,12},{12,8},{16,20},{20,16},{24,28},{28,24},{1,5},{5... | collective-permute-start | bytes 884744 | tf_op jit(solution)/shard_map/ppermute | solution.py:643
  187.4 5.7 %collective-permute-start.27 = (bf16[192,768]{1,0:T(8,128)(2,1)S(1)}, bf16[192,768]{1,0:T(8,128)(2,1)S(1)}, u32[]{:S(2)}, u32[]{:S(2)}) collective-permute-start(bf16[192,768]{1,0:T(8,128)(2,1)S(1)} %add_convert_fusion.2.refs_0_), channel_id=1, source_target_pairs={{0,8},{4,12},{8,0},{12,4},{16,24},{20,28},{24,16},{28,20},{1,9},{5... | collective-permute-start | bytes 884744 | tf_op jit(solution)/shard_map/ppermute | solution.py:650
  188.6 12.2 %collective-permute-start.32 = (bf16[4,64,768]{2,1,0:T(8,128)(2,1)S(1)}, bf16[4,64,768]{2,1,0:T(8,128)(2,1)S(1)}, u32[]{:S(2)}, u32[]{:S(2)}) collective-permute-start(bf16[4,64,768]{2,1,0:T(8,128)(2,1)S(1)} %copy-done.13), channel_id=1, source_target_pairs={{0,1},{1,0},{2,3},{3,2},{4,5},{5,4},{6,7},{7,6},{8,9},{9,8},{10,11... | collective-permute-start | bytes 1179656 | tf_op jit(solution)/shard_map/ppermute | solution.py:640
  190.2 14.7 %collective-permute-start.33 = (bf16[4,64,768]{2,1,0:T(8,128)(2,1)S(1)}, bf16[4,64,768]{2,1,0:T(8,128)(2,1)S(1)}, u32[]{:S(2)}, u32[]{:S(2)}) collective-permute-start(bf16[4,64,768]{2,1,0:T(8,128)(2,1)S(1)} %copy-done.14), channel_id=1, source_target_pairs={{0,2},{1,3},{2,0},{3,1},{4,6},{5,7},{6,4},{7,5},{8,10},{9,11},{10,... | collective-permute-start | bytes 1179656 | tf_op jit(solution)/shard_map/ppermute | solution.py:640
  190.8 14.1 %collective-permute-start.34 = (bf16[4,64,768]{2,1,0:T(8,128)(2,1)S(1)}, bf16[4,64,768]{2,1,0:T(8,128)(2,1)S(1)}, u32[]{:S(2)}, u32[]{:S(2)}) collective-permute-start(bf16[4,64,768]{2,1,0:T(8,128)(2,1)S(1)} %copy-done.15), channel_id=1, source_target_pairs={{0,3},{1,2},{2,1},{3,0},{4,7},{5,6},{6,5},{7,4},{8,11},{9,10},{10,... | collective-permute-start | bytes 1179656 | tf_op jit(solution)/shard_map/ppermute | solution.py:640
  191.6 27.2 %copy-start.3 = (bf16[4,64,768]{2,1,0:T(8,128)(2,1)S(1)}, bf16[4,64,768]{2,1,0:T(8,128)(2,1)}, u32[]{:S(2)}) copy-start(bf16[4,64,768]{2,1,0:T(8,128)(2,1)} %get-tuple-element.384.refs_0_) | copy-start | bytes 1179652
  191.6 13.4 %collective-permute-start.26 = (bf16[160,768]{1,0:T(8,128)(2,1)S(1)}, bf16[160,768]{1,0:T(8,128)(2,1)S(1)}, u32[]{:S(2)}, u32[]{:S(2)}) collective-permute-start(bf16[160,768]{1,0:T(8,128)(2,1)S(1)} %add_convert_fusion.5), channel_id=1, source_target_pairs={{0,24},{4,28},{8,16},{12,20},{16,8},{20,12},{24,0},{28,4},{1,25},{... | collective-permute-start | bytes 737288 | tf_op jit(solution)/shard_map/ppermute | solution.py:650
  193.2 11.8 %collective-permute-start.38 = (bf16[480,384]{1,0:T(8,128)(2,1)S(1)}, bf16[480,384]{1,0:T(8,128)(2,1)S(1)}, u32[]{:S(2)}, u32[]{:S(2)}) collective-permute-start(bf16[480,384]{1,0:T(8,128)(2,1)S(1)} %add_convert_fusion.refs_0_), channel_id=1, source_target_pairs={{0,4},{4,0},{8,12},{12,8},{16,20},{20,16},{24,28},{28,24},{1,5},{5... | collective-permute-start | bytes 1105928 | tf_op jit(solution)/shard_map/ppermute | solution.py:643
  200.8 11.8 %collective-permute-start.37 = (bf16[480,384]{1,0:T(8,128)(2,1)S(1)}, bf16[480,384]{1,0:T(8,128)(2,1)S(1)}, u32[]{:S(2)}, u32[]{:S(2)}) collective-permute-start(bf16[480,384]{1,0:T(8,128)(2,1)S(1)} %add_convert_fusion.refs_0_), channel_id=1, source_target_pairs={{0,8},{4,12},{8,0},{12,4},{16,24},{20,28},{24,16},{28,20},{1,9},{5... | collective-permute-start | bytes 1105928 | tf_op jit(solution)/shard_map/ppermute | solution.py:650
  212.6 11.0 %collective-permute-start.39 = (bf16[480,384]{1,0:T(8,128)(2,1)S(1)}, bf16[480,384]{1,0:T(8,128)(2,1)S(1)}, u32[]{:S(2)}, u32[]{:S(2)}) collective-permute-start(bf16[480,384]{1,0:T(8,128)(2,1)S(1)} %collective-permute-done.37.refs_1_), channel_id=1, source_target_pairs={{0,4},{4,0},{8,12},{12,8},{16,20},{20,16},{24,28},{28,24},{1,5},{5... | collective-permute-start | bytes 1105928 | tf_op jit(solution)/shard_map/ppermute | solution.py:643
  214.5 7.0 %collective-permute-start.40 = (bf16[192,768]{1,0:T(8,128)(2,1)S(1)}, bf16[192,768]{1,0:T(8,128)(2,1)S(1)}, u32[]{:S(2)}, u32[]{:S(2)}) collective-permute-start(bf16[192,768]{1,0:T(8,128)(2,1)S(1)} %collective-permute-done.27.refs_1_), channel_id=1, source_target_pairs={{0,4},{4,0},{8,12},{12,8},{16,20},{20,16},{24,28},{28,24},{1,5},{5... | collective-permute-start | bytes 884744 | tf_op jit(solution)/shard_map/ppermute | solution.py:643
  214.5 9.1 %collective-permute-start.36 = (bf16[160,768]{1,0:T(8,128)(2,1)S(1)}, bf16[160,768]{1,0:T(8,128)(2,1)S(1)}, u32[]{:S(2)}, u32[]{:S(2)}) collective-permute-start(bf16[160,768]{1,0:T(8,128)(2,1)S(1)} %add_convert_fusion.4.refs_0_), channel_id=1, source_target_pairs={{0,4},{4,0},{8,12},{12,8},{16,20},{20,16},{24,28},{28,24},{1,5},{5... | collective-permute-start | bytes 737288 | tf_op jit(solution)/shard_map/ppermute | solution.py:643
  215.0 8.6 %collective-permute-start.35 = (bf16[160,768]{1,0:T(8,128)(2,1)S(1)}, bf16[160,768]{1,0:T(8,128)(2,1)S(1)}, u32[]{:S(2)}, u32[]{:S(2)}) collective-permute-start(bf16[160,768]{1,0:T(8,128)(2,1)S(1)} %add_convert_fusion.4.refs_0_), channel_id=1, source_target_pairs={{0,8},{4,12},{8,0},{12,4},{16,24},{20,28},{24,16},{28,20},{1,9},{5... | collective-permute-start | bytes 737288 | tf_op jit(solution)/shard_map/ppermute | solution.py:650
  223.6 2.8 %collective-permute-start.41 = (bf16[160,768]{1,0:T(8,128)(2,1)S(1)}, bf16[160,768]{1,0:T(8,128)(2,1)S(1)}, u32[]{:S(2)}, u32[]{:S(2)}) collective-permute-start(bf16[160,768]{1,0:T(8,128)(2,1)S(1)} %collective-permute-done.35.refs_1_), channel_id=1, source_target_pairs={{0,4},{4,0},{8,12},{12,8},{16,20},{20,16},{24,28},{28,24},{1,5},{5... | collective-permute-start | bytes 737288 | tf_op jit(solution)/shard_map/ppermute | solution.py:643
  (8 other events, 27.9 us)

commit v3 on v2

--- a/solution.py
+++ b/solution.py
@@ -705,12 +705,11 @@
 
 
 def qkv_kernel(info, gproj_t, normed_n, mlp_sums, *refs):
-    *att, keep, send, total, vectors = refs
+    *att, keep, send, vectors = refs
     c = pl.program_id(0)
     model = mlp_sums.shape[1]
-    rows = total.shape[0] // 2
+    rows = gproj_t.shape[0] // 2
     part = model // 4
-    total[...] = dot(gproj_t[...], normed_n[...])
 
     for i in range(4):
 
@@ -728,7 +727,8 @@
 
     for side, target in enumerate((keep, send)):
         which = lax.bitwise_xor(info[1], side)
-        target[0, :rows] = total[pl.ds(pl.multiple_of(which * rows, rows), rows), :].astype(BF16)
+        half = gproj_t[pl.ds(pl.multiple_of(which * rows, rows), rows), :]
+        target[0, :rows] = dot(half, normed_n[...]).astype(BF16)
         target[0, rows:] = vectors[which].astype(BF16)
 
 
@@ -749,7 +749,7 @@
             in_specs=[pl.BlockSpec((rows, gproj_t.shape[1]), lambda c, info: (c, 0))]
             + [whole(o.shape) for o in others],
             out_specs=[pl.BlockSpec(block, lambda c, info: (c, 0, 0))] * 2,
-            scratch_shapes=[pltpu.VMEM((rows, model), F32), pltpu.VMEM((2, VECTOR_ROWS, model), F32)],
+            scratch_shapes=[pltpu.VMEM((2, VECTOR_ROWS, model), F32)],
         ),
         out_shape=[out, out],
         compiler_params=params(24),

time: 229 us -> 228 us (level)
  transfers between devices with their start and end apart: 42 -> 42, of which waited for: 12 -> 13; matrix products, arithmetic and copies ran while one was open for 1% -> 1% of each run, Pallas kernels for 30% -> 30%
where the time goes in v3:
time: 228 us
  Pallas kernels  120 us (53%)
  waiting for transfers between devices  56 us (25%)
  starting transfers between devices  47 us (21%)
  local copies, waits for them, and re-layouts  3.63 us (2%)
    pallas_call x1, Pallas kernels, mlp_call(): pl.pallas_call(functools.partial(mlp_kernel, ncol), grid_spec=pltpu.Prefe...  44.2 us
    ppermute x9, waiting for transfers between devices, z_swap(): lax.ppermute(array, 'clip', [(i, i ^ 2 * distance) for i in range(self.nc...  35.4 us
    pallas_call x2, Pallas kernels, attend_back_call(): pl.pallas_call(functools.partial(attend_back_kernel, ncol, block, first),...  27.2 us
    ppermute x24, starting transfers between devices, col_swap(): lax.ppermute(array, 'col', [(i, i ^ distance) for i in range(self.ncol)])  20.2 us
    ppermute x24, waiting for transfers between devices, col_swap(): lax.ppermute(array, 'col', [(i, i ^ distance) for i in range(self.ncol)])  16.3 us
    pallas_call x1, Pallas kernels, attend_call(): pl.pallas_call(functools.partial(attend_kernel, ncol, block, first), grid...  15.8 us
    ppermute x9, starting transfers between devices, core_swap(): return lax.ppermute(array, 'clip', [(i, i ^ 1) for i in range(self.nclip)])  15.4 us
    ppermute x9, starting transfers between devices, z_swap(): lax.ppermute(array, 'clip', [(i, i ^ 2 * distance) for i in range(self.nc...  11.5 us
  transfers between devices with their start and end apart: 42, of which 13 were waited for; matrix products, arithmetic and copies ran while one was open for 1% of the time, Pallas kernels for 30%

profile of v3, /device:TPU:17, one launch (start us, length us, event | category | flops | bytes accessed | tf_op | source)
XLA Modules:
  0.0 228.1 jit_solution(7502548189577300568)
XLA Ops:
  0.8 2.8 %take_frames.2 = (bf16[4,64,768]{2,1,0:T(8,128)(2,1)}, bf16[4,64,768]{2,1,0:T(8,128)(2,1)}, bf16[4,64,768]{2,1,0:T(8,128)(2,1)}) custom-call(s32[5]{0:T(128)S(1)} %stack.27.info, bf16[16,64,768]{2,1,0:T(8,128)(2,1)} %refs_0_.11, bf16[16,64,768]{2,1,0:T(8,128)(2,1)} %refs_0_.11, bf16[16,64,768]{2,1,0:T(8,128)(2,1)} %refs_0_.11), custom_call_target="tpu_custom_call" | custom-call | bytes 1500000 | tf_op jit(solution)/shard_map/take_frames/pallas_call | solution.py:584
  3.7 1.2 collective-permute-start
  4.9 1.2 collective-permute-start.1
  7.3 2.8 %take_frames.3 = (bf16[4,64,768]{2,1,0:T(8,128)(2,1)}, bf16[4,64,768]{2,1,0:T(8,128)(2,1)}, bf16[4,64,768]{2,1,0:T(8,128)(2,1)}) custom-call(s32[5]{0:T(128)S(1)} %stack.27.info, bf16[16,64,768]{2,1,0:T(8,128)(2,1)} %refs_0_.9, bf16[16,64,768]{2,1,0:T(8,128)(2,1)} %refs_0_.9, bf16[16,64,768]{2,1,0:T(8,128)(2,1)} %refs_0_.9), custom_call_target="tpu_custom_call" | custom-call | bytes 1500000 | tf_op jit(solution)/shard_map/take_frames/pallas_call | solution.py:584
  10.1 3.8 %collective-permute-done.refs_1_ = bf16[4,64,768]{2,1,0:T(8,128)(2,1)S(1)} collective-permute-done((bf16[4,64,768]{2,1,0:T(8,128)(2,1)}, bf16[4,64,768]{2,1,0:T(8,128)(2,1)S(1)}, u32[]{:S(2)}, u32[]{:S(2)}) %collective-permute-start) | collective-permute-done | bytes 393248 | tf_op jit(solution)/shard_map/ppermute | solution.py:640
  13.9 1.2 collective-permute-start.3
  15.1 1.2 collective-permute-start.4
  16.7 6.6 %collective-permute-done.2.refs_3_ = bf16[4,64,768]{2,1,0:T(8,128)(2,1)S(1)} collective-permute-done((bf16[4,64,768]{2,1,0:T(8,128)(2,1)}, bf16[4,64,768]{2,1,0:T(8,128)(2,1)S(1)}, u32[]{:S(2)}, u32[]{:S(2)}) %collective-permute-start.2) | collective-permute-done | bytes 393248 | tf_op jit(solution)/shard_map/ppermute | solution.py:640
  23.3 15.8 %attend.1 = (bf16[2304,1024]{1,0:T(8,128)(2,1)}, bf16[768,1024]{1,0:T(8,128)(2,1)}, f32[1024,768]{1,0:T(8,128)}, f32[4,16,256]{2,1,0:T(8,128)}) custom-call(s32[5]{0:T(128)S(1)} %stack.27.info, s32[4]{0:T(128)S(1)} %dynamic-slice_bitcast_fusion.lens, bf16[16,64,768]{2,1,0:T(8,128)(2,1)S(1)} %copy-done, bf16[4,64,768]{2,1,0:T(8,128)(2,1)S(1)} %collective-permute-done.refs_1_, ...), custom_call_target="tpu_custom_call" | custom-call | bytes 15000000 | tf_op jit(solution)/shard_map/attend/pallas_call | solution.py:189
  39.1 2.5 %collective-permute-done.4.refs_2_ = bf16[4,64,768]{2,1,0:T(8,128)(2,1)} collective-permute-done((bf16[4,64,768]{2,1,0:T(8,128)(2,1)}, bf16[4,64,768]{2,1,0:T(8,128)(2,1)}, u32[]{:S(2)}, u32[]{:S(2)}) %collective-permute-start.4) | collective-permute-done | bytes 393248 | tf_op jit(solution)/shard_map/ppermute | solution.py:640
  41.5 44.2 %mlp.1 = (bf16[4,64,768]{2,1,0:T(8,128)(2,1)}, bf16[4,64,768]{2,1,0:T(8,128)(2,1)}, bf16[4,64,768]{2,1,0:T(8,128)(2,1)}, bf16[4,64,768]{2,1,0:T(8,128)(2,1)}, f3...) custom-call(s32[5]{0:T(128)} %copy-done.8, ...), custom_call_target="tpu_custom_call" | custom-call | bytes 60000000 | tf_op jit(solution)/shard_map/mlp/pallas_call | solution.py:375
  85.8 1.1 collective-permute-start.6
  86.9 4.3 %collective-permute-done.6.refs_4_.refs_5_.refs_6_.refs_7_ = bf16[4,384,768]{2,1,0:T(8,128)(2,1)S(1)} collective-permute-done((bf16[4,384,768]{2,1,0:T(8,128)(2,1)}, bf16[4,384,768]{2,1,0:T(8,128)(2,1)S(1)}, u32[]{:S(2)}, u32[]{:S(2)}) %collective-permute-start.6) | collective-permute-done | bytes 2359328 | tf_op jit(solution)/shard_map/ppermute | solution.py:643
  91.2 1.7 copy-done.2
  92.9 1.1 sum_core.3
  94.0 1.3 collective-permute-start.7
  95.6 13.9 %attend_back.2 = (bf16[2304,1024]{1,0:T(8,128)(2,1)}, bf16[1024,768]{1,0:T(8,128)(2,1)}, f32[16,768]{1,0:T(8,128)}, bf16[4,64,768]{2,1,0:T(8,128)(2,1)}, bf16[4,...) custom-call(s32[5]{0:T(128)S(1)} %copy-done.9, ...), custom_call_target="tpu_custom_call" | custom-call | bytes 22500000 | tf_op jit(solution)/shard_map/attend_back/pallas_call | solution.py:524
  109.6 0.8 sum_first.3
  110.4 1.3 sum_core.4
  111.7 1.5 collective-permute-start.12
  113.4 1.2 collective-permute-start.10
  114.7 13.3 %attend_back.3 = (bf16[2304,1024]{1,0:T(8,128)(2,1)}, bf16[1024,768]{1,0:T(8,128)(2,1)}, f32[16,768]{1,0:T(8,128)}, bf16[4,64,768]{2,1,0:T(8,128)(2,1)}, bf16[4,...) custom-call(s32[5]{0:T(128)S(1)} %copy-done.9, ...), custom_call_target="tpu_custom_call", output_to_operand_aliasing={{0}: (14, {}), {1}: (15, {}), {3}: (16, {}), {4}: (17, {}),... | custom-call | bytes 22500000 | tf_op jit(solution)/shard_map/attend_back/pallas_call | solution.py:524
  128.0 0.8 copy-done.12
  128.8 7.1 %grad_qkv.1 = (bf16[4,320,768]{2,1,0:T(8,128)(2,1)S(1)}, bf16[4,320,768]{2,1,0:T(8,128)(2,1)S(1)}) custom-call(s32[5]{0:T(128)S(1)} %copy-done.9, bf16[2304,1024]{1,0:T(8,128)(2,1)} %get-tuple-element.284.gproj_t, bf16[1024,768]{1,0:T(8,128)(2,1)} %get-tuple-element.285.normed_n, f32[16,768]{1,0:T(8,128)S(1)} %copy-done.10, f32[16,768]{1,0:T(8,128)S(1)} %copy-done.11, ...), custom_call_target="tpu_custom_call" | custom-call | bytes 9000000 | tf_op jit(solution)/shard_map/grad_qkv/pallas_call | solution.py:744
  136.2 2.4 %collective-permute-start.14 = (bf16[4,320,768]{2,1,0:T(8,128)(2,1)S(1)}, bf16[4,320,768]{2,1,0:T(8,128)(2,1)S(1)}, u32[]{:S(2)}, u32[]{:S(2)}) collective-permute-start(bf16[4,320,768]{2,1,0:T(8,128)(2,1)S(1)} %get-tuple-element.292), channel_id=1, source_target_pairs={{0,4},{4,0},{8,12},{12,8},{16,20},{20,16},{24,28},{28,24},{1,5},{5... | collective-permute-start | bytes 5898248 | tf_op jit(solution)/shard_map/ppermute | solution.py:643
  138.7 0.9 sum_first.4
  139.6 0.7 collective-permute-start.15
  140.2 1.1 collective-permute-start.16
  141.3 0.7 sum_second.3
  142.0 1.4 collective-permute-start.17
  143.4 6.7 %collective-permute-done.17 = bf16[192,768]{1,0:T(8,128)(2,1)S(1)} collective-permute-done((bf16[192,768]{1,0:T(8,128)(2,1)S(1)}, bf16[192,768]{1,0:T(8,128)(2,1)S(1)}, u32[]{:S(2)}, u32[]{:S(2)}) %collective-permute-start.17) | collective-permute-done | bytes 294944 | tf_op jit(solution)/shard_map/ppermute | solution.py:650
  150.1 1.3 sum_core.5
  151.4 1.1 collective-permute-start.18
  152.6 0.6 collective-permute-start.19
  153.3 0.8 sum_second.4
  154.1 1.4 collective-permute-start.20
  155.4 7.1 %collective-permute-done.20 = bf16[480,384]{1,0:T(8,128)(2,1)S(1)} collective-permute-done((bf16[480,384]{1,0:T(8,128)(2,1)S(1)}, bf16[480,384]{1,0:T(8,128)(2,1)S(1)}, u32[]{:S(2)}, u32[]{:S(2)}) %collective-permute-start.20) | collective-permute-done | bytes 368672 | tf_op jit(solution)/shard_map/ppermute | solution.py:650
  162.8 1.1 collective-permute-done.19.land_b
  163.9 0.8 sum_first.5
  164.7 0.7 collective-permute-start.21
  165.3 0.6 collective-permute-start.22
  166.3 0.9 collective-permute-start.29
  167.2 0.9 collective-permute-start.30
  168.0 1.8 collective-permute-done.21.land_a
  169.8 0.9 collective-permute-start.31
  170.7 0.7 sum_second.5
  171.4 1.7 collective-permute-start.24
  173.1 12.6 %collective-permute-done.25 = bf16[480,384]{1,0:T(8,128)(2,1)S(1)} collective-permute-done((bf16[480,384]{1,0:T(8,128)(2,1)S(1)}, bf16[480,384]{1,0:T(8,128)(2,1)S(1)}, u32[]{:S(2)}, u32[]{:S(2)}) %collective-permute-start.25) | collective-permute-done | bytes 368672 | tf_op jit(solution)/shard_map/ppermute | solution.py:650
  185.7 1.4 collective-permute-start.28
  187.2 1.1 collective-permute-start.27
  188.3 1.6 collective-permute-start.32
  190.0 0.6 collective-permute-start.33
  190.6 0.7 collective-permute-start.34
  191.5 1.4 collective-permute-done.27.refs_1_
  192.9 7.6 %collective-permute-start.38 = (bf16[480,384]{1,0:T(8,128)(2,1)S(1)}, bf16[480,384]{1,0:T(8,128)(2,1)S(1)}, u32[]{:S(2)}, u32[]{:S(2)}) collective-permute-start(bf16[480,384]{1,0:T(8,128)(2,1)S(1)} %add_convert_fusion.refs_0_), channel_id=1, source_target_pairs={{0,4},{4,0},{8,12},{12,8},{16,20},{20,16},{24,28},{28,24},{1,5},{5... | collective-permute-start | bytes 1105928 | tf_op jit(solution)/shard_map/ppermute | solution.py:643
  200.5 4.2 %collective-permute-start.37 = (bf16[480,384]{1,0:T(8,128)(2,1)S(1)}, bf16[480,384]{1,0:T(8,128)(2,1)S(1)}, u32[]{:S(2)}, u32[]{:S(2)}) collective-permute-start(bf16[480,384]{1,0:T(8,128)(2,1)S(1)} %add_convert_fusion.refs_0_), channel_id=1, source_target_pairs={{0,8},{4,12},{8,0},{12,4},{16,24},{20,28},{24,16},{28,20},{1,9},{5... | collective-permute-start | bytes 1105928 | tf_op jit(solution)/shard_map/ppermute | solution.py:650
  204.8 7.5 %collective-permute-done.37.refs_1_ = bf16[480,384]{1,0:T(8,128)(2,1)S(1)} collective-permute-done((bf16[480,384]{1,0:T(8,128)(2,1)S(1)}, bf16[480,384]{1,0:T(8,128)(2,1)S(1)}, u32[]{:S(2)}, u32[]{:S(2)}) %collective-permute-start.37) | collective-permute-done | bytes 368672 | tf_op jit(solution)/shard_map/ppermute | solution.py:650
  212.3 1.9 collective-permute-start.39
  214.7 1.5 collective-permute-start.35
  216.2 2.3 place_frames.2
  218.5 2.7 %place_frames.3 = f32[16,64,768]{2,1,0:T(8,128)} custom-call(s32[5]{0:T(128)S(1)} %copy-done.9, bf16[4,64,768]{2,1,0:T(8,128)(2,1)S(1)} %copy-done.3, bf16[4,64,768]{2,1,0:T(8,128)(2,1)S(1)} %collective-permute-done.32.refs_1_, bf16[4,64,768]{2,1,0:T(8,128)(2,1)S(1)} %collective-permute-done.33.refs_2_, bf16[4,64,768]{2,1,0:T(8,128)(2,1)S(1)} %collective-permute-done.34.refs_3_), custom_call_target="tpu_custom_call" | custom-call | bytes 3000000 | tf_op jit(solution)/shard_map/place_frames/pallas_call | solution.py:610
  221.2 2.2 finish_down.1
  223.7 2.4 %finish_up.1 = (f32[768,768]{1,0:T(8,128)}, f32[192,768]{1,0:T(8,128)}) custom-call(s32[5]{0:T(128)S(1)} %copy-done.9, bf16[480,384]{1,0:T(8,128)(2,1)S(1)} %add_convert_fusion.refs_0_, bf16[480,384]{1,0:T(8,128)(2,1)S(1)} %collective-permute-done.37.refs_1_, bf16[480,384]{1,0:T(8,128)(2,1)S(1)} %collective-permute-done.38.refs_2_, ...), custom_call_target="tpu_custom_call" | custom-call | bytes 3000000 | tf_op jit(solution)/shard_map/finish_up/pallas_call | solution.py:887
  226.2 1.9 finish_qkv.1
  (118 shorter events, 4.6 us)
Async XLA Ops:
  0.7 22.5 %copy-start.8 = (s32[5]{0:T(128)}, s32[5]{0:T(128)S(1)}, u32[]{:S(2)}) copy-start(s32[5]{0:T(128)S(1)} %stack.27.info) | copy-start | bytes 64
  0.8 6.3 %copy-start.17 = (bf16[3072]{0:T(1024)(128)(2,1)S(1)}, bf16[3072]{0:T(1024)(128)(2,1)}, u32[]{:S(2)}) copy-start(bf16[3072]{0:T(1024)(128)(2,1)} %param.29) | copy-start | bytes 18436
  0.8 6.3 %copy-start.18 = (bf16[1536]{0:T(1024)(128)(2,1)S(1)}, bf16[1536]{0:T(1024)(128)(2,1)}, u32[]{:S(2)}) copy-start(bf16[1536]{0:T(1024)(128)(2,1)} %param.23) | copy-start | bytes 9220
  0.8 6.3 %copy-start.19 = (bf16[768]{0:T(1024)(128)(2,1)S(1)}, bf16[768]{0:T(1024)(128)(2,1)}, u32[]{:S(2)}) copy-start(bf16[768]{0:T(1024)(128)(2,1)} %param.31) | copy-start | bytes 4612
  0.8 6.3 %copy-start.20 = (bf16[768]{0:T(1024)(128)(2,1)S(1)}, bf16[768]{0:T(1024)(128)(2,1)}, u32[]{:S(2)}) copy-start(bf16[768]{0:T(1024)(128)(2,1)} %param.27) | copy-start | bytes 4612
  0.8 6.3 %copy-start.21 = (bf16[768]{0:T(1024)(128)(2,1)S(1)}, bf16[768]{0:T(1024)(128)(2,1)}, u32[]{:S(2)}) copy-start(bf16[768]{0:T(1024)(128)(2,1)} %param.26) | copy-start | bytes 4612
  0.8 6.3 %copy-start.22 = (bf16[768]{0:T(1024)(128)(2,1)S(1)}, bf16[768]{0:T(1024)(128)(2,1)}, u32[]{:S(2)}) copy-start(bf16[768]{0:T(1024)(128)(2,1)} %param.25) | copy-start | bytes 4612
  0.8 6.3 %copy-start.23 = (bf16[768]{0:T(1024)(128)(2,1)S(1)}, bf16[768]{0:T(1024)(128)(2,1)}, u32[]{:S(2)}) copy-start(bf16[768]{0:T(1024)(128)(2,1)} %param.21) | copy-start | bytes 4612
  3.7 10.2 %collective-permute-start = (bf16[4,64,768]{2,1,0:T(8,128)(2,1)}, bf16[4,64,768]{2,1,0:T(8,128)(2,1)S(1)}, u32[]{:S(2)}, u32[]{:S(2)}) collective-permute-start(bf16[4,64,768]{2,1,0:T(8,128)(2,1)} %get-tuple-element.219), channel_id=1, source_target_pairs={{0,1},{1,0},{2,3},{3,2},{4,5},{5,4},{6,7},{7,6},{8,9},{9,8},{10,11... | collective-permute-start | bytes 1179656 | tf_op jit(solution)/shard_map/ppermute | solution.py:640
  4.9 11.8 %collective-permute-start.1 = (bf16[4,64,768]{2,1,0:T(8,128)(2,1)}, bf16[4,64,768]{2,1,0:T(8,128)(2,1)S(1)}, u32[]{:S(2)}, u32[]{:S(2)}) collective-permute-start(bf16[4,64,768]{2,1,0:T(8,128)(2,1)} %get-tuple-element.225), channel_id=1, source_target_pairs={{0,2},{1,3},{2,0},{3,1},{4,6},{5,7},{6,4},{7,5},{8,10},{9,11},{10,... | collective-permute-start | bytes 1179656 | tf_op jit(solution)/shard_map/ppermute | solution.py:640
  6.1 17.2 %collective-permute-start.2 = (bf16[4,64,768]{2,1,0:T(8,128)(2,1)}, bf16[4,64,768]{2,1,0:T(8,128)(2,1)S(1)}, u32[]{:S(2)}, u32[]{:S(2)}) collective-permute-start(bf16[4,64,768]{2,1,0:T(8,128)(2,1)} %get-tuple-element.226), channel_id=1, source_target_pairs={{0,3},{1,2},{2,1},{3,0},{4,7},{5,6},{6,5},{7,4},{8,11},{9,10},{10,... | collective-permute-start | bytes 1179656 | tf_op jit(solution)/shard_map/ppermute | solution.py:640
  7.3 16.0 %copy-start.4 = (f32[12,768]{1,0:T(8,128)}, f32[12,768]{1,0:T(8,128)S(1)}, u32[]{:S(2)}) copy-start(f32[12,768]{1,0:T(8,128)S(1)} %reshape.58.refs_5_.refs_6_) | copy-start | bytes 110596
  7.3 16.0 %copy-start = (bf16[16,64,768]{2,1,0:T(8,128)(2,1)S(1)}, bf16[16,64,768]{2,1,0:T(8,128)(2,1)}, u32[]{:S(2)}) copy-start(bf16[16,64,768]{2,1,0:T(8,128)(2,1)} %refs_0_.11) | copy-start | bytes 4718596
  13.9 25.2 %collective-permute-start.3 = (bf16[4,64,768]{2,1,0:T(8,128)(2,1)}, bf16[4,64,768]{2,1,0:T(8,128)(2,1)S(1)}, u32[]{:S(2)}, u32[]{:S(2)}) collective-permute-start(bf16[4,64,768]{2,1,0:T(8,128)(2,1)} %get-tuple-element.236), channel_id=1, source_target_pairs={{0,1},{1,0},{2,3},{3,2},{4,5},{5,4},{6,7},{7,6},{8,9},{9,8},{10,11... | collective-permute-start | bytes 1179656 | tf_op jit(solution)/shard_map/ppermute | solution.py:640
  15.1 26.4 %collective-permute-start.4 = (bf16[4,64,768]{2,1,0:T(8,128)(2,1)}, bf16[4,64,768]{2,1,0:T(8,128)(2,1)}, u32[]{:S(2)}, u32[]{:S(2)}) collective-permute-start(bf16[4,64,768]{2,1,0:T(8,128)(2,1)} %get-tuple-element.237), channel_id=1, source_target_pairs={{0,2},{1,3},{2,0},{3,1},{4,6},{5,7},{6,4},{7,5},{8,10},{9,11},{10,... | collective-permute-start | bytes 1179656 | tf_op jit(solution)/shard_map/ppermute | solution.py:640
  16.3 25.2 %collective-permute-start.5 = (bf16[4,64,768]{2,1,0:T(8,128)(2,1)}, bf16[4,64,768]{2,1,0:T(8,128)(2,1)}, u32[]{:S(2)}, u32[]{:S(2)}) collective-permute-start(bf16[4,64,768]{2,1,0:T(8,128)(2,1)} %get-tuple-element.238), channel_id=1, source_target_pairs={{0,3},{1,2},{2,1},{3,0},{4,7},{5,6},{6,5},{7,4},{8,11},{9,10},{10,... | collective-permute-start | bytes 1179656 | tf_op jit(solution)/shard_map/ppermute | solution.py:640
  41.5 49.7 %copy-start.9 = (s32[5]{0:T(128)S(1)}, s32[5]{0:T(128)}, u32[]{:S(2)}) copy-start(s32[5]{0:T(128)} %copy-done.8) | copy-start | bytes 64
  85.8 5.5 %collective-permute-start.6 = (bf16[4,384,768]{2,1,0:T(8,128)(2,1)}, bf16[4,384,768]{2,1,0:T(8,128)(2,1)S(1)}, u32[]{:S(2)}, u32[]{:S(2)}) collective-permute-start(bf16[4,384,768]{2,1,0:T(8,128)(2,1)} %get-tuple-element.245), channel_id=1, source_target_pairs={{0,4},{4,0},{8,12},{12,8},{16,20},{20,16},{24,28},{28,24},{1,5},{5... | collective-permute-start | bytes 7077896 | tf_op jit(solution)/shard_map/ppermute | solution.py:643
  86.9 22.7 %collective-permute-start.9 = (bf16[4,960,384]{2,1,0:T(8,128)(2,1)}, bf16[4,960,384]{2,1,0:T(8,128)(2,1)S(1)}, u32[]{:S(2)}, u32[]{:S(2)}) collective-permute-start(bf16[4,960,384]{2,1,0:T(8,128)(2,1)} %get-tuple-element.249), channel_id=1, source_target_pairs={{0,4},{4,0},{8,12},{12,8},{16,20},{20,16},{24,28},{28,24},{1,5},{5... | collective-permute-start | bytes 8847368 | tf_op jit(solution)/shard_map/ppermute | solution.py:643
  94.0 15.5 %collective-permute-start.7 = (bf16[2,192,768]{2,1,0:T(8,128)(2,1)S(1)}, bf16[2,192,768]{2,1,0:T(8,128)(2,1)S(1)}, u32[]{:S(2)}, u32[]{:S(2)}) collective-permute-start(bf16[2,192,768]{2,1,0:T(8,128)(2,1)S(1)} %get-tuple-element.247), channel_id=1, source_target_pairs={{0,1},{1,0},{2,3},{3,2},{4,5},{5,4},{6,7},{7,6},{8,9},{9,8},{10,11... | collective-permute-start | bytes 1769480 | tf_op jit(solution)/shard_map/ppermute | solution.py:640
  95.3 14.2 %collective-permute-start.8 = (bf16[2,192,768]{2,1,0:T(8,128)(2,1)S(1)}, bf16[2,192,768]{2,1,0:T(8,128)(2,1)S(1)}, u32[]{:S(2)}, u32[]{:S(2)}) collective-permute-start(bf16[2,192,768]{2,1,0:T(8,128)(2,1)S(1)} %get-tuple-element.248), channel_id=1, source_target_pairs={{0,2},{1,3},{2,0},{3,1},{4,6},{5,7},{6,4},{7,5},{8,10},{9,11},{10,... | collective-permute-start | bytes 1769480 | tf_op jit(solution)/shard_map/ppermute | solution.py:640
  95.6 14.8 %copy-start.1 = (bf16[4,960,384]{2,1,0:T(8,128)(2,1)S(1)}, bf16[4,960,384]{2,1,0:T(8,128)(2,1)}, u32[]{:S(2)}) copy-start(bf16[4,960,384]{2,1,0:T(8,128)(2,1)} %get-tuple-element.266.refs_0_.refs_1_.refs_2_.refs_3_) | copy-start | bytes 8847364
  111.7 24.5 %collective-permute-start.12 = (bf16[2,480,384]{2,1,0:T(8,128)(2,1)S(1)}, bf16[2,480,384]{2,1,0:T(8,128)(2,1)S(1)}, u32[]{:S(2)}, u32[]{:S(2)}) collective-permute-start(bf16[2,480,384]{2,1,0:T(8,128)(2,1)S(1)} %get-tuple-element.270), channel_id=1, source_target_pairs={{0,1},{1,0},{2,3},{3,2},{4,5},{5,4},{6,7},{7,6},{8,9},{9,8},{10,11... | collective-permute-start | bytes 2211848 | tf_op jit(solution)/shard_map/ppermute | solution.py:640
  113.2 23.1 %collective-permute-start.13 = (bf16[2,480,384]{2,1,0:T(8,128)(2,1)S(1)}, bf16[2,480,384]{2,1,0:T(8,128)(2,1)S(1)}, u32[]{:S(2)}, u32[]{:S(2)}) collective-permute-start(bf16[2,480,384]{2,1,0:T(8,128)(2,1)S(1)} %get-tuple-element.271), channel_id=1, source_target_pairs={{0,2},{1,3},{2,0},{3,1},{4,6},{5,7},{6,4},{7,5},{8,10},{9,11},{10,... | collective-permute-start | bytes 2211848 | tf_op jit(solution)/shard_map/ppermute | solution.py:640
  113.4 22.8 %collective-permute-start.10 = (bf16[192,768]{1,0:T(8,128)(2,1)S(1)}, bf16[192,768]{1,0:T(8,128)(2,1)S(1)}, u32[]{:S(2)}, u32[]{:S(2)}) collective-permute-start(bf16[192,768]{1,0:T(8,128)(2,1)S(1)} %get-tuple-element.264), channel_id=1, source_target_pairs={{0,2},{1,3},{2,0},{3,1},{4,6},{5,7},{6,4},{7,5},{8,10},{9,11},{10,... | collective-permute-start | bytes 884744 | tf_op jit(solution)/shard_map/ppermute | solution.py:640
  114.6 21.6 %collective-permute-start.11 = (bf16[192,768]{1,0:T(8,128)(2,1)S(1)}, bf16[192,768]{1,0:T(8,128)(2,1)S(1)}, u32[]{:S(2)}, u32[]{:S(2)}) collective-permute-start(bf16[192,768]{1,0:T(8,128)(2,1)S(1)} %get-tuple-element.265), channel_id=1, source_target_pairs={{0,1},{1,0},{2,3},{3,2},{4,5},{5,4},{6,7},{7,6},{8,9},{9,8},{10,11... | collective-permute-start | bytes 884744 | tf_op jit(solution)/shard_map/ppermute | solution.py:640
  114.7 13.3 %copy-start.10 = (f32[16,768]{1,0:T(8,128)S(1)}, f32[16,768]{1,0:T(8,128)}, u32[]{:S(2)}) copy-start(f32[16,768]{1,0:T(8,128)} %get-tuple-element.286.mlp_sums) | copy-start | bytes 147460
  114.7 13.3 %copy-start.11 = (f32[16,768]{1,0:T(8,128)S(1)}, f32[16,768]{1,0:T(8,128)}, u32[]{:S(2)}) copy-start(f32[16,768]{1,0:T(8,128)} %get-tuple-element.287.refs_0_) | copy-start | bytes 147460
  136.2 13.9 %collective-permute-start.14 = (bf16[4,320,768]{2,1,0:T(8,128)(2,1)S(1)}, bf16[4,320,768]{2,1,0:T(8,128)(2,1)S(1)}, u32[]{:S(2)}, u32[]{:S(2)}) collective-permute-start(bf16[4,320,768]{2,1,0:T(8,128)(2,1)S(1)} %get-tuple-element.292), channel_id=1, source_target_pairs={{0,4},{4,0},{8,12},{12,8},{16,20},{20,16},{24,28},{28,24},{1,5},{5... | collective-permute-start | bytes 5898248 | tf_op jit(solution)/shard_map/ppermute | solution.py:643
  139.6 10.5 %collective-permute-start.15 = (bf16[480,384]{1,0:T(8,128)(2,1)S(1)}, bf16[480,384]{1,0:T(8,128)(2,1)S(1)}, u32[]{:S(2)}, u32[]{:S(2)}) collective-permute-start(bf16[480,384]{1,0:T(8,128)(2,1)S(1)} %get-tuple-element.298), channel_id=1, source_target_pairs={{0,2},{1,3},{2,0},{3,1},{4,6},{5,7},{6,4},{7,5},{8,10},{9,11},{10,... | collective-permute-start | bytes 1105928 | tf_op jit(solution)/shard_map/ppermute | solution.py:640
  140.2 9.9 %collective-permute-start.16 = (bf16[480,384]{1,0:T(8,128)(2,1)S(1)}, bf16[480,384]{1,0:T(8,128)(2,1)S(1)}, u32[]{:S(2)}, u32[]{:S(2)}) collective-permute-start(bf16[480,384]{1,0:T(8,128)(2,1)S(1)} %get-tuple-element.299), channel_id=1, source_target_pairs={{0,1},{1,0},{2,3},{3,2},{4,5},{5,4},{6,7},{7,6},{8,9},{9,8},{10,11... | collective-permute-start | bytes 1105928 | tf_op jit(solution)/shard_map/ppermute | solution.py:640
  142.0 8.0 %collective-permute-start.17 = (bf16[192,768]{1,0:T(8,128)(2,1)S(1)}, bf16[192,768]{1,0:T(8,128)(2,1)S(1)}, u32[]{:S(2)}, u32[]{:S(2)}) collective-permute-start(bf16[192,768]{1,0:T(8,128)(2,1)S(1)} %get-tuple-element.306), channel_id=1, source_target_pairs={{0,8},{4,12},{8,0},{12,4},{16,24},{20,28},{24,16},{28,20},{1,9},{5... | collective-permute-start | bytes 884744 | tf_op jit(solution)/shard_map/ppermute | solution.py:650
  151.4 11.4 %collective-permute-start.18 = (bf16[2,160,768]{2,1,0:T(8,128)(2,1)S(1)}, bf16[2,160,768]{2,1,0:T(8,128)(2,1)S(1)}, u32[]{:S(2)}, u32[]{:S(2)}) collective-permute-start(bf16[2,160,768]{2,1,0:T(8,128)(2,1)S(1)} %get-tuple-element.314), channel_id=1, source_target_pairs={{0,1},{1,0},{2,3},{3,2},{4,5},{5,4},{6,7},{7,6},{8,9},{9,8},{10,11... | collective-permute-start | bytes 1474568 | tf_op jit(solution)/shard_map/ppermute | solution.py:640
  152.6 11.3 %collective-permute-start.19 = (bf16[2,160,768]{2,1,0:T(8,128)(2,1)S(1)}, bf16[2,160,768]{2,1,0:T(8,128)(2,1)S(1)}, u32[]{:S(2)}, u32[]{:S(2)}) collective-permute-start(bf16[2,160,768]{2,1,0:T(8,128)(2,1)S(1)} %get-tuple-element.315), channel_id=1, source_target_pairs={{0,2},{1,3},{2,0},{3,1},{4,6},{5,7},{6,4},{7,5},{8,10},{9,11},{10,... | collective-permute-start | bytes 1474568 | tf_op jit(solution)/shard_map/ppermute | solution.py:640
  153.2 13.0 %copy-start.29 = (bf16[4,64,768]{2,1,0:T(8,128)(2,1)S(1)}, bf16[4,64,768]{2,1,0:T(8,128)(2,1)}, u32[]{:S(2)}) copy-start(bf16[4,64,768]{2,1,0:T(8,128)(2,1)} %get-tuple-element.358) | copy-start | bytes 1179652
  153.3 13.9 %copy-start.28 = (bf16[4,64,768]{2,1,0:T(8,128)(2,1)S(1)}, bf16[4,64,768]{2,1,0:T(8,128)(2,1)}, u32[]{:S(2)}) copy-start(bf16[4,64,768]{2,1,0:T(8,128)(2,1)} %get-tuple-element.359) | copy-start | bytes 1179652
  153.3 16.5 %copy-start.27 = (bf16[4,64,768]{2,1,0:T(8,128)(2,1)S(1)}, bf16[4,64,768]{2,1,0:T(8,128)(2,1)}, u32[]{:S(2)}) copy-start(bf16[4,64,768]{2,1,0:T(8,128)(2,1)} %get-tuple-element.360) | copy-start | bytes 1179652
  154.1 8.5 %collective-permute-start.20 = (bf16[480,384]{1,0:T(8,128)(2,1)S(1)}, bf16[480,384]{1,0:T(8,128)(2,1)S(1)}, u32[]{:S(2)}, u32[]{:S(2)}) collective-permute-start(bf16[480,384]{1,0:T(8,128)(2,1)S(1)} %get-tuple-element.324), channel_id=1, source_target_pairs={{0,8},{4,12},{8,0},{12,4},{16,24},{20,28},{24,16},{28,20},{1,9},{5... | collective-permute-start | bytes 1105928 | tf_op jit(solution)/shard_map/ppermute | solution.py:650
  155.4 11.7 %collective-permute-start.23 = (bf16[192,768]{1,0:T(8,128)(2,1)S(1)}, bf16[192,768]{1,0:T(8,128)(2,1)S(1)}, u32[]{:S(2)}, u32[]{:S(2)}) collective-permute-start(bf16[192,768]{1,0:T(8,128)(2,1)S(1)} %add_convert_fusion.3), channel_id=1, source_target_pairs={{0,24},{4,28},{8,16},{12,20},{16,8},{20,12},{24,0},{28,4},{1,25},{... | collective-permute-start | bytes 884744 | tf_op jit(solution)/shard_map/ppermute | solution.py:650
  163.9 24.4 %copy-start.13 = (bf16[4,64,768]{2,1,0:T(8,128)(2,1)S(1)}, bf16[4,64,768]{2,1,0:T(8,128)(2,1)}, u32[]{:S(2)}) copy-start(bf16[4,64,768]{2,1,0:T(8,128)(2,1)} %get-tuple-element.361) | copy-start | bytes 1179652
  163.9 26.1 %copy-start.14 = (bf16[4,64,768]{2,1,0:T(8,128)(2,1)S(1)}, bf16[4,64,768]{2,1,0:T(8,128)(2,1)}, u32[]{:S(2)}) copy-start(bf16[4,64,768]{2,1,0:T(8,128)(2,1)} %get-tuple-element.362) | copy-start | bytes 1179652
  163.9 26.7 %copy-start.15 = (bf16[4,64,768]{2,1,0:T(8,128)(2,1)S(1)}, bf16[4,64,768]{2,1,0:T(8,128)(2,1)}, u32[]{:S(2)}) copy-start(bf16[4,64,768]{2,1,0:T(8,128)(2,1)} %get-tuple-element.363) | copy-start | bytes 1179652
  164.7 5.1 %collective-permute-start.21 = (bf16[160,768]{1,0:T(8,128)(2,1)S(1)}, bf16[160,768]{1,0:T(8,128)(2,1)S(1)}, u32[]{:S(2)}, u32[]{:S(2)}) collective-permute-start(bf16[160,768]{1,0:T(8,128)(2,1)S(1)} %get-tuple-element.334), channel_id=1, source_target_pairs={{0,2},{1,3},{2,0},{3,1},{4,6},{5,7},{6,4},{7,5},{8,10},{9,11},{10,... | collective-permute-start | bytes 737288 | tf_op jit(solution)/shard_map/ppermute | solution.py:640
  165.3 5.4 %collective-permute-start.22 = (bf16[160,768]{1,0:T(8,128)(2,1)S(1)}, bf16[160,768]{1,0:T(8,128)(2,1)S(1)}, u32[]{:S(2)}, u32[]{:S(2)}) collective-permute-start(bf16[160,768]{1,0:T(8,128)(2,1)S(1)} %get-tuple-element.335), channel_id=1, source_target_pairs={{0,1},{1,0},{2,3},{3,2},{4,5},{5,4},{6,7},{7,6},{8,9},{9,8},{10,11... | collective-permute-start | bytes 737288 | tf_op jit(solution)/shard_map/ppermute | solution.py:640
  166.0 50.2 %copy-start.6 = (bf16[4,64,768]{2,1,0:T(8,128)(2,1)S(1)}, bf16[4,64,768]{2,1,0:T(8,128)(2,1)}, u32[]{:S(2)}) copy-start(bf16[4,64,768]{2,1,0:T(8,128)(2,1)} %get-tuple-element.372.refs_0_) | copy-start | bytes 1179652
  166.1 19.7 %collective-permute-start.25 = (bf16[480,384]{1,0:T(8,128)(2,1)S(1)}, bf16[480,384]{1,0:T(8,128)(2,1)S(1)}, u32[]{:S(2)}, u32[]{:S(2)}) collective-permute-start(bf16[480,384]{1,0:T(8,128)(2,1)S(1)} %add_convert_fusion.1), channel_id=1, source_target_pairs={{0,24},{4,28},{8,16},{12,20},{16,8},{20,12},{24,0},{28,4},{1,25},{... | collective-permute-start | bytes 1105928 | tf_op jit(solution)/shard_map/ppermute | solution.py:650
  166.3 22.0 %collective-permute-start.29 = (bf16[4,64,768]{2,1,0:T(8,128)(2,1)S(1)}, bf16[4,64,768]{2,1,0:T(8,128)(2,1)S(1)}, u32[]{:S(2)}, u32[]{:S(2)}) collective-permute-start(bf16[4,64,768]{2,1,0:T(8,128)(2,1)S(1)} %copy-done.29), channel_id=1, source_target_pairs={{0,1},{1,0},{2,3},{3,2},{4,5},{5,4},{6,7},{7,6},{8,9},{9,8},{10,11... | collective-permute-start | bytes 1179656 | tf_op jit(solution)/shard_map/ppermute | solution.py:640
  167.2 22.8 %collective-permute-start.30 = (bf16[4,64,768]{2,1,0:T(8,128)(2,1)S(1)}, bf16[4,64,768]{2,1,0:T(8,128)(2,1)S(1)}, u32[]{:S(2)}, u32[]{:S(2)}) collective-permute-start(bf16[4,64,768]{2,1,0:T(8,128)(2,1)S(1)} %copy-done.28), channel_id=1, source_target_pairs={{0,2},{1,3},{2,0},{3,1},{4,6},{5,7},{6,4},{7,5},{8,10},{9,11},{10,... | collective-permute-start | bytes 1179656 | tf_op jit(solution)/shard_map/ppermute | solution.py:640
  169.8 20.8 %collective-permute-start.31 = (bf16[4,64,768]{2,1,0:T(8,128)(2,1)S(1)}, bf16[4,64,768]{2,1,0:T(8,128)(2,1)S(1)}, u32[]{:S(2)}, u32[]{:S(2)}) collective-permute-start(bf16[4,64,768]{2,1,0:T(8,128)(2,1)S(1)} %copy-done.27), channel_id=1, source_target_pairs={{0,3},{1,2},{2,1},{3,0},{4,7},{5,6},{6,5},{7,4},{8,11},{9,10},{10,... | collective-permute-start | bytes 1179656 | tf_op jit(solution)/shard_map/ppermute | solution.py:640
  171.4 15.8 %collective-permute-start.24 = (bf16[160,768]{1,0:T(8,128)(2,1)S(1)}, bf16[160,768]{1,0:T(8,128)(2,1)S(1)}, u32[]{:S(2)}, u32[]{:S(2)}) collective-permute-start(bf16[160,768]{1,0:T(8,128)(2,1)S(1)} %get-tuple-element.347), channel_id=1, source_target_pairs={{0,8},{4,12},{8,0},{12,4},{16,24},{20,28},{24,16},{28,20},{1,9},{5... | collective-permute-start | bytes 737288 | tf_op jit(solution)/shard_map/ppermute | solution.py:650
  185.7 5.6 %collective-permute-start.28 = (bf16[192,768]{1,0:T(8,128)(2,1)S(1)}, bf16[192,768]{1,0:T(8,128)(2,1)S(1)}, u32[]{:S(2)}, u32[]{:S(2)}) collective-permute-start(bf16[192,768]{1,0:T(8,128)(2,1)S(1)} %add_convert_fusion.2.refs_0_), channel_id=1, source_target_pairs={{0,4},{4,0},{8,12},{12,8},{16,20},{20,16},{24,28},{28,24},{1,5},{5... | collective-permute-start | bytes 884744 | tf_op jit(solution)/shard_map/ppermute | solution.py:643
  187.2 5.7 %collective-permute-start.27 = (bf16[192,768]{1,0:T(8,128)(2,1)S(1)}, bf16[192,768]{1,0:T(8,128)(2,1)S(1)}, u32[]{:S(2)}, u32[]{:S(2)}) collective-permute-start(bf16[192,768]{1,0:T(8,128)(2,1)S(1)} %add_convert_fusion.2.refs_0_), channel_id=1, source_target_pairs={{0,8},{4,12},{8,0},{12,4},{16,24},{20,28},{24,16},{28,20},{1,9},{5... | collective-permute-start | bytes 884744 | tf_op jit(solution)/shard_map/ppermute | solution.py:650
  188.3 12.2 %collective-permute-start.32 = (bf16[4,64,768]{2,1,0:T(8,128)(2,1)S(1)}, bf16[4,64,768]{2,1,0:T(8,128)(2,1)S(1)}, u32[]{:S(2)}, u32[]{:S(2)}) collective-permute-start(bf16[4,64,768]{2,1,0:T(8,128)(2,1)S(1)} %copy-done.13), channel_id=1, source_target_pairs={{0,1},{1,0},{2,3},{3,2},{4,5},{5,4},{6,7},{7,6},{8,9},{9,8},{10,11... | collective-permute-start | bytes 1179656 | tf_op jit(solution)/shard_map/ppermute | solution.py:640
  190.0 14.7 %collective-permute-start.33 = (bf16[4,64,768]{2,1,0:T(8,128)(2,1)S(1)}, bf16[4,64,768]{2,1,0:T(8,128)(2,1)S(1)}, u32[]{:S(2)}, u32[]{:S(2)}) collective-permute-start(bf16[4,64,768]{2,1,0:T(8,128)(2,1)S(1)} %copy-done.14), channel_id=1, source_target_pairs={{0,2},{1,3},{2,0},{3,1},{4,6},{5,7},{6,4},{7,5},{8,10},{9,11},{10,... | collective-permute-start | bytes 1179656 | tf_op jit(solution)/shard_map/ppermute | solution.py:640
  190.6 14.1 %collective-permute-start.34 = (bf16[4,64,768]{2,1,0:T(8,128)(2,1)S(1)}, bf16[4,64,768]{2,1,0:T(8,128)(2,1)S(1)}, u32[]{:S(2)}, u32[]{:S(2)}) collective-permute-start(bf16[4,64,768]{2,1,0:T(8,128)(2,1)S(1)} %copy-done.15), channel_id=1, source_target_pairs={{0,3},{1,2},{2,1},{3,0},{4,7},{5,6},{6,5},{7,4},{8,11},{9,10},{10,... | collective-permute-start | bytes 1179656 | tf_op jit(solution)/shard_map/ppermute | solution.py:640
  191.3 27.2 %copy-start.3 = (bf16[4,64,768]{2,1,0:T(8,128)(2,1)S(1)}, bf16[4,64,768]{2,1,0:T(8,128)(2,1)}, u32[]{:S(2)}) copy-start(bf16[4,64,768]{2,1,0:T(8,128)(2,1)} %get-tuple-element.384.refs_0_) | copy-start | bytes 1179652
  191.3 13.4 %collective-permute-start.26 = (bf16[160,768]{1,0:T(8,128)(2,1)S(1)}, bf16[160,768]{1,0:T(8,128)(2,1)S(1)}, u32[]{:S(2)}, u32[]{:S(2)}) collective-permute-start(bf16[160,768]{1,0:T(8,128)(2,1)S(1)} %add_convert_fusion.5), channel_id=1, source_target_pairs={{0,24},{4,28},{8,16},{12,20},{16,8},{20,12},{24,0},{28,4},{1,25},{... | collective-permute-start | bytes 737288 | tf_op jit(solution)/shard_map/ppermute | solution.py:650
  192.9 11.8 %collective-permute-start.38 = (bf16[480,384]{1,0:T(8,128)(2,1)S(1)}, bf16[480,384]{1,0:T(8,128)(2,1)S(1)}, u32[]{:S(2)}, u32[]{:S(2)}) collective-permute-start(bf16[480,384]{1,0:T(8,128)(2,1)S(1)} %add_convert_fusion.refs_0_), channel_id=1, source_target_pairs={{0,4},{4,0},{8,12},{12,8},{16,20},{20,16},{24,28},{28,24},{1,5},{5... | collective-permute-start | bytes 1105928 | tf_op jit(solution)/shard_map/ppermute | solution.py:643
  200.5 11.8 %collective-permute-start.37 = (bf16[480,384]{1,0:T(8,128)(2,1)S(1)}, bf16[480,384]{1,0:T(8,128)(2,1)S(1)}, u32[]{:S(2)}, u32[]{:S(2)}) collective-permute-start(bf16[480,384]{1,0:T(8,128)(2,1)S(1)} %add_convert_fusion.refs_0_), channel_id=1, source_target_pairs={{0,8},{4,12},{8,0},{12,4},{16,24},{20,28},{24,16},{28,20},{1,9},{5... | collective-permute-start | bytes 1105928 | tf_op jit(solution)/shard_map/ppermute | solution.py:650
  212.3 11.0 %collective-permute-start.39 = (bf16[480,384]{1,0:T(8,128)(2,1)S(1)}, bf16[480,384]{1,0:T(8,128)(2,1)S(1)}, u32[]{:S(2)}, u32[]{:S(2)}) collective-permute-start(bf16[480,384]{1,0:T(8,128)(2,1)S(1)} %collective-permute-done.37.refs_1_), channel_id=1, source_target_pairs={{0,4},{4,0},{8,12},{12,8},{16,20},{20,16},{24,28},{28,24},{1,5},{5... | collective-permute-start | bytes 1105928 | tf_op jit(solution)/shard_map/ppermute | solution.py:643
  214.2 7.0 %collective-permute-start.40 = (bf16[192,768]{1,0:T(8,128)(2,1)S(1)}, bf16[192,768]{1,0:T(8,128)(2,1)S(1)}, u32[]{:S(2)}, u32[]{:S(2)}) collective-permute-start(bf16[192,768]{1,0:T(8,128)(2,1)S(1)} %collective-permute-done.27.refs_1_), channel_id=1, source_target_pairs={{0,4},{4,0},{8,12},{12,8},{16,20},{20,16},{24,28},{28,24},{1,5},{5... | collective-permute-start | bytes 884744 | tf_op jit(solution)/shard_map/ppermute | solution.py:643
  214.2 9.1 %collective-permute-start.36 = (bf16[160,768]{1,0:T(8,128)(2,1)S(1)}, bf16[160,768]{1,0:T(8,128)(2,1)S(1)}, u32[]{:S(2)}, u32[]{:S(2)}) collective-permute-start(bf16[160,768]{1,0:T(8,128)(2,1)S(1)} %add_convert_fusion.4.refs_0_), channel_id=1, source_target_pairs={{0,4},{4,0},{8,12},{12,8},{16,20},{20,16},{24,28},{28,24},{1,5},{5... | collective-permute-start | bytes 737288 | tf_op jit(solution)/shard_map/ppermute | solution.py:643
  214.7 8.6 %collective-permute-start.35 = (bf16[160,768]{1,0:T(8,128)(2,1)S(1)}, bf16[160,768]{1,0:T(8,128)(2,1)S(1)}, u32[]{:S(2)}, u32[]{:S(2)}) collective-permute-start(bf16[160,768]{1,0:T(8,128)(2,1)S(1)} %add_convert_fusion.4.refs_0_), channel_id=1, source_target_pairs={{0,8},{4,12},{8,0},{12,4},{16,24},{20,28},{24,16},{28,20},{1,9},{5... | collective-permute-start | bytes 737288 | tf_op jit(solution)/shard_map/ppermute | solution.py:650
  223.4 2.8 %collective-permute-start.41 = (bf16[160,768]{1,0:T(8,128)(2,1)S(1)}, bf16[160,768]{1,0:T(8,128)(2,1)S(1)}, u32[]{:S(2)}, u32[]{:S(2)}) collective-permute-start(bf16[160,768]{1,0:T(8,128)(2,1)S(1)} %collective-permute-done.35.refs_1_), channel_id=1, source_target_pairs={{0,4},{4,0},{8,12},{12,8},{16,20},{20,16},{24,28},{28,24},{1,5},{5... | collective-permute-start | bytes 737288 | tf_op jit(solution)/shard_map/ppermute | solution.py:643
  (8 other events, 27.9 us)
